TPU v7x, 512 devices: a whole 4x8x8 slice. The times are simulated.
512 devices in a mesh: rep: 32 (over y, z_hi), trow: 4 (over z_lo, core), tcol: 4 (over x).
Axes of the slice: x: 4, y: 8, z: 8 (z_hi: 4, z_lo: 2; z = z_hi * 2 + z_lo), core: 2. Of those that a mesh axis runs over, the one named last changes fastest.
Arguments:
- pseudo_grads: bfloat16 [32, 5120, 1024], P('rep', 'trow', 'tcol'), may hold values from -1200 to 1200
- left_gram: float32 [16, 320, 320], P(('trow', 'tcol')), may hold values from -102.4 to 61.44
- right_gram: float32 [4, 256, 256], P('tcol'), may hold values from -512 to 307.2
- left_basis: float32 [16, 320, 320], P(('trow', 'tcol')), may hold values from -1 to 2
- right_basis: float32 [4, 256, 256], P('tcol'), may hold values from -1 to 2
- first_moment: float32 [5120, 1024], P(('trow', 'rep'), 'tcol'), may hold values from -1.8 to 1.8
- second_moment: float32 [5120, 1024], P(('trow', 'rep'), 'tcol'), may hold values from 0.05 to 1
Outputs:
- update: bfloat16 [5120, 1024], P('trow', 'tcol')
- new_left_gram: float32 [16, 320, 320], P(('trow', 'tcol'))
- new_left_basis: float32 [16, 320, 320], P(('trow', 'tcol'))
- new_right_gram: float32 [4, 256, 256], P('tcol')
- new_right_basis: float32 [4, 256, 256], P('tcol')
- new_first_moment: float32 [5120, 1024], P(('trow', 'rep'), 'tcol')
- new_second_moment: float32 [5120, 1024], P(('trow', 'rep'), 'tcol')
All inputs are finite; a program needn't handle non-finite values.
Results may differ from a plain program's by a relative error of at most 0.001.
Values sent between devices are 32-bit elements; how exact they have to be, the bound alone decides.
No kernel may reach another device: no remote copies, remote signals or barrier semaphores. Data moves between devices by JAX's collectives and lax.ppermute only.
A program may use at most 64 MiB of HBM per device.

v0:
```python
import math

import jax
import jax.numpy as jnp
from jax import lax
from jax.sharding import PartitionSpec as P

D = 5120
KV = 1024
LB = 320
RB = 256


highest = lax.Precision.HIGHEST
beta_gram = 0.95
beta_first = 0.95
beta_second = 0.95
first_bias = 1.0 - 0.95**4
second_bias = 1.0 - 0.95**4
clip_ratio = 0.5


def refresh(gram, basis):
    powered = jnp.einsum("bij,bjk->bik", gram, basis, precision=highest)
    crossed = jnp.einsum("bki,bkj->bij", powered, powered, precision=highest)
    factor = jnp.linalg.cholesky(crossed)

    def solve_one(chol_factor, powered_block):
        return jax.scipy.linalg.solve_triangular(chol_factor, powered_block.T, lower=True).T

    return jax.vmap(solve_one)(factor, powered)


def rotate(tile_grad, left_blocks, right_blocks):
    stacked = tile_grad.reshape(left_blocks.shape[0], left_blocks.shape[1], tile_grad.shape[1])
    turned = jnp.einsum("bki,bkc->bic", left_blocks, stacked, precision=highest).reshape(
        tile_grad.shape
    )
    split_cols = turned.reshape(tile_grad.shape[0], right_blocks.shape[0], right_blocks.shape[1])
    return jnp.einsum("dbk,bkj->dbj", split_cols, right_blocks, precision=highest).reshape(
        tile_grad.shape
    )


def unrotate(tile_dir, left_blocks, right_blocks):
    stacked = tile_dir.reshape(left_blocks.shape[0], left_blocks.shape[1], tile_dir.shape[1])
    turned = jnp.einsum("bik,bkc->bic", left_blocks, stacked, precision=highest).reshape(
        tile_dir.shape
    )
    split_cols = turned.reshape(tile_dir.shape[0], right_blocks.shape[0], right_blocks.shape[1])
    return jnp.einsum("dbk,bjk->dbj", split_cols, right_blocks, precision=highest).reshape(
        tile_dir.shape
    )


def adam_step(rotated, first_moment, second_moment):
    moment = beta_first * first_moment + (1.0 - beta_first) * rotated
    second = beta_second * second_moment + (1.0 - beta_second) * rotated * rotated
    direction = moment / first_bias / (jnp.sqrt(second / second_bias) + 1e-08)
    return (moment, second, direction)


def right_partial(values):
    split_cols = values.reshape(values.shape[0], values.shape[1] // RB, RB)
    return jnp.einsum("dbi,dbj->bij", split_cols, split_cols, precision=highest)


def clip_factor(squares):
    return clip_ratio * math.sqrt(D * KV) / (jnp.sqrt(squares) + 1e-06)


def shards(
    pseudo_grads, left_gram, right_gram, left_basis, right_basis, first_moment, second_moment
):
    replicas = lax.axis_size("rep")
    local_grad = pseudo_grads[0].astype(jnp.float32)
    average = lax.psum(local_grad, "rep") / replicas
    squares = lax.psum(jnp.sum(average * average), ("trow", "tcol"))
    factor = clip_factor(squares)
    gradient = average * factor
    right_input = average * factor
    right_summed = lax.psum(right_partial(right_input), "trow")
    right_new = beta_gram * right_gram + (1.0 - beta_gram) * right_summed
    right_basis_new = refresh(right_new, right_basis)
    stacked = gradient.reshape(gradient.shape[0] // LB, LB, gradient.shape[1])
    left_part = jnp.einsum("bic,bjc->bij", stacked, stacked, precision=highest)
    left_summed = lax.psum_scatter(left_part, "tcol", scatter_dimension=0, tiled=True)
    left_new = beta_gram * left_gram + (1.0 - beta_gram) * left_summed
    left_basis_new = refresh(left_new, left_basis)
    row_bases = lax.all_gather(left_basis_new, "tcol", axis=0, tiled=True)
    rotated = rotate(gradient, row_bases, right_basis_new)
    row_count = first_moment.shape[0]
    own_rows = lax.dynamic_slice_in_dim(rotated, lax.axis_index("rep") * row_count, row_count, 0)
    moment, second, direction = adam_step(own_rows, first_moment, second_moment)
    whole_direction = lax.all_gather(direction, "rep", axis=0, tiled=True)
    update = unrotate(whole_direction, row_bases, right_basis_new).astype(jnp.bfloat16)
    return (update, left_new, left_basis_new, right_new, right_basis_new, moment, second)


def solution(mesh):
    placed = (
        P("rep", "trow", "tcol"),
        P(("trow", "tcol"), None, None),
        P("tcol", None, None),
        P(("trow", "tcol"), None, None),
        P("tcol", None, None),
        P(("trow", "rep"), "tcol"),
        P(("trow", "rep"), "tcol"),
    )
    return jax.shard_map(
        shards,
        mesh=mesh,
        in_specs=placed,
        out_specs=(
            P("trow", "tcol"),
            P(("trow", "tcol"), None, None),
            P(("trow", "tcol"), None, None),
            P("tcol", None, None),
            P("tcol", None, None),
            P(("trow", "rep"), "tcol"),
            P(("trow", "rep"), "tcol"),
        ),
        check_vma=False,
    )
```

profile of v0, /device:TPU:6, one launch (start us, length us, event | category | flops | bytes accessed | tf_op | source)
XLA Modules:
  0.0 723.1 jit_solution(17487891854692755136)
XLA Ops:
  7.2 2.3 bitcast_convert_fusion
  9.6 328.3 %all-reduce.7.cloned.1.call-done = f32[1280,256]{1,0:T(8,128)} async-done(((f32[1280,256]{1,0:T(8,128)}), f32[1280,256]{1,0:T(8,128)}) %all-reduce.7.cloned.1.call-update) | async-done | bytes 1310736 | tf_op jit(solution)/shard_map/psum | solution.py:77
  337.9 2.4 multiply_reduce_fusion
  340.3 26.8 %psum.22 = f32[]{:T(128)} all-reduce(f32[]{:T(128)} %multiply_reduce_fusion), channel_id=1, replica_groups=mesh['rep'=32,'trow'=4,'tcol'=4] {'trow','tcol'}, use_global_device_ids=true, to_apply=%region_2.0 | all-reduce | flops 1 | bytes 8 | tf_op jit(solution)/shard_map/psum | solution.py:78
  367.9 3.0 convolution_bitcast_fusion
  370.9 3.6 fusion.41
  374.8 38.2 %all-reduce.9.cloned.1.call-done = f32[1,256,256]{2,1,0:T(8,128)} async-done(((f32[1,256,256]{2,1,0:T(8,128)}), f32[1,256,256]{2,1,0:T(8,128)}) %all-reduce.9.cloned.1.call-update) | async-done | bytes 262160 | tf_op jit(solution)/shard_map/psum | solution.py:82
  413.0 1.0 multiply_add_fusion.1
  414.0 0.7 copy-done.5
  415.7 0.8 copy.25
  416.5 31.9 %reduce-scatter.2.cloned.1.call-done = f32[1,320,320]{2,1,0:T(8,128)} async-done(((f32[4,320,320]{2,1,0:T(8,128)}), f32[1,320,320]{2,1,0:T(8,128)}) %reduce-scatter.2.cloned.1.call-update) | async-done | bytes 409616 | tf_op jit(solution)/shard_map/reduce_scatter | solution.py:87
  448.4 1.1 multiply_add_fusion
  449.6 1.1 fusion.12
  450.6 1.2 fusion.42
  451.9 1.0 copy.28
  452.9 1.1 fusion.11
  454.0 0.8 copy-done.4
  454.7 11.7 %custom-call.47 = f32[1,128,128]{2,1,0:T(8,128)S(1)} custom-call(f32[1,128,128]{2,1,0:T(8,128)S(1)} %cholesky.309), custom_call_target="Cholesky" | custom-call | tf_op jit(solution)/shard_map/jit(cholesky)/cholesky | solution.py:26
  466.5 9.8 %custom-call.48 = f32[1,1,128,128]{2,3,1,0:T(8,128)S(1)} custom-call(f32[1,1,128,128]{3,2,1,0:T(8,128)S(1)} %get-tuple-element.68), custom_call_target="InvertDiagBlocksLowerTriangular" | custom-call | tf_op jit(solution)/shard_map/jit(cholesky)/cholesky | solution.py:26
  476.3 1.1 constant_dynamic-update-slice_fusion.2
  477.5 1.2 fusion.7
  479.3 12.7 %custom-call.49 = f32[1,128,128]{2,1,0:T(8,128)S(1)} custom-call(f32[1,128,128]{2,1,0:T(8,128)} %cholesky.313), custom_call_target="Cholesky" | custom-call | tf_op jit(solution)/shard_map/jit(cholesky)/cholesky | solution.py:26
  492.7 10.6 %custom-call.50 = f32[1,1,128,128]{2,3,1,0:T(8,128)S(1)} custom-call(f32[1,1,128,128]{3,2,1,0:T(8,128)} %get-tuple-element.65), custom_call_target="InvertDiagBlocksLowerTriangular" | custom-call | tf_op jit(solution)/shard_map/jit(cholesky)/cholesky | solution.py:26
  503.5 1.0 fusion.10
  504.5 5.8 custom-call.51
  513.7 0.7 copy-done.2
  514.4 5.8 while.3
  515.0 2.3 bitcast_dynamic-update-slice_fusion.6
  517.9 2.3 bitcast_dynamic-update-slice_fusion.6
  520.3 29.5 %custom-call.52 = f32[1,3,128,128]{2,3,1,0:T(8,128)S(1)} custom-call(f32[1,3,128,128]{3,2,1,0:T(8,128)S(1)} %pad_maximum_fusion.1), custom_call_target="InvertDiagBlocksLowerTriangular" | custom-call | tf_op jit(solution)/shard_map/vmap(jit(_solve_triangular))/triangular_solve | solution.py:29
  550.1 1.1 fusion.2
  551.6 1.3 fusion.4
  553.2 0.8 maximum_bitcast_fusion
  554.6 11.7 %custom-call.43 = f32[1,128,128]{2,1,0:T(8,128)S(1)} custom-call(f32[1,128,128]{2,1,0:T(8,128)S(1)} %cholesky.306), custom_call_target="Cholesky" | custom-call | tf_op jit(solution)/shard_map/jit(cholesky)/cholesky | solution.py:26
  566.3 9.8 %custom-call.44 = f32[1,1,128,128]{2,3,1,0:T(8,128)S(1)} custom-call(f32[1,1,128,128]{3,2,1,0:T(8,128)S(1)} %get-tuple-element.63), custom_call_target="InvertDiagBlocksLowerTriangular" | custom-call | tf_op jit(solution)/shard_map/jit(cholesky)/cholesky | solution.py:26
  576.6 11.7 %custom-call.45 = f32[1,128,128]{2,1,0:T(8,128)S(1)} custom-call(f32[1,128,128]{2,1,0:T(8,128)S(1)} %fusion.8), custom_call_target="Cholesky" | custom-call | tf_op jit(solution)/shard_map/jit(cholesky)/cholesky | solution.py:26
  590.4 4.0 while.2
  591.0 1.4 bitcast_dynamic-update-slice_fusion.5
  593.0 1.4 bitcast_dynamic-update-slice_fusion.5
  594.4 19.8 %custom-call.46 = f32[1,2,128,128]{2,3,1,0:T(8,128)S(1)} custom-call(f32[1,2,128,128]{3,2,1,0:T(8,128)S(1)} %bitcast.253), custom_call_target="InvertDiagBlocksLowerTriangular" | custom-call | tf_op jit(solution)/shard_map/vmap(jit(_solve_triangular))/triangular_solve | solution.py:29
  615.3 5.3 fusion.43
  620.6 1.2 fusion.19
  621.9 0.7 add_divide_fusion
  622.6 0.8 copy.33
  623.4 85.5 %all-gather.5.cloned.1.call-done = f32[1280,256]{1,0:T(8,128)} async-done(((f32[40,256]{1,0:T(8,128)}), f32[1280,256]{1,0:T(8,128)}) %all-gather.5.cloned.1.call-update) | async-done | bytes 1310736 | tf_op jit(solution)/shard_map/all_gather | solution.py:95
  708.9 4.2 fusion.44
  713.1 2.2 fusion
  715.3 1.1 copy.32
  (78 shorter events, 10.6 us)
Async XLA Ops:
  7.2 442.4 %copy-start = (f32[1,320,320]{2,1,0:T(8,128)S(1)}, f32[1,320,320]{2,1,0:T(8,128)}, u32[]{:S(2)}) copy-start(f32[1,320,320]{2,1,0:T(8,128)} %param.10) | copy-start | bytes 1228804
  7.2 330.7 %all-reduce.7.cloned.1.call-start = ((), (), s32[]{:S(2)}) async-start(), calls=%async_computation.1 | async-start | bytes 2621440 | tf_op jit(solution)/shard_map/psum | solution.py:77
  9.6 403.4 %all-reduce.9.cloned.1.call-start = ((), (), s32[]{:S(2)}) async-start(), calls=%async_computation.2 | async-start | bytes 524288 | tf_op jit(solution)/shard_map/psum | solution.py:82
  337.9 29.9 %copy-start.1 = (f32[1280,256]{1,0:T(8,128)S(1)}, f32[1280,256]{1,0:T(8,128)}, u32[]{:S(2)}) copy-start(f32[1280,256]{1,0:T(8,128)} %all-reduce.7.cloned.1.call-done) | copy-start | bytes 3932164
  370.9 77.5 %reduce-scatter.2.cloned.1.call-start = ((), (), s32[]{:S(2)}) async-start(), calls=%async_computation.3 | async-start | bytes 2457600 | tf_op jit(solution)/shard_map/reduce_scatter | solution.py:87
  374.5 38.5 %copy-start.8 = (f32[1,256,256]{2,1,0:T(8,128)S(1)}, f32[1,256,256]{2,1,0:T(8,128)}, u32[]{:S(2)}) copy-start(f32[1,256,256]{2,1,0:T(8,128)} %param.9) | copy-start | bytes 786436
  374.5 40.2 %copy-start.9 = (f32[1,256,256]{2,1,0:T(8,128)S(1)}, f32[1,256,256]{2,1,0:T(8,128)}, u32[]{:S(2)}) copy-start(f32[1,256,256]{2,1,0:T(8,128)} %param.11) | copy-start | bytes 786436
  374.5 240.8 %all-gather.3.cloned.1.call-start = ((), (), s32[]{:S(2)}) async-start(), calls=%async_computation.4 | async-start | bytes 2457600 | tf_op jit(solution)/shard_map/all_gather | solution.py:90
  374.8 73.6 %copy-start.7 = (f32[1,320,320]{2,1,0:T(8,128)S(1)}, f32[1,320,320]{2,1,0:T(8,128)}, u32[]{:S(2)}) copy-start(f32[1,320,320]{2,1,0:T(8,128)} %param.8) | copy-start | bytes 1228804
  414.0 0.7 copy-start.5
  449.5 2.3 copy-start.3
  453.9 0.8 copy-start.4
  513.6 0.8 copy-start.2
  551.6 2.9 copy-start.6
  554.0 154.8 %all-gather.5.cloned.1.call-start = ((), (), s32[]{:S(2)}) async-start(), calls=%async_computation.5 | async-start | bytes 1351680 | tf_op jit(solution)/shard_map/all_gather | solution.py:95
  620.6 1.3 copy-start.10
  620.6 1.3 copy-start.11
Sparse Core Ops, SparseCore 0:
  10.9 326.9 all-reduce.6
  371.0 41.9 all-reduce.8
  415.9 32.5 reduce-scatter.1
  554.2 35.1 all-gather.2
  622.7 86.1 all-gather.4
where the time goes:
time: 728 us; the launch traced here: 723 us
  waiting for transfers between devices  484 us (66%)
  other arithmetic  146 us (20%)
  matrix products  30.9 us (4%)
  blocking collectives  26.8 us (4%)
  between operations  18.5 us (3%)
  local copies, waits for them, and re-layouts  16.5 us (2%)
    psum x1, waiting for transfers between devices, shards(): average = lax.psum(local_grad, 'rep') / replicas  328 us
    another operation x16, other arithmetic, refresh(): factor = jnp.linalg.cholesky(crossed)  86.7 us
    all_gather x1, waiting for transfers between devices, shards(): whole_direction = lax.all_gather(direction, 'rep', axis=0, tiled=True)  85.5 us
    another operation x9, other arithmetic, solve_one(): jax.scipy.linalg.solve_triangular(chol_factor, powered_block.T, lower=True)  49.5 us
    psum x1, waiting for transfers between devices, shards(): right_summed = lax.psum(right_partial(right_input), 'trow')  38.2 us
    reduce_scatter x1, waiting for transfers between devices, shards(): lax.psum_scatter(left_part, 'tcol', scatter_dimension=0, tiled=True)  31.9 us
    psum x1, blocking collectives, shards(): squares = lax.psum(jnp.sum(average * average), ('trow', 'tcol'))  26.8 us
  transfers between devices with their start and end apart: 5, of which 4 were waited for; matrix products, arithmetic and copies ran while one was open for 9% of the time, Pallas kernels for 0%

commit v1 on v0

v1 whole, which is shorter than its diff:
```python
import math

import jax
import jax.numpy as jnp
from jax import lax
from jax.experimental import pallas as pl
from jax.experimental.pallas import tpu as pltpu
from jax.sharding import Mesh, PartitionSpec as P

D = 5120
KV = 1024
LB = 320
RB = 256
NB = 64

highest = lax.Precision.HIGHEST
beta_gram = 0.95
beta_first = 0.95
beta_second = 0.95
first_bias = 1.0 - 0.95**4
second_bias = 1.0 - 0.95**4
clip_ratio = 0.5

REP = ("yk", "y2", "zh")
ROW = ("zl", "core")
MEMBERS = ("y2", "zh")
RIGHT_GROUP = ("yk", "zl", "core")


def mm(a, b, ca=1, cb=0):
    return lax.dot_general(
        a, b, (((ca,), (cb,)), ((), ())), precision=highest, preferred_element_type=jnp.float32
    )


def eliminate(rows, off):
    row_id = lax.broadcasted_iota(jnp.int32, (8, 128), 0)
    for g in range(8):
        count = 8 - g
        cols = [
            [
                jnp.broadcast_to(rows[g + h][:, off + 8 * g + t : off + 8 * g + t + 1], (8, 128))
                for h in range(count)
            ]
            for t in range(8)
        ]
        pivots = jnp.ones((8, 128), jnp.float32)
        for t in range(8):
            pivot = jnp.broadcast_to(cols[t][0][t : t + 1, :], (8, 128))
            inv = 1.0 / pivot
            pivots = jnp.where(row_id == t, pivot, pivots)
            f = [c * inv for c in cols[t]]
            f[0] = jnp.where(row_id > t, f[0], 0.0)
            for u in range(t + 1, 8):
                lead = jnp.broadcast_to(cols[u][0][t : t + 1, :], (8, 128))
                cols[u] = [c - fh * lead for c, fh in zip(cols[u], f)]
            lead = jnp.broadcast_to(rows[g][t : t + 1, :], (8, 128))
            for h in range(count):
                rows[g + h] = rows[g + h] - f[h] * lead
            yield
        scale = lax.rsqrt(pivots)
        scale = scale * (1.5 - 0.5 * pivots * scale * scale)
        rows[g] = rows[g] * scale


def load_block(s_ref, at):
    base = (at // 128) * 128
    off = at - base
    other = 64 - off
    width = min(128, s_ref.shape[1] - base)
    lane = lax.broadcasted_iota(jnp.int32, (8, 128), 1)
    row = lax.broadcasted_iota(jnp.int32, (8, 128), 0)
    rows = []
    for g in range(8):
        piece = s_ref[at + 8 * g : at + 8 * g + 8, base : base + width]
        if width < 128:
            piece = jnp.concatenate([piece, jnp.zeros((8, 128 - width), jnp.float32)], axis=1)
        eye = (lane == row + (8 * g + other)).astype(jnp.float32)
        rows.append(jnp.where((lane >= off) & (lane < off + 64), piece, eye))
    return rows, off, other


def apply_block(rows, other, s_ref, pt_ref, qt_ref, at):
    n = s_ref.shape[0]
    inv = jnp.concatenate(rows, axis=0)
    if other:
        inv = pltpu.roll(inv, 64, axis=1)
    inv = inv[:, :64]
    wp = mm(inv, pt_ref[at : at + 64, :])
    qt_ref[at : at + 64, :] = wp
    if at + 64 < n:
        start = ((at + 64) // 128) * 128
        ws = mm(inv, s_ref[at : at + 64, start:])
        s_ref[start:, start:] = s_ref[start:, start:] - mm(ws, ws, 0, 0)
        pt_ref[start:, :] = pt_ref[start:, :] - mm(ws, wp, 0, 0)


def refresh_kernel(
    member_ref, factor_ref, gl_ref, bl_ref, gr_ref, br_ref, tile_ref, fm_ref, sm_ref,
    qlt_ref, qrt_ref, m_ref, v_ref, turned_ref,
    sl_ref, pl_ref, sr_ref, pr_ref,
):
    for g_ref, b_ref, s_ref, p_ref in (
        (gl_ref, bl_ref, sl_ref, pl_ref),
        (gr_ref, br_ref, sr_ref, pr_ref),
    ):
        pt = mm(b_ref[...], g_ref[...], 0, 0)
        p_ref[...] = pt
        s_ref[...] = mm(pt, pt, 1, 1)
    for step in range(LB // NB):
        at = step * NB
        jobs = []
        for s_ref, p_ref, q_ref in ((sl_ref, pl_ref, qlt_ref), (sr_ref, pr_ref, qrt_ref)):
            if at < s_ref.shape[0]:
                rows, off, other = load_block(s_ref, at)
                jobs.append((rows, other, s_ref, p_ref, q_ref, eliminate(rows, off)))
        live = [j[5] for j in jobs]
        while live:
            live = [g for g in live if next(g, 1) is None]
        for rows, other, s_ref, p_ref, q_ref, _ in jobs:
            apply_block(rows, other, s_ref, p_ref, q_ref, at)
    start = pl.multiple_of(member_ref[0] * 40, 8)
    own = qlt_ref[pl.ds(start, 40), :]
    rotated = mm(mm(own, tile_ref[...]) * factor_ref[0], qrt_ref[...], 1, 1)
    moment = beta_first * fm_ref[...] + (1.0 - beta_first) * rotated
    second = beta_second * sm_ref[...] + (1.0 - beta_second) * rotated * rotated
    direction = moment / first_bias / (jnp.sqrt(second / second_bias) + 1e-08)
    m_ref[...] = moment
    v_ref[...] = second
    turned_ref[...] = mm(direction, qrt_ref[...])


def refresh(member, factor, gl, bl, gr, br, tile, fm, sm):
    f32 = jnp.float32
    smem = pl.BlockSpec(memory_space=pltpu.SMEM)
    vmem = pl.BlockSpec(memory_space=pltpu.VMEM)
    return pl.pallas_call(
        refresh_kernel,
        out_shape=(
            jax.ShapeDtypeStruct((LB, LB), f32),
            jax.ShapeDtypeStruct((RB, RB), f32),
            jax.ShapeDtypeStruct((40, RB), f32),
            jax.ShapeDtypeStruct((40, RB), f32),
            jax.ShapeDtypeStruct((40, RB), f32),
        ),
        in_specs=[smem, smem] + [vmem] * 7,
        out_specs=(vmem,) * 5,
        scratch_shapes=[
            pltpu.VMEM((LB, LB), f32),
            pltpu.VMEM((LB, LB), f32),
            pltpu.VMEM((RB, RB), f32),
            pltpu.VMEM((RB, RB), f32),
        ],
        compiler_params=pltpu.CompilerParams(vmem_limit_bytes=24 * 2**20),
        cost_estimate=pl.CostEstimate(
            flops=40_000_000_000, bytes_accessed=4_000_000, transcendentals=0
        ),
        name="refresh",
    )(member, factor, gl, bl, gr, br, tile, fm, sm)


def place_kernel(y_ref, *refs):
    halves, out_ref = refs[:-1], refs[-1]
    y = y_ref[0]
    for n, (shift, first, count) in enumerate(PLACES):
        source = lax.rem(y + shift + 8, 8)
        at = pl.multiple_of(source * 160 + first, 16)
        out_ref[pl.ds(at, count), :] = halves[n][...].astype(jnp.bfloat16)


PLACES = (
    (0, 0, 160), (-1, 0, 160), (-2, 0, 160), (-3, 0, 160), (-4, 0, 80),
    (1, 0, 160), (2, 0, 160), (3, 0, 160), (4, 80, 80),
)


def place(y, halves):
    vmem = pl.BlockSpec(memory_space=pltpu.VMEM)
    return pl.pallas_call(
        place_kernel,
        out_shape=jax.ShapeDtypeStruct((1280, RB), jnp.bfloat16),
        in_specs=[pl.BlockSpec(memory_space=pltpu.SMEM)] + [vmem] * len(halves),
        out_specs=vmem,
        compiler_params=pltpu.CompilerParams(vmem_limit_bytes=16 * 2**20),
        name="place",
    )(y, *halves)


def gather_all(x, axes, count):
    copies = jnp.broadcast_to(x[None], (count,) + x.shape)
    return lax.all_to_all(copies, axes, 0, 0, tiled=True)


def shift_perm(size, by):
    return [(s, (s + by) % size) for s in range(size)]


def shards(
    pseudo_grads, left_gram, right_gram, left_basis, right_basis, first_moment, second_moment
):
    k = lax.axis_index("yk")
    x = lax.axis_index("x")
    y = lax.axis_index(("yk", "y2"))
    member = lax.axis_index(MEMBERS)

    held = jnp.concatenate([left_gram, left_basis], axis=0)
    moved = jnp.where(x == k, held, 0.0)
    for by in range(1, 4):
        moved = moved + lax.ppermute(
            held, ("yk", "x"), [(b * 4 + b, b * 4 + (b + by) % 4) for b in range(4)]
        )
    gram_k, basis_k = moved[0], moved[1]

    pieces = pseudo_grads[0].astype(jnp.float32).reshape(32, 40, RB)
    arrived = lax.all_to_all(pieces, REP, 0, 0, tiled=True)
    own = jnp.sum(arrived, axis=0) * (1.0 / 32.0)

    tile = gather_all(own, MEMBERS, 8).reshape(LB, RB)
    squares = jnp.full((8, RB), jnp.sum(tile * tile), jnp.float32)
    tiles = [tile] + [lax.ppermute(tile, "x", shift_perm(4, by)) for by in range(1, 4)]
    row_squares = squares
    for by in range(1, 4):
        row_squares = row_squares + lax.ppermute(squares, "x", shift_perm(4, by))

    right_part = mm(tile, tile, 0, 0).reshape(16, 16, RB)
    right_own = jnp.sum(lax.all_to_all(right_part, RIGHT_GROUP, 0, 0, tiled=True), axis=0)
    right_all = gather_all(jnp.concatenate([right_own, row_squares], axis=0), RIGHT_GROUP, 16)
    right_raw = right_all[:, :16].reshape(RB, RB)
    total = jnp.sum(right_all[:, 16, 0])
    factor = clip_ratio * math.sqrt(D * KV) / (jnp.sqrt(total) + 1e-06)
    weight = (1.0 - beta_gram) * factor * factor
    right_new = beta_gram * right_gram[0] + weight * right_raw

    left_raw = mm(tiles[0], tiles[0], 1, 1)
    for t in tiles[1:]:
        left_raw = left_raw + mm(t, t, 1, 1)
    left_new = beta_gram * gram_k + weight * left_raw
    swap = [(a * 4 + b, b * 4 + a) for a in range(4) for b in range(4)]
    left_new_out = lax.ppermute(left_new, ("yk", "x"), swap)

    qlt, qrt, moment, second, turned = refresh(
        member.astype(jnp.int32).reshape(1), factor.reshape(1), left_new, basis_k,
        right_new, right_basis[0], tile, first_moment, second_moment,
    )
    left_basis_out = lax.ppermute(qlt, ("yk", "x"), swap).T

    whole_turned = gather_all(turned, MEMBERS, 8).reshape(LB, RB)
    half = lax.dynamic_slice_in_dim(qlt, lax.axis_index("y2") * 160, 160, 1)
    mine = mm(half, whole_turned, 0, 0)
    ring = ("yk", "y2")
    right, left = [mine], [mine]
    for step in range(1, 4):
        right.append(lax.ppermute(right[-1], ring, shift_perm(8, 1)))
        left.append(lax.ppermute(left[-1], ring, shift_perm(8, -1)))
    right.append(lax.ppermute(right[-1][:80], ring, shift_perm(8, 1)))
    left.append(lax.ppermute(left[-1][80:], ring, shift_perm(8, -1)))
    update = place(y.astype(jnp.int32).reshape(1), right + left[1:])
    return (
        update, left_new_out[None], left_basis_out[None], right_new[None], qrt.T[None],
        moment, second,
    )


def solution(mesh):
    fine = Mesh(
        mesh.devices.reshape(4, 2, 4, 2, 2, 4), ("yk", "y2", "zh", "zl", "core", "x")
    )
    left = P(ROW + ("x",), None, None)
    right = P("x", None, None)
    moments = P(ROW + REP, "x")
    return jax.shard_map(
        shards,
        mesh=fine,
        in_specs=(P(REP, ROW, "x"), left, right, left, right, moments, moments),
        out_specs=(P(ROW, "x"), left, left, right, right, moments, moments),
        check_vma=False,
    )
```

time: 728 us -> 269 us (0.37)
  waiting for transfers between devices: 484 us -> 117 us
  other arithmetic: 146 us -> 8.65 us
  starting transfers between devices: 0.78 us -> 101 us
  blocking collectives: 26.8 us -> 0 us
  matrix products: 30.9 us -> 7.84 us
  Pallas kernels: 0 us -> 21.1 us
  between operations: 18.5 us -> 1.86 us
  local copies, waits for them, and re-layouts: 16.5 us -> 7.93 us
    psum x2 -> x0, waiting for transfers between devices: 366 us -> none  [the longest x1 328 us: shards(): average = lax.psum(local_grad, 'rep') / replicas]
    another operation x25 -> x0, other arithmetic: 136 us -> none  [the longest x16 86.7 us: refresh(): factor = jnp.linalg.cholesky(crossed)]
    all_gather x2 -> x0, waiting for transfers between devices: 85.5 us -> none  [the longest x1 85.5 us: shards(): whole_direction = lax.all_gather(direction, 'rep', axis=0, tiled=True)]
    all_to_all x0 -> x5, waiting for transfers between devices: none -> 61.5 us  [the longest x3 31.4 us: gather_all(): return lax.all_to_all(copies, axes, 0, 0, tiled=True)]
    ppermute x0 -> x19, starting transfers between devices: none -> 59.2 us  [the longest x3 10.4 us: shards(): row_squares = row_squares + lax.ppermute(squares, 'x', shift_perm(4, by))]
    ppermute x0 -> x19, waiting for transfers between devices: none -> 55.5 us  [the longest x3 53 us: shards(): left.append(lax.ppermute(left[-1], ring, shift_perm(8, -1)))]
    all_to_all x0 -> x5, starting transfers between devices: none -> 41.3 us  [the longest x3 19.6 us: gather_all(): return lax.all_to_all(copies, axes, 0, 0, tiled=True)]
    reduce_scatter x1 -> x0, waiting for transfers between devices: 31.9 us -> none  [shards(): lax.psum_scatter(left_part, 'tcol', scatter_dimension=0, tiled=True)]
  transfers between devices with their start and end apart: 5 -> 24, of which waited for: 4 -> 8; matrix products, arithmetic and copies ran while one was open for 9% -> 6% of each run, Pallas kernels for 0% -> 0%
where the time goes in v1:
time: 269 us; the launch traced here: 265 us
  waiting for transfers between devices  117 us (43%)
  starting transfers between devices  101 us (38%)
  Pallas kernels  21.1 us (8%)
  other arithmetic  8.65 us (3%)
  local copies, waits for them, and re-layouts  7.93 us (3%)
  matrix products  7.84 us (3%)
    ppermute x3, waiting for transfers between devices, shards(): left.append(lax.ppermute(left[-1], ring, shift_perm(8, -1)))  53 us
    all_to_all x3, waiting for transfers between devices, gather_all(): return lax.all_to_all(copies, axes, 0, 0, tiled=True)  31.4 us
    all_to_all x1, waiting for transfers between devices, shards(): arrived = lax.all_to_all(pieces, REP, 0, 0, tiled=True)  30 us
    pallas_call x1, Pallas kernels, refresh(): pl.pallas_call(refresh_kernel, out_shape=(jax.ShapeDtypeStruct((LB, LB),...  20.2 us
    all_to_all x3, starting transfers between devices, gather_all(): return lax.all_to_all(copies, axes, 0, 0, tiled=True)  19.6 us
    all_to_all x1, starting transfers between devices, shards(): arrived = lax.all_to_all(pieces, REP, 0, 0, tiled=True)  16.1 us
    ppermute x3, starting transfers between devices, shards(): row_squares = row_squares + lax.ppermute(squares, 'x', shift_perm(4, by))  10.4 us
    ppermute x3, starting transfers between devices, shards(): left.append(lax.ppermute(left[-1], ring, shift_perm(8, -1)))  9.72 us
  transfers between devices with their start and end apart: 24, of which 8 were waited for; matrix products, arithmetic and copies ran while one was open for 6% of the time, Pallas kernels for 0%

profile of v1, /device:TPU:6, one launch (start us, length us, event | category | flops | bytes accessed | tf_op | source)
XLA Modules:
  0.0 265.0 jit_solution(15373298221742181097)
XLA Ops:
  0.6 2.3 convert.1
  2.9 16.1 %all-to-all-start = ((f32[32,40,256]{2,1,0:T(8,128)}), f32[32,40,256]{2,1,0:T(8,128)S(1)}, u32[]{:S(2)}, u32[]{:S(2)}) async-start(f32[32,40,256]{2,1,0:T(8,128)} %convert.1), calls=%async_computation | async-start | bytes 2621440 | tf_op jit(solution)/shard_map/all_to_all | solution.py:215
  19.1 1.3 collective-permute-start.5
  20.4 1.6 collective-permute-start.4
  22.0 1.6 collective-permute-start.3
  23.6 30.0 %all-to-all-done = f32[32,40,256]{2,1,0:T(8,128)S(1)} async-done(((f32[32,40,256]{2,1,0:T(8,128)}), f32[32,40,256]{2,1,0:T(8,128)S(1)}, u32[]{:S(2)}, u32[]{:S(2)}) %all-to-all-start) | async-done | bytes 1310752 | tf_op jit(solution)/shard_map/all_to_all | solution.py:215
  53.8 0.7 broadcast_in_dim.18
  54.5 6.0 %all-to-all-start.1 = ((f32[8,40,256]{2,1,0:T(8,128)}), f32[8,40,256]{2,1,0:T(8,128)S(1)}, u32[]{:S(2)}, u32[]{:S(2)}) async-start(f32[8,40,256]{2,1,0:T(8,128)} %broadcast_in_dim.18), calls=%async_computation.1 | async-start | bytes 655360 | tf_op jit(solution)/shard_map/all_to_all | solution.py:191
  60.5 1.7 add_add_fusion
  62.2 9.5 %all-to-all-done.1 = f32[8,40,256]{2,1,0:T(8,128)S(1)} async-done(((f32[8,40,256]{2,1,0:T(8,128)}), f32[8,40,256]{2,1,0:T(8,128)S(1)}, u32[]{:S(2)}, u32[]{:S(2)}) %all-to-all-start.1) | async-done | bytes 327712 | tf_op jit(solution)/shard_map/all_to_all | solution.py:191
  71.9 1.3 fusion.7
  73.2 5.6 %all-to-all-start.2 = ((f32[16,16,256]{2,1,0:T(8,128)}), f32[16,16,256]{2,1,0:T(8,128)S(1)}, u32[]{:S(2)}, u32[]{:S(2)}) async-start(f32[16,16,256]{2,1,0:T(8,128)} %fusion.7), calls=%async_computation.2 | async-start | bytes 524288 | tf_op jit(solution)/shard_map/all_to_all | solution.py:226
  80.2 3.3 %collective-permute-start.1 = (f32[8,256]{1,0:T(8,128)S(1)}, f32[8,256]{1,0:T(8,128)S(1)}, u32[]{:S(2)}, u32[]{:S(2)}) collective-permute-start(f32[8,256]{1,0:T(8,128)S(1)} %broadcast_in_dim.36), channel_id=1, source_target_pairs={{0,2},{1,3},{2,0},{3,1},{4,6},{5,7},{6,4},{7,5},{8,10},{9,11},{10,... | collective-permute-start | bytes 24584 | tf_op jit(solution)/shard_map/ppermute | solution.py:223
  83.5 1.9 collective-permute-start.2
  85.4 5.1 %collective-permute-start = (f32[8,256]{1,0:T(8,128)S(1)}, f32[8,256]{1,0:T(8,128)S(1)}, u32[]{:S(2)}, u32[]{:S(2)}) collective-permute-start(f32[8,256]{1,0:T(8,128)S(1)} %broadcast_in_dim.36), channel_id=1, source_target_pairs={{0,1},{1,2},{2,3},{3,0},{4,5},{5,6},{6,7},{7,4},{8,9},{9,10},{10,1... | collective-permute-start | bytes 24584 | tf_op jit(solution)/shard_map/ppermute | solution.py:223
  90.6 2.8 %collective-permute-start.7 = (f32[320,256]{1,0:T(8,128)S(1)}, f32[320,256]{1,0:T(8,128)}, u32[]{:S(2)}, u32[]{:S(2)}) collective-permute-start(f32[320,256]{1,0:T(8,128)S(1)} %bitcast.46), channel_id=1, source_target_pairs={{0,2},{1,3},{2,0},{3,1},{4,6},{5,7},{6,4},{7,5},{8,10},{9,11},{10,... | collective-permute-start | bytes 983048 | tf_op jit(solution)/shard_map/ppermute | solution.py:220
  93.4 2.5 collective-permute-start.6
  96.0 3.3 %collective-permute-start.8 = (f32[320,256]{1,0:T(8,128)S(1)}, f32[320,256]{1,0:T(8,128)}, u32[]{:S(2)}, u32[]{:S(2)}) collective-permute-start(f32[320,256]{1,0:T(8,128)S(1)} %bitcast.48), channel_id=1, source_target_pairs={{0,3},{1,0},{2,1},{3,2},{4,7},{5,4},{6,5},{7,6},{8,11},{9,8},{10,9... | collective-permute-start | bytes 983048 | tf_op jit(solution)/shard_map/ppermute | solution.py:220
  100.0 0.8 broadcast_in_dim.37
  100.8 8.3 %all-to-all-start.3 = ((f32[16,24,256]{2,1,0:T(8,128)}), f32[16,24,256]{2,1,0:T(8,128)}, u32[]{:S(2)}, u32[]{:S(2)}) async-start(f32[16,24,256]{2,1,0:T(8,128)} %broadcast_in_dim.37), calls=%async_computation.3 | async-start | bytes 786432 | tf_op jit(solution)/shard_map/all_to_all | solution.py:191
  110.3 1.7 fusion.9
  112.1 1.5 convolution_add_fusion.1
  113.6 9.1 %all-to-all-done.3 = f32[16,24,256]{2,1,0:T(8,128)} async-done(((f32[16,24,256]{2,1,0:T(8,128)}), f32[16,24,256]{2,1,0:T(8,128)}, u32[]{:S(2)}, u32[]{:S(2)}) %all-to-all-start.3) | async-done | bytes 393248 | tf_op jit(solution)/shard_map/all_to_all | solution.py:191
  122.7 1.5 slice_reduce_fusion
  124.9 1.0 slice_multiply_fusion.1
  126.1 1.8 fusion.3.gl_ref
  127.9 20.2 %refresh.1 = (f32[320,320]{1,0:T(8,128)S(1)}, f32[256,256]{1,0:T(8,128)S(1)}, f32[40,256]{1,0:T(8,128)}, f32[40,256]{1,0:T(8,128)}, f32[40,256]{1,0:T(8,128)S(1)}) custom-call(s32[1]{0:T(128)} %bitcast.1.member_ref, f32[1]{0:T(128)} %bitcast.7.factor_ref, f32[320,320]{1,0:T(8,128)S(1)} %fusion.3.gl_ref, f32[320,320]{1,0:T(8,128)S(1)} %slice_bitcast_fusion.bl_ref, ...), custom_call_target="tpu_custom_call" | custom-call | flops 40000000000 | bytes 4000000 | tf_op jit(solution)/shard_map/refresh/pallas_call | solution.py:137
  148.1 0.7 broadcast_in_dim.39
  148.9 5.3 %all-to-all-start.4 = ((f32[8,40,256]{2,1,0:T(8,128)}), f32[8,40,256]{2,1,0:T(8,128)S(1)}, u32[]{:S(2)}, u32[]{:S(2)}) async-start(f32[8,40,256]{2,1,0:T(8,128)} %broadcast_in_dim.39), calls=%async_computation.4 | async-start | bytes 655360 | tf_op jit(solution)/shard_map/all_to_all | solution.py:191
  154.2 12.8 %all-to-all-done.4 = f32[8,40,256]{2,1,0:T(8,128)S(1)} async-done(((f32[8,40,256]{2,1,0:T(8,128)}), f32[8,40,256]{2,1,0:T(8,128)S(1)}, u32[]{:S(2)}, u32[]{:S(2)}) %all-to-all-start.4) | async-done | bytes 327712 | tf_op jit(solution)/shard_map/all_to_all | solution.py:191
  166.9 0.9 fusion.4.refs_0_
  167.8 3.3 %collective-permute-start.13 = (f32[160,256]{1,0:T(8,128)S(1)}, f32[160,256]{1,0:T(8,128)S(1)}, u32[]{:S(2)}, u32[]{:S(2)}) collective-permute-start(f32[160,256]{1,0:T(8,128)S(1)} %fusion.4.refs_0_), channel_id=1, source_target_pairs={{0,448},{64,0},{128,64},{192,128},{256,192},{320,256},{384,320},{4... | collective-permute-start | bytes 491528 | tf_op jit(solution)/shard_map/ppermute | solution.py:254
  171.1 2.5 collective-permute-start.9
  173.7 1.4 collective-permute-done.13.refs_5_
  175.0 4.5 %collective-permute-start.14 = (f32[160,256]{1,0:T(8,128)S(1)}, f32[160,256]{1,0:T(8,128)S(1)}, u32[]{:S(2)}, u32[]{:S(2)}) collective-permute-start(f32[160,256]{1,0:T(8,128)S(1)} %collective-permute-done.13.refs_5_), channel_id=1, source_target_pairs={{0,448},{64,0},{128,64},{192,128},{256,192},{320,256},{384,320},{4... | collective-permute-start | bytes 491528 | tf_op jit(solution)/shard_map/ppermute | solution.py:254
  179.5 1.9 collective-permute-start.10
  181.5 4.6 %collective-permute-start.18 = (f32[320,320]{1,0:T(8,128)S(1)}, f32[320,320]{1,0:T(8,128)}, u32[]{:S(2)}, u32[]{:S(2)}) collective-permute-start(f32[320,320]{1,0:T(8,128)S(1)} %get-tuple-element.12), channel_id=1, source_target_pairs={{0,0},{1,128},{2,256},{3,384},{128,1},{129,129},{130,257},{131,385... | collective-permute-start | bytes 1228808 | tf_op jit(solution)/shard_map/ppermute | solution.py:245
  186.1 5.4 %collective-permute-start.17 = (f32[320,320]{1,0:T(8,128)S(1)}, f32[320,320]{1,0:T(8,128)}, u32[]{:S(2)}, u32[]{:S(2)}) collective-permute-start(f32[320,320]{1,0:T(8,128)S(1)} %fusion.3.gl_ref), channel_id=1, source_target_pairs={{0,0},{1,128},{2,256},{3,384},{128,1},{129,129},{130,257},{131,385... | collective-permute-start | bytes 1228808 | tf_op jit(solution)/shard_map/ppermute | solution.py:239
  191.5 1.9 collective-permute-start.15
  193.5 3.9 %collective-permute-start.11 = (f32[160,256]{1,0:T(8,128)S(1)}, f32[160,256]{1,0:T(8,128)S(1)}, u32[]{:S(2)}, u32[]{:S(2)}) collective-permute-start(f32[160,256]{1,0:T(8,128)S(1)} %collective-permute-done.10.refs_2_), channel_id=1, source_target_pairs={{0,64},{64,128},{128,192},{192,256},{256,320},{320,384},{384,448},... | collective-permute-start | bytes 491528 | tf_op jit(solution)/shard_map/ppermute | solution.py:253
  197.4 51.6 %collective-permute-done.15.refs_7_ = f32[160,256]{1,0:T(8,128)S(1)} collective-permute-done((f32[160,256]{1,0:T(8,128)S(1)}, f32[160,256]{1,0:T(8,128)S(1)}, u32[]{:S(2)}, u32[]{:S(2)}) %collective-permute-start.15) | collective-permute-done | bytes 163872 | tf_op jit(solution)/shard_map/ppermute | solution.py:254
  249.1 5.6 %collective-permute-start.16 = (f32[80,256]{1,0:T(8,128)S(1)}, f32[80,256]{1,0:T(8,128)S(1)}, u32[]{:S(2)}, u32[]{:S(2)}) collective-permute-start(f32[80,256]{1,0:T(8,128)S(1)} %slice.29), channel_id=1, source_target_pairs={{0,448},{64,0},{128,64},{192,128},{256,192},{320,256},{384,320},{4... | collective-permute-start | bytes 245768 | tf_op jit(solution)/shard_map/ppermute | solution.py:256
  254.7 1.9 collective-permute-start.12
  257.3 0.8 copy.19
  258.2 2.0 copy.18
  260.2 2.0 collective-permute-done.12.refs_4_
  262.2 0.9 place.1
  263.1 1.8 copy.22
  (47 shorter events, 4.4 us)
Async XLA Ops:
  2.9 16.1 %copy-start.5 = (f32[1,320,320]{2,1,0:T(8,128)S(1)}, f32[1,320,320]{2,1,0:T(8,128)}, u32[]{:S(2)}) copy-start(f32[1,320,320]{2,1,0:T(8,128)} %param.8) | copy-start | bytes 1228804
  2.9 16.2 %copy-start.6 = (f32[1,320,320]{2,1,0:T(8,128)S(1)}, f32[1,320,320]{2,1,0:T(8,128)}, u32[]{:S(2)}) copy-start(f32[1,320,320]{2,1,0:T(8,128)} %param.10) | copy-start | bytes 1228804
  2.9 50.8 %all-to-all-start = ((f32[32,40,256]{2,1,0:T(8,128)}), f32[32,40,256]{2,1,0:T(8,128)S(1)}, u32[]{:S(2)}, u32[]{:S(2)}) async-start(f32[32,40,256]{2,1,0:T(8,128)} %convert.1), calls=%async_computation | async-start | bytes 2621440 | tf_op jit(solution)/shard_map/all_to_all | solution.py:215
  19.1 41.4 %collective-permute-start.5 = (f32[2,320,320]{2,1,0:T(8,128)S(1)}, f32[2,320,320]{2,1,0:T(8,128)S(1)}, u32[]{:S(2)}, u32[]{:S(2)}) collective-permute-start(f32[2,320,320]{2,1,0:T(8,128)S(1)} %constant_dynamic-update-slice_fusion), channel_id=1, source_target_pairs={{0,3},{129,128},{258,257},{387,386},{4,7},{133,132},{262,261},{391... | collective-permute-start | bytes 2457608 | tf_op jit(solution)/shard_map/ppermute | solution.py:209
  20.4 40.1 %collective-permute-start.4 = (f32[2,320,320]{2,1,0:T(8,128)S(1)}, f32[2,320,320]{2,1,0:T(8,128)}, u32[]{:S(2)}, u32[]{:S(2)}) collective-permute-start(f32[2,320,320]{2,1,0:T(8,128)S(1)} %constant_dynamic-update-slice_fusion), channel_id=1, source_target_pairs={{0,2},{129,131},{258,256},{387,385},{4,6},{133,135},{262,260},{391... | collective-permute-start | bytes 2457608 | tf_op jit(solution)/shard_map/ppermute | solution.py:209
  22.0 38.5 %collective-permute-start.3 = (f32[2,320,320]{2,1,0:T(8,128)S(1)}, f32[2,320,320]{2,1,0:T(8,128)}, u32[]{:S(2)}, u32[]{:S(2)}) collective-permute-start(f32[2,320,320]{2,1,0:T(8,128)S(1)} %constant_dynamic-update-slice_fusion), channel_id=1, source_target_pairs={{0,1},{129,130},{258,259},{387,384},{4,5},{133,134},{262,263},{391... | collective-permute-start | bytes 2457608 | tf_op jit(solution)/shard_map/ppermute | solution.py:209
  54.5 17.2 %all-to-all-start.1 = ((f32[8,40,256]{2,1,0:T(8,128)}), f32[8,40,256]{2,1,0:T(8,128)S(1)}, u32[]{:S(2)}, u32[]{:S(2)}) async-start(f32[8,40,256]{2,1,0:T(8,128)} %broadcast_in_dim.18), calls=%async_computation.1 | async-start | bytes 655360 | tf_op jit(solution)/shard_map/all_to_all | solution.py:191
  73.2 26.8 %all-to-all-start.2 = ((f32[16,16,256]{2,1,0:T(8,128)}), f32[16,16,256]{2,1,0:T(8,128)S(1)}, u32[]{:S(2)}, u32[]{:S(2)}) async-start(f32[16,16,256]{2,1,0:T(8,128)} %fusion.7), calls=%async_computation.2 | async-start | bytes 524288 | tf_op jit(solution)/shard_map/all_to_all | solution.py:226
  80.2 15.8 %collective-permute-start.1 = (f32[8,256]{1,0:T(8,128)S(1)}, f32[8,256]{1,0:T(8,128)S(1)}, u32[]{:S(2)}, u32[]{:S(2)}) collective-permute-start(f32[8,256]{1,0:T(8,128)S(1)} %broadcast_in_dim.36), channel_id=1, source_target_pairs={{0,2},{1,3},{2,0},{3,1},{4,6},{5,7},{6,4},{7,5},{8,10},{9,11},{10,... | collective-permute-start | bytes 24584 | tf_op jit(solution)/shard_map/ppermute | solution.py:223
  83.5 15.8 %collective-permute-start.2 = (f32[8,256]{1,0:T(8,128)S(1)}, f32[8,256]{1,0:T(8,128)S(1)}, u32[]{:S(2)}, u32[]{:S(2)}) collective-permute-start(f32[8,256]{1,0:T(8,128)S(1)} %broadcast_in_dim.36), channel_id=1, source_target_pairs={{0,3},{1,0},{2,1},{3,2},{4,7},{5,4},{6,5},{7,6},{8,11},{9,8},{10,9... | collective-permute-start | bytes 24584 | tf_op jit(solution)/shard_map/ppermute | solution.py:223
  85.4 13.9 %collective-permute-start = (f32[8,256]{1,0:T(8,128)S(1)}, f32[8,256]{1,0:T(8,128)S(1)}, u32[]{:S(2)}, u32[]{:S(2)}) collective-permute-start(f32[8,256]{1,0:T(8,128)S(1)} %broadcast_in_dim.36), channel_id=1, source_target_pairs={{0,1},{1,2},{2,3},{3,0},{4,5},{5,6},{6,7},{7,4},{8,9},{9,10},{10,1... | collective-permute-start | bytes 24584 | tf_op jit(solution)/shard_map/ppermute | solution.py:223
  90.6 35.4 %collective-permute-start.7 = (f32[320,256]{1,0:T(8,128)S(1)}, f32[320,256]{1,0:T(8,128)}, u32[]{:S(2)}, u32[]{:S(2)}) collective-permute-start(f32[320,256]{1,0:T(8,128)S(1)} %bitcast.46), channel_id=1, source_target_pairs={{0,2},{1,3},{2,0},{3,1},{4,6},{5,7},{6,4},{7,5},{8,10},{9,11},{10,... | collective-permute-start | bytes 983048 | tf_op jit(solution)/shard_map/ppermute | solution.py:220
  93.4 18.7 %collective-permute-start.6 = (f32[320,256]{1,0:T(8,128)S(1)}, f32[320,256]{1,0:T(8,128)S(1)}, u32[]{:S(2)}, u32[]{:S(2)}) collective-permute-start(f32[320,256]{1,0:T(8,128)S(1)} %bitcast.47), channel_id=1, source_target_pairs={{0,1},{1,2},{2,3},{3,0},{4,5},{5,6},{6,7},{7,4},{8,9},{9,10},{10,1... | collective-permute-start | bytes 983048 | tf_op jit(solution)/shard_map/ppermute | solution.py:220
  96.0 14.4 %collective-permute-start.8 = (f32[320,256]{1,0:T(8,128)S(1)}, f32[320,256]{1,0:T(8,128)}, u32[]{:S(2)}, u32[]{:S(2)}) collective-permute-start(f32[320,256]{1,0:T(8,128)S(1)} %bitcast.48), channel_id=1, source_target_pairs={{0,3},{1,0},{2,1},{3,2},{4,7},{5,4},{6,5},{7,6},{8,11},{9,8},{10,9... | collective-permute-start | bytes 983048 | tf_op jit(solution)/shard_map/ppermute | solution.py:220
  100.8 21.9 %all-to-all-start.3 = ((f32[16,24,256]{2,1,0:T(8,128)}), f32[16,24,256]{2,1,0:T(8,128)}, u32[]{:S(2)}, u32[]{:S(2)}) async-start(f32[16,24,256]{2,1,0:T(8,128)} %broadcast_in_dim.37), calls=%async_computation.3 | async-start | bytes 786432 | tf_op jit(solution)/shard_map/all_to_all | solution.py:191
  112.1 13.9 %copy-start.4 = (f32[1,256,256]{2,1,0:T(8,128)S(1)}, f32[1,256,256]{2,1,0:T(8,128)}, u32[]{:S(2)}) copy-start(f32[1,256,256]{2,1,0:T(8,128)} %param.9) | copy-start | bytes 786436
  124.9 1.2 copy-start.3
  126.0 1.9 copy-start
  126.0 1.9 copy-start.1
  126.0 1.9 copy-start.2
  148.9 18.1 %all-to-all-start.4 = ((f32[8,40,256]{2,1,0:T(8,128)}), f32[8,40,256]{2,1,0:T(8,128)S(1)}, u32[]{:S(2)}, u32[]{:S(2)}) async-start(f32[8,40,256]{2,1,0:T(8,128)} %broadcast_in_dim.39), calls=%async_computation.4 | async-start | bytes 655360 | tf_op jit(solution)/shard_map/all_to_all | solution.py:191
  167.8 7.2 %collective-permute-start.13 = (f32[160,256]{1,0:T(8,128)S(1)}, f32[160,256]{1,0:T(8,128)S(1)}, u32[]{:S(2)}, u32[]{:S(2)}) collective-permute-start(f32[160,256]{1,0:T(8,128)S(1)} %fusion.4.refs_0_), channel_id=1, source_target_pairs={{0,448},{64,0},{128,64},{192,128},{256,192},{320,256},{384,320},{4... | collective-permute-start | bytes 491528 | tf_op jit(solution)/shard_map/ppermute | solution.py:254
  171.1 8.4 %collective-permute-start.9 = (f32[160,256]{1,0:T(8,128)S(1)}, f32[160,256]{1,0:T(8,128)S(1)}, u32[]{:S(2)}, u32[]{:S(2)}) collective-permute-start(f32[160,256]{1,0:T(8,128)S(1)} %fusion.4.refs_0_), channel_id=1, source_target_pairs={{0,64},{64,128},{128,192},{192,256},{256,320},{320,384},{384,448},... | collective-permute-start | bytes 491528 | tf_op jit(solution)/shard_map/ppermute | solution.py:253
  175.0 16.5 %collective-permute-start.14 = (f32[160,256]{1,0:T(8,128)S(1)}, f32[160,256]{1,0:T(8,128)S(1)}, u32[]{:S(2)}, u32[]{:S(2)}) collective-permute-start(f32[160,256]{1,0:T(8,128)S(1)} %collective-permute-done.13.refs_5_), channel_id=1, source_target_pairs={{0,448},{64,0},{128,64},{192,128},{256,192},{320,256},{384,320},{4... | collective-permute-start | bytes 491528 | tf_op jit(solution)/shard_map/ppermute | solution.py:254
  179.5 13.9 %collective-permute-start.10 = (f32[160,256]{1,0:T(8,128)S(1)}, f32[160,256]{1,0:T(8,128)S(1)}, u32[]{:S(2)}, u32[]{:S(2)}) collective-permute-start(f32[160,256]{1,0:T(8,128)S(1)} %collective-permute-done.9.refs_1_), channel_id=1, source_target_pairs={{0,64},{64,128},{128,192},{192,256},{256,320},{320,384},{384,448},... | collective-permute-start | bytes 491528 | tf_op jit(solution)/shard_map/ppermute | solution.py:253
  181.5 76.7 %collective-permute-start.18 = (f32[320,320]{1,0:T(8,128)S(1)}, f32[320,320]{1,0:T(8,128)}, u32[]{:S(2)}, u32[]{:S(2)}) collective-permute-start(f32[320,320]{1,0:T(8,128)S(1)} %get-tuple-element.12), channel_id=1, source_target_pairs={{0,0},{1,128},{2,256},{3,384},{128,1},{129,129},{130,257},{131,385... | collective-permute-start | bytes 1228808 | tf_op jit(solution)/shard_map/ppermute | solution.py:245
  186.1 74.1 %collective-permute-start.17 = (f32[320,320]{1,0:T(8,128)S(1)}, f32[320,320]{1,0:T(8,128)}, u32[]{:S(2)}, u32[]{:S(2)}) collective-permute-start(f32[320,320]{1,0:T(8,128)S(1)} %fusion.3.gl_ref), channel_id=1, source_target_pairs={{0,0},{1,128},{2,256},{3,384},{128,1},{129,129},{130,257},{131,385... | collective-permute-start | bytes 1228808 | tf_op jit(solution)/shard_map/ppermute | solution.py:239
  191.5 57.5 %collective-permute-start.15 = (f32[160,256]{1,0:T(8,128)S(1)}, f32[160,256]{1,0:T(8,128)S(1)}, u32[]{:S(2)}, u32[]{:S(2)}) collective-permute-start(f32[160,256]{1,0:T(8,128)S(1)} %collective-permute-done.14.refs_6_), channel_id=1, source_target_pairs={{0,448},{64,0},{128,64},{192,128},{256,192},{320,256},{384,320},{4... | collective-permute-start | bytes 491528 | tf_op jit(solution)/shard_map/ppermute | solution.py:254
  193.5 61.2 %collective-permute-start.11 = (f32[160,256]{1,0:T(8,128)S(1)}, f32[160,256]{1,0:T(8,128)S(1)}, u32[]{:S(2)}, u32[]{:S(2)}) collective-permute-start(f32[160,256]{1,0:T(8,128)S(1)} %collective-permute-done.10.refs_2_), channel_id=1, source_target_pairs={{0,64},{64,128},{128,192},{192,256},{256,320},{320,384},{384,448},... | collective-permute-start | bytes 491528 | tf_op jit(solution)/shard_map/ppermute | solution.py:253
  249.1 11.2 %collective-permute-start.16 = (f32[80,256]{1,0:T(8,128)S(1)}, f32[80,256]{1,0:T(8,128)S(1)}, u32[]{:S(2)}, u32[]{:S(2)}) collective-permute-start(f32[80,256]{1,0:T(8,128)S(1)} %slice.29), channel_id=1, source_target_pairs={{0,448},{64,0},{128,64},{192,128},{256,192},{320,256},{384,320},{4... | collective-permute-start | bytes 245768 | tf_op jit(solution)/shard_map/ppermute | solution.py:256
  254.7 7.5 %collective-permute-start.12 = (f32[80,256]{1,0:T(8,128)S(1)}, f32[80,256]{1,0:T(8,128)S(1)}, u32[]{:S(2)}, u32[]{:S(2)}) collective-permute-start(f32[80,256]{1,0:T(8,128)S(1)} %slice.28), channel_id=1, source_target_pairs={{0,64},{64,128},{128,192},{192,256},{256,320},{320,384},{384,448},... | collective-permute-start | bytes 245768 | tf_op jit(solution)/shard_map/ppermute | solution.py:255

commit v2 on v1

v2 whole, which is shorter than its diff:
```python
import math

import jax
import jax.numpy as jnp
from jax import lax
from jax.experimental import pallas as pl
from jax.experimental.pallas import tpu as pltpu
from jax.sharding import Mesh, PartitionSpec as P

D = 5120
KV = 1024
LB = 320
RB = 256
NB = 64

highest = lax.Precision.HIGHEST
beta_gram = 0.95
beta_first = 0.95
beta_second = 0.95
first_bias = 1.0 - 0.95**4
second_bias = 1.0 - 0.95**4
clip_ratio = 0.5

REP = ("yk", "y2", "zh")
ROW = ("zl", "core")
MEMBERS = ("y2", "zh")
RIGHT_GROUP = ("yk", "zl", "core")


def mm(a, b, ca=1, cb=0):
    return lax.dot_general(
        a, b, (((ca,), (cb,)), ((), ())), precision=highest, preferred_element_type=jnp.float32
    )


def eliminate(rows, off):
    row_id = lax.broadcasted_iota(jnp.int32, (8, 128), 0)
    for g in range(8):
        count = 8 - g
        cols = [
            [
                jnp.broadcast_to(rows[g + h][:, off + 8 * g + t : off + 8 * g + t + 1], (8, 128))
                for h in range(count)
            ]
            for t in range(8)
        ]
        pivots = jnp.ones((8, 128), jnp.float32)
        for t in range(8):
            pivot = jnp.broadcast_to(cols[t][0][t : t + 1, :], (8, 128))
            inv = 1.0 / pivot
            pivots = jnp.where(row_id == t, pivot, pivots)
            f = [c * inv for c in cols[t]]
            f[0] = jnp.where(row_id > t, f[0], 0.0)
            for u in range(t + 1, 8):
                lead = jnp.broadcast_to(cols[u][0][t : t + 1, :], (8, 128))
                cols[u] = [c - fh * lead for c, fh in zip(cols[u], f)]
            lead = jnp.broadcast_to(rows[g][t : t + 1, :], (8, 128))
            for h in range(count):
                rows[g + h] = rows[g + h] - f[h] * lead
            yield
        scale = lax.rsqrt(pivots)
        scale = scale * (1.5 - 0.5 * pivots * scale * scale)
        rows[g] = rows[g] * scale


def load_block(s_ref, at):
    base = (at // 128) * 128
    off = at - base
    other = 64 - off
    width = min(128, s_ref.shape[1] - base)
    lane = lax.broadcasted_iota(jnp.int32, (8, 128), 1)
    row = lax.broadcasted_iota(jnp.int32, (8, 128), 0)
    rows = []
    for g in range(8):
        piece = s_ref[at + 8 * g : at + 8 * g + 8, base : base + width]
        if width < 128:
            piece = jnp.concatenate([piece, jnp.zeros((8, 128 - width), jnp.float32)], axis=1)
        eye = (lane == row + (8 * g + other)).astype(jnp.float32)
        rows.append(jnp.where((lane >= off) & (lane < off + 64), piece, eye))
    return rows, off, other


def apply_block(rows, other, s_ref, pt_ref, qt_ref, at):
    n = s_ref.shape[0]
    inv = jnp.concatenate(rows, axis=0)
    if other:
        inv = pltpu.roll(inv, 64, axis=1)
    inv = inv[:, :64]
    wp = mm(inv, pt_ref[at : at + 64, :])
    qt_ref[at : at + 64, :] = wp
    if at + 64 < n:
        start = ((at + 64) // 128) * 128
        ws = mm(inv, s_ref[at : at + 64, start:])
        s_ref[start:, start:] = s_ref[start:, start:] - mm(ws, ws, 0, 0)
        pt_ref[start:, :] = pt_ref[start:, :] - mm(ws, wp, 0, 0)


def factorize(jobs):
    for gram, basis, s_ref, p_ref, _ in jobs:
        pt = mm(basis, gram, 0, 0)
        p_ref[...] = pt
        s_ref[...] = mm(pt, pt, 1, 1)
    for step in range(LB // NB):
        at = step * NB
        blocks = []
        for _, _, s_ref, p_ref, qt_ref in jobs:
            if at < s_ref.shape[0]:
                rows, off, other = load_block(s_ref, at)
                blocks.append((rows, other, s_ref, p_ref, qt_ref, eliminate(rows, off)))
        live = [b[5] for b in blocks]
        while live:
            live = [g for g in live if next(g, 1) is None]
        for rows, other, s_ref, p_ref, qt_ref, _ in blocks:
            apply_block(rows, other, s_ref, p_ref, qt_ref, at)


def refresh_kernel(
    member_ref, left_raw_ref, gl_ref, bl_ref, right_raw_ref, gr_ref, br_ref, tile_ref, moments_ref,
    gr_out_ref, qr_out_ref, m_ref, v_ref, u_ref, factor_ref,
    sl_ref, pl_ref, qlt_ref, sr_ref, pr_ref, qrt_ref, ms_ref, vs_ref,
):
    packed = right_raw_ref[...]
    row = lax.broadcasted_iota(jnp.int32, (RB, RB), 0)
    col = lax.broadcasted_iota(jnp.int32, (RB, RB), 1)
    slot = (row % 16 == 0) & (col == row + 1)
    total = jnp.sum(jnp.where(slot, packed, 0.0), keepdims=True)
    right_raw = jnp.where(slot, packed.T, packed)
    factor = clip_ratio * math.sqrt(D * KV) / (jnp.sqrt(total) + 1e-06)
    factor_ref[...] = jnp.broadcast_to(factor, factor_ref.shape)
    weight = (1.0 - beta_gram) * factor * factor
    right_new = beta_gram * gr_ref[...] + weight * right_raw
    gr_out_ref[...] = right_new
    left_new = beta_gram * gl_ref[...] + weight * left_raw_ref[...]
    factorize(
        [
            (left_new, bl_ref[...], sl_ref, pl_ref, qlt_ref),
            (right_new, br_ref[...], sr_ref, pr_ref, qrt_ref),
        ]
    )
    qrt = qrt_ref[...]
    qr_out_ref[...] = qrt.T
    rotated = mm(mm(qlt_ref[...], tile_ref[...]) * factor, qrt, 1, 1)
    moment = beta_first * moments_ref[:, :40, :].reshape(LB, RB) + (1.0 - beta_first) * rotated
    second = beta_second * moments_ref[:, 40:, :].reshape(LB, RB)
    second = second + (1.0 - beta_second) * rotated * rotated
    ms_ref[...] = moment
    vs_ref[...] = second
    direction = moment / first_bias / (jnp.sqrt(second / second_bias) + 1e-08)
    u_ref[...] = mm(qlt_ref[...], mm(direction, qrt), 0, 0)
    own = pl.ds(pl.multiple_of(member_ref[0] * 40, 8), 40)
    m_ref[...] = ms_ref[own, :]
    v_ref[...] = vs_ref[own, :]


def shape_of(*dims):
    return jax.ShapeDtypeStruct(dims, jnp.float32)


def whole():
    return pl.BlockSpec(memory_space=pltpu.VMEM)


def refresh(member, left_raw, gl, bl, right_raw, gr, br, tile, moments):
    f32 = jnp.float32
    return pl.pallas_call(
        refresh_kernel,
        out_shape=(
            shape_of(RB, RB), shape_of(RB, RB), shape_of(40, RB), shape_of(40, RB),
            shape_of(LB, RB), shape_of(8, 128),
        ),
        in_specs=[pl.BlockSpec(memory_space=pltpu.SMEM)] + [whole()] * 8,
        out_specs=(whole(),) * 6,
        scratch_shapes=[pltpu.VMEM((LB, LB), f32)] * 3
        + [pltpu.VMEM((RB, RB), f32)] * 3
        + [pltpu.VMEM((LB, RB), f32)] * 2,
        compiler_params=pltpu.CompilerParams(vmem_limit_bytes=24 * 2**20),
        cost_estimate=pl.CostEstimate(
            flops=25_000_000_000, bytes_accessed=4_000_000, transcendentals=0
        ),
        name="refresh",
    )(member, left_raw, gl, bl, right_raw, gr, br, tile, moments)


def held_kernel(factor_ref, raw_ref, g_ref, b_ref, g_out_ref, q_out_ref, s_ref, p_ref, qt_ref):
    factor = factor_ref[:1, :1]
    gram = beta_gram * g_ref[...] + (1.0 - beta_gram) * factor * factor * raw_ref[...]
    g_out_ref[...] = gram
    factorize([(gram, b_ref[...], s_ref, p_ref, qt_ref)])
    q_out_ref[...] = qt_ref[...].T


def refresh_held(factor, raw, gram, basis):
    f32 = jnp.float32
    return pl.pallas_call(
        held_kernel,
        out_shape=(shape_of(LB, LB), shape_of(LB, LB)),
        in_specs=[whole()] * 4,
        out_specs=(whole(),) * 2,
        scratch_shapes=[pltpu.VMEM((LB, LB), f32)] * 3,
        compiler_params=pltpu.CompilerParams(vmem_limit_bytes=24 * 2**20),
        cost_estimate=pl.CostEstimate(
            flops=18_000_000_000, bytes_accessed=2_000_000, transcendentals=0
        ),
        name="refresh_held",
    )(factor, raw, gram, basis)


PLACES = ((0, 0, 320), (-1, 0, 320), (1, 0, 320), (2, 0, 160), (2, 160, 160))


def place_kernel(k_ref, *refs):
    parts, out_ref, rounded_ref, sems = refs[:-3], refs[-3], refs[-2], refs[-1]
    copies = []
    for n, (shift, first, count) in enumerate(PLACES):
        source = lax.rem(k_ref[0] + shift + 4, 4)
        at = pl.ds(pl.multiple_of(source * LB + first, 16), count)
        rounded_ref[at, :] = parts[n][...].astype(jnp.bfloat16)
        copies.append(pltpu.make_async_copy(rounded_ref.at[at], out_ref.at[at], sems.at[n]))
        copies[-1].start()
    for copy in copies:
        copy.wait()


def place(k, parts):
    return pl.pallas_call(
        place_kernel,
        out_shape=jax.ShapeDtypeStruct((4 * LB, RB), jnp.bfloat16),
        in_specs=[pl.BlockSpec(memory_space=pltpu.SMEM)] + [whole()] * len(parts),
        out_specs=pl.BlockSpec(memory_space=pl.ANY),
        scratch_shapes=[
            pltpu.VMEM((4 * LB, RB), jnp.bfloat16),
            pltpu.SemaphoreType.DMA((len(PLACES),)),
        ],
        compiler_params=pltpu.CompilerParams(vmem_limit_bytes=16 * 2**20),
        name="place",
    )(k, *parts)


def gather_all(x, axes, count):
    copies = jnp.broadcast_to(x[None], (count,) + x.shape)
    return lax.all_to_all(copies, axes, 0, 0, tiled=True)


def shift_perm(size, by):
    return [(s, (s + by) % size) for s in range(size)]


def shards(
    pseudo_grads, left_gram, right_gram, left_basis, right_basis, first_moment, second_moment
):
    k = lax.axis_index("yk")
    x = lax.axis_index("x")
    member = lax.axis_index(MEMBERS)

    moments = lax.all_gather(
        jnp.concatenate([first_moment, second_moment], axis=0), MEMBERS, axis=0, tiled=False
    )

    held = jnp.concatenate([left_gram, left_basis], axis=0)
    moved = jnp.where(x == k, held, 0.0)
    for by in range(1, 4):
        moved = moved + lax.ppermute(
            held, ("yk", "x"), [(b * 4 + b, b * 4 + (b + by) % 4) for b in range(4)]
        )

    pieces = pseudo_grads[0].astype(jnp.float32).reshape(32, 40, RB)
    arrived = lax.all_to_all(pieces, REP, 0, 0, tiled=True)
    own = jnp.sum(arrived, axis=0) * (1.0 / 32.0)

    tile = gather_all(own, MEMBERS, 8).reshape(LB, RB)
    right_part = mm(tile, tile, 0, 0).reshape(16, 16, RB)
    right_own = jnp.sum(lax.all_to_all(right_part, RIGHT_GROUP, 0, 0, tiled=True), axis=0)
    tiles = [tile] + [lax.ppermute(tile, "x", shift_perm(4, by)) for by in range(1, 4)]
    squares = sum(jnp.sum(t * t) for t in tiles)

    group = lax.axis_index(RIGHT_GROUP)
    row = lax.broadcasted_iota(jnp.int32, (16, RB), 0)
    col = lax.broadcasted_iota(jnp.int32, (16, RB), 1)
    packed = jnp.where((row == 0) & (col == 16 * group + 1), squares, right_own)
    right_raw = gather_all(packed, RIGHT_GROUP, 16).reshape(RB, RB)

    left_raw = mm(tiles[0], tiles[0], 1, 1)
    for t in tiles[1:]:
        left_raw = left_raw + mm(t, t, 1, 1)
    swap = [(a * 4 + b, b * 4 + a) for a in range(4) for b in range(4)]
    held_raw = lax.ppermute(left_raw, ("yk", "x"), swap)

    right_new, right_basis_new, moment, second, turned, factor = refresh(
        member.astype(jnp.int32).reshape(1), left_raw, moved[0], moved[1], right_raw,
        right_gram[0], right_basis[0], tile, moments,
    )

    before = lax.ppermute(turned, "yk", shift_perm(4, 1))
    after = lax.ppermute(turned, "yk", shift_perm(4, -1))
    left_new, left_basis_new = refresh_held(factor, held_raw, left_gram[0], left_basis[0])
    before, after, left_new, left_basis_new = lax.optimization_barrier(
        (before, after, left_new, left_basis_new)
    )
    upper = lax.ppermute(before[:160], "yk", shift_perm(4, 1))
    lower = lax.ppermute(after[160:], "yk", shift_perm(4, -1))
    update = place(k.astype(jnp.int32).reshape(1), [turned, before, after, upper, lower])
    return (
        update, left_new[None], left_basis_new[None], right_new[None], right_basis_new[None],
        moment, second,
    )


def solution(mesh):
    fine = Mesh(
        mesh.devices.reshape(4, 2, 4, 2, 2, 4), ("yk", "y2", "zh", "zl", "core", "x")
    )
    left = P(ROW + ("x",), None, None)
    right = P("x", None, None)
    moments = P(ROW + REP, "x")
    return jax.shard_map(
        shards,
        mesh=fine,
        in_specs=(P(REP, ROW, "x"), left, right, left, right, moments, moments),
        out_specs=(P(ROW, "x"), left, left, right, right, moments, moments),
        check_vma=False,
    )
```

time: 269 us -> 218 us (0.81)
  waiting for transfers between devices: 117 us -> 21 us
  blocking collectives: 0 us -> 56 us
  starting transfers between devices: 101 us -> 68.4 us
  Pallas kernels: 21.1 us -> 41.5 us
    all_gather x0 -> x1, blocking collectives: none -> 56 us  [shards(): lax.all_gather(jnp.concatenate([first_moment, second_moment], axis=0), ME...]
    ppermute x13 -> x5, waiting for transfers between devices: 55 us -> 11.5 us  [the longest x1 5.29 us: shards(): upper = lax.ppermute(before[:160], 'yk', shift_perm(4, 1))]
    all_to_all x1, waiting for transfers between devices: 30 us -> 0.01 us  [shards(): arrived = lax.all_to_all(pieces, REP, 0, 0, tiled=True)]
    ppermute x13 -> x5, starting transfers between devices: 46 us -> 19.7 us  [the longest x1 5.77 us: shards(): held_raw = lax.ppermute(left_raw, ('yk', 'x'), swap)]
    all_to_all x3 -> x2, waiting for transfers between devices: 31.4 us -> 8.81 us  [gather_all(): return lax.all_to_all(copies, axes, 0, 0, tiled=True)]
    pallas_call x2 -> x3, Pallas kernels: 21.1 us -> 41.5 us  [the longest x1 24.2 us: refresh(): pl.pallas_call(refresh_kernel, out_shape=(shape_of(RB, RB), shape_of(RB,...]
    all_to_all x3 -> x2, starting transfers between devices: 19.6 us -> 11.1 us  [gather_all(): return lax.all_to_all(copies, axes, 0, 0, tiled=True)]
    dot_general x6 -> x5, matrix products: 7.84 us -> 9.78 us  [mm(): lax.dot_general(a, b, (((ca,), (cb,)), ((), ())), precision=highest, pref...]
  transfers between devices with their start and end apart: 24 -> 15, of which waited for: 8 -> 6; matrix products, arithmetic and copies ran while one was open for 6% -> 9% of each run, Pallas kernels for 0% -> 19%
where the time goes in v2:
time: 218 us; the launch traced here: 216 us
  starting transfers between devices  68.4 us (31%)
  blocking collectives  56 us (26%)
  Pallas kernels  41.5 us (19%)
  waiting for transfers between devices  21 us (10%)
  matrix products  9.78 us (4%)
  other arithmetic  9.15 us (4%)
  local copies, waits for them, and re-layouts  6.03 us (3%)
  between operations  3.69 us (2%)
    all_gather x1, blocking collectives, shards(): lax.all_gather(jnp.concatenate([first_moment, second_moment], axis=0), ME...  56 us
    pallas_call x1, Pallas kernels, refresh(): pl.pallas_call(refresh_kernel, out_shape=(shape_of(RB, RB), shape_of(RB,...  24.2 us
    pallas_call x1, Pallas kernels, refresh_held(): pl.pallas_call(held_kernel, out_shape=(shape_of(LB, LB), shape_of(LB, LB)...  16.5 us
    all_to_all x1, starting transfers between devices, shards(): arrived = lax.all_to_all(pieces, REP, 0, 0, tiled=True)  16.1 us
    all_to_all x2, starting transfers between devices, gather_all(): return lax.all_to_all(copies, axes, 0, 0, tiled=True)  11.1 us
    ppermute x3, starting transfers between devices, shards(): lax.ppermute(tile, 'x', shift_perm(4, by))  9.84 us
    dot_general x5, matrix products, mm(): lax.dot_general(a, b, (((ca,), (cb,)), ((), ())), precision=highest, pref...  9.78 us
    all_to_all x2, waiting for transfers between devices, gather_all(): return lax.all_to_all(copies, axes, 0, 0, tiled=True)  8.81 us
  transfers between devices with their start and end apart: 15, of which 6 were waited for; matrix products, arithmetic and copies ran while one was open for 9% of the time, Pallas kernels for 19%

profile of v2, /device:TPU:6, one launch (start us, length us, event | category | flops | bytes accessed | tf_op | source)
XLA Modules:
  0.0 215.6 jit_solution(11386916009472179674)
XLA Ops:
  0.6 2.3 %convert.1 = f32[32,40,256]{2,1,0:T(8,128)} convert(bf16[32,40,256]{2,1,0:T(8,128)(2,1)} %bitcast.47) | non-fusion elementwise | flops 327680 | bytes 1966080 | tf_op jit(solution)/shard_map/convert_element_type | solution.py:266
  2.9 16.1 %all-to-all-start = ((f32[32,40,256]{2,1,0:T(8,128)}), f32[32,40,256]{2,1,0:T(8,128)S(1)}, u32[]{:S(2)}, u32[]{:S(2)}) async-start(f32[32,40,256]{2,1,0:T(8,128)} %convert.1), calls=%async_computation | async-start | bytes 2621440 | tf_op jit(solution)/shard_map/all_to_all | solution.py:267
  19.0 0.0 copy-start.6
  19.0 0.8 constant_dynamic-update-slice_fusion.1
  19.9 0.8 constant_dynamic-update-slice_fusion
  20.7 1.3 collective-permute-start.5
  22.0 1.6 collective-permute-start.4
  23.6 1.6 collective-permute-start.3
  25.3 56.0 %all-gather = f32[640,256]{1,0:T(8,128)S(1)} all-gather(f32[80,256]{1,0:T(8,128)S(1)} %pad_maximum_fusion), channel_id=2, replica_groups=mesh['yk'=4,'y2'=2,'zh'=4,'zl'=2,'core'=2,'x'=4] {'y2','zh'}, dimensions={0}, use_global_device_ids=true | all-gather | bytes 737280 | tf_op jit(solution)/shard_map/all_gather | solution.py:255
  81.3 0.1 reduce_sum.54
  81.4 0.7 broadcast_in_dim.32
  82.1 3.6 %all-to-all-start.1 = ((f32[8,40,256]{2,1,0:T(8,128)}), f32[8,40,256]{2,1,0:T(8,128)S(1)}, u32[]{:S(2)}, u32[]{:S(2)}) async-start(f32[8,40,256]{2,1,0:T(8,128)} %broadcast_in_dim.32), calls=%async_computation.1 | async-start | bytes 655360 | tf_op jit(solution)/shard_map/all_to_all | solution.py:241
  85.8 2.0 add_add_fusion
  87.8 0.1 slice_bitcast_fusion
  87.8 7.7 %all-to-all-done.1 = f32[8,40,256]{2,1,0:T(8,128)S(1)} async-done(((f32[8,40,256]{2,1,0:T(8,128)}), f32[8,40,256]{2,1,0:T(8,128)S(1)}, u32[]{:S(2)}, u32[]{:S(2)}) %all-to-all-start.1) | async-done | bytes 327712 | tf_op jit(solution)/shard_map/all_to_all | solution.py:241
  95.5 2.6 %collective-permute-start.2 = (f32[320,256]{1,0:T(8,128)S(1)}, f32[320,256]{1,0:T(8,128)}, u32[]{:S(2)}, u32[]{:S(2)}) collective-permute-start(f32[320,256]{1,0:T(8,128)S(1)} %bitcast.34), channel_id=1, source_target_pairs={{0,3},{1,0},{2,1},{3,2},{4,7},{5,4},{6,5},{7,6},{8,11},{9,8},{10,9... | collective-permute-start | bytes 983048 | tf_op jit(solution)/shard_map/ppermute | solution.py:273
  98.1 3.0 %collective-permute-start.1 = (f32[320,256]{1,0:T(8,128)S(1)}, f32[320,256]{1,0:T(8,128)}, u32[]{:S(2)}, u32[]{:S(2)}) collective-permute-start(f32[320,256]{1,0:T(8,128)S(1)} %bitcast.35), channel_id=1, source_target_pairs={{0,2},{1,3},{2,0},{3,1},{4,6},{5,7},{6,4},{7,5},{8,10},{9,11},{10,... | collective-permute-start | bytes 983048 | tf_op jit(solution)/shard_map/ppermute | solution.py:273
  101.1 4.2 %collective-permute-start = (f32[320,256]{1,0:T(8,128)S(1)}, f32[320,256]{1,0:T(8,128)S(1)}, u32[]{:S(2)}, u32[]{:S(2)}) collective-permute-start(f32[320,256]{1,0:T(8,128)S(1)} %bitcast.36), channel_id=1, source_target_pairs={{0,1},{1,2},{2,3},{3,0},{4,5},{5,6},{6,7},{7,4},{8,9},{9,10},{10,1... | collective-permute-start | bytes 983048 | tf_op jit(solution)/shard_map/ppermute | solution.py:273
  105.4 1.5 fusion.1
  106.8 0.9 copy.15
  107.7 2.3 %fusion.3 = f32[16,16,256]{2,1,0:T(8,128)} fusion(f32[16,16,320]{2,1,0:T(8,128)} %bitcast.46, f32[320,256,1]{1,0,2:T(8,128)S(1)} %bitcast.39), kind=kOutput, calls=%fused_computation.19 | convolution fusion | flops 251658240 | bytes 917504 | tf_op jit(solution)/shard_map/dot_general | solution.py:31
  110.0 7.1 %all-to-all-start.2 = ((f32[16,16,256]{2,1,0:T(8,128)}), f32[16,16,256]{2,1,0:T(8,128)S(1)}, u32[]{:S(2)}, u32[]{:S(2)}) async-start(f32[16,16,256]{2,1,0:T(8,128)} %fusion.3), calls=%async_computation.2 | async-start | bytes 524288 | tf_op jit(solution)/shard_map/all_to_all | solution.py:272
  117.1 0.7 multiply_reduce_fusion.3
  117.8 0.7 multiply_reduce_fusion.2
  119.8 1.7 multiply_reduce_fusion.1
  122.1 1.7 multiply_reduce_fusion
  124.4 2.5 %convolution_add_fusion.1 = f32[320,320]{1,0:T(8,128)} fusion(f32[320,320]{1,0:T(8,128)} %fusion.1, f32[320,256]{1,0:T(8,128)S(1)} %collective-permute-done), kind=kOutput, calls=%fused_computation.2 | convolution fusion | flops 314675200 | bytes 1146880 | tf_op jit(solution)/shard_map/dot_general | solution.py:31
  126.9 0.7 all-to-all-done.2
  127.6 0.1 and_select_fusion
  127.7 0.7 broadcast_in_dim.35
  128.4 7.5 %all-to-all-start.3 = ((f32[16,16,256]{2,1,0:T(8,128)}), f32[16,16,256]{2,1,0:T(8,128)}, u32[]{:S(2)}, u32[]{:S(2)}) async-start(f32[16,16,256]{2,1,0:T(8,128)} %broadcast_in_dim.35), calls=%async_computation.3 | async-start | bytes 524288 | tf_op jit(solution)/shard_map/all_to_all | solution.py:241
  135.9 0.0 copy-start.4
  135.9 1.8 fusion.2
  137.7 1.8 fusion.left_raw_ref
  139.5 5.8 %collective-permute-start.8 = (f32[320,320]{1,0:T(8,128)S(1)}, f32[320,320]{1,0:T(8,128)}, u32[]{:S(2)}, u32[]{:S(2)}) collective-permute-start(f32[320,320]{1,0:T(8,128)S(1)} %fusion.left_raw_ref), channel_id=1, source_target_pairs={{0,0},{1,128},{2,256},{3,384},{128,1},{129,129},{130,257},{131,385... | collective-permute-start | bytes 1228808 | tf_op jit(solution)/shard_map/ppermute | solution.py:286
  145.3 1.1 all-to-all-done.3
  146.4 0.9 copy-done.2
  147.4 0.9 copy-done.3
  148.3 24.2 %refresh.1 = (f32[256,256]{1,0:T(8,128)}, f32[256,256]{1,0:T(8,128)}, f32[40,256]{1,0:T(8,128)}, f32[40,256]{1,0:T(8,128)}, f32[320,256]{1,0:T(8,128)S(1)}, /*index=5*/f32[8,128]{1,0:T(8,128)S(1)}) custom-call(s32[1]{0:T(128)} %bitcast.1.member_ref, f32[320,320]{1,0:T(8,128)S(1)} %fusion.left_raw_ref, f32[320,320]{1,0:T(8,128)S(1)} %get-tuple-element.32.gl_ref, ...), custom_call_target="tpu_custom_call" | custom-call | flops 24999999488 | bytes 4000000 | tf_op jit(solution)/shard_map/refresh/pallas_call | solution.py:165
  172.5 5.2 %collective-permute-start.7 = (f32[320,256]{1,0:T(8,128)S(1)}, f32[320,256]{1,0:T(8,128)S(1)}, u32[]{:S(2)}, u32[]{:S(2)}) collective-permute-start(f32[320,256]{1,0:T(8,128)S(1)} %get-tuple-element.19.refs_0_), channel_id=1, source_target_pairs={{0,384},{128,0},{256,128},{384,256},{1,385},{129,1},{257,129},{385... | collective-permute-start | bytes 983048 | tf_op jit(solution)/shard_map/ppermute | solution.py:294
  177.7 1.9 collective-permute-start.6
  179.6 16.5 %refresh_held.1 = (f32[320,320]{1,0:T(8,128)}, f32[320,320]{1,0:T(8,128)}) custom-call(f32[8,128]{1,0:T(8,128)S(1)} %get-tuple-element.20.factor_ref, f32[320,320]{1,0:T(8,128)} %collective-permute-done.8.raw_ref, f32[320,320]{1,0:T(8,128)S(1)} %bitcast.42, f32[320,320]{1,0:T(8,128)S(1)} %bitcast.43), custom_call_target="tpu_custom_call" | custom-call | flops 17999998976 | bytes 2000000 | tf_op jit(solution)/shard_map/refresh_held/pallas_call | solution.py:194
  196.1 1.1 collective-permute-done.6.refs_1_
  197.2 4.9 %collective-permute-start.10 = (f32[160,256]{1,0:T(8,128)S(1)}, f32[160,256]{1,0:T(8,128)S(1)}, u32[]{:S(2)}, u32[]{:S(2)}) collective-permute-start(f32[160,256]{1,0:T(8,128)S(1)} %slice.15), channel_id=1, source_target_pairs={{0,384},{128,0},{256,128},{384,256},{1,385},{129,1},{257,129},{385... | collective-permute-start | bytes 491528 | tf_op jit(solution)/shard_map/ppermute | solution.py:300
  202.2 1.9 collective-permute-start.9
  204.1 5.1 %collective-permute-done.10.refs_4_ = f32[160,256]{1,0:T(8,128)S(1)} collective-permute-done((f32[160,256]{1,0:T(8,128)S(1)}, f32[160,256]{1,0:T(8,128)S(1)}, u32[]{:S(2)}, u32[]{:S(2)}) %collective-permute-start.10) | collective-permute-done | bytes 163872 | tf_op jit(solution)/shard_map/ppermute | solution.py:300
  209.2 5.3 %collective-permute-done.9.refs_3_ = f32[160,256]{1,0:T(8,128)S(1)} collective-permute-done((f32[160,256]{1,0:T(8,128)S(1)}, f32[160,256]{1,0:T(8,128)S(1)}, u32[]{:S(2)}, u32[]{:S(2)}) %collective-permute-start.9) | collective-permute-done | bytes 163872 | tf_op jit(solution)/shard_map/ppermute | solution.py:299
  214.5 0.9 place.1
  (26 shorter events, 0.1 us)
Async XLA Ops:
  2.9 16.1 %copy-start = (f32[1,320,320]{2,1,0:T(8,128)S(1)}, f32[1,320,320]{2,1,0:T(8,128)}, u32[]{:S(2)}) copy-start(f32[1,320,320]{2,1,0:T(8,128)} %param.8) | copy-start | bytes 1228804
  2.9 16.9 %copy-start.1 = (f32[1,320,320]{2,1,0:T(8,128)S(1)}, f32[1,320,320]{2,1,0:T(8,128)}, u32[]{:S(2)}) copy-start(f32[1,320,320]{2,1,0:T(8,128)} %param.10) | copy-start | bytes 1228804
  2.9 78.3 %all-to-all-start = ((f32[32,40,256]{2,1,0:T(8,128)}), f32[32,40,256]{2,1,0:T(8,128)S(1)}, u32[]{:S(2)}, u32[]{:S(2)}) async-start(f32[32,40,256]{2,1,0:T(8,128)} %convert.1), calls=%async_computation | async-start | bytes 2621440 | tf_op jit(solution)/shard_map/all_to_all | solution.py:267
  19.0 6.2 %copy-start.5 = (f32[40,256]{1,0:T(8,128)S(1)}, f32[40,256]{1,0:T(8,128)}, u32[]{:S(2)}) copy-start(f32[40,256]{1,0:T(8,128)} %param.13) | copy-start | bytes 122884
  19.0 6.2 %copy-start.6 = (f32[40,256]{1,0:T(8,128)S(1)}, f32[40,256]{1,0:T(8,128)}, u32[]{:S(2)}) copy-start(f32[40,256]{1,0:T(8,128)} %param.12) | copy-start | bytes 122884
  20.7 65.1 %collective-permute-start.5 = (f32[2,320,320]{2,1,0:T(8,128)}, f32[2,320,320]{2,1,0:T(8,128)}, u32[]{:S(2)}, u32[]{:S(2)}) collective-permute-start(f32[2,320,320]{2,1,0:T(8,128)} %constant_dynamic-update-slice_fusion), channel_id=1, source_target_pairs={{0,3},{129,128},{258,257},{387,386},{4,7},{133,132},{262,261},{391... | collective-permute-start | bytes 2457608 | tf_op jit(solution)/shard_map/ppermute | solution.py:262
  22.0 63.8 %collective-permute-start.4 = (f32[2,320,320]{2,1,0:T(8,128)}, f32[2,320,320]{2,1,0:T(8,128)}, u32[]{:S(2)}, u32[]{:S(2)}) collective-permute-start(f32[2,320,320]{2,1,0:T(8,128)} %constant_dynamic-update-slice_fusion), channel_id=1, source_target_pairs={{0,2},{129,131},{258,256},{387,385},{4,6},{133,135},{262,260},{391... | collective-permute-start | bytes 2457608 | tf_op jit(solution)/shard_map/ppermute | solution.py:262
  23.6 62.2 %collective-permute-start.3 = (f32[2,320,320]{2,1,0:T(8,128)}, f32[2,320,320]{2,1,0:T(8,128)}, u32[]{:S(2)}, u32[]{:S(2)}) collective-permute-start(f32[2,320,320]{2,1,0:T(8,128)} %constant_dynamic-update-slice_fusion), channel_id=1, source_target_pairs={{0,1},{129,130},{258,259},{387,384},{4,5},{133,134},{262,263},{391... | collective-permute-start | bytes 2457608 | tf_op jit(solution)/shard_map/ppermute | solution.py:262
  82.1 13.4 %all-to-all-start.1 = ((f32[8,40,256]{2,1,0:T(8,128)}), f32[8,40,256]{2,1,0:T(8,128)S(1)}, u32[]{:S(2)}, u32[]{:S(2)}) async-start(f32[8,40,256]{2,1,0:T(8,128)} %broadcast_in_dim.32), calls=%async_computation.1 | async-start | bytes 655360 | tf_op jit(solution)/shard_map/all_to_all | solution.py:241
  95.5 26.6 %collective-permute-start.2 = (f32[320,256]{1,0:T(8,128)S(1)}, f32[320,256]{1,0:T(8,128)}, u32[]{:S(2)}, u32[]{:S(2)}) collective-permute-start(f32[320,256]{1,0:T(8,128)S(1)} %bitcast.34), channel_id=1, source_target_pairs={{0,3},{1,0},{2,1},{3,2},{4,7},{5,4},{6,5},{7,6},{8,11},{9,8},{10,9... | collective-permute-start | bytes 983048 | tf_op jit(solution)/shard_map/ppermute | solution.py:273
  98.1 21.7 %collective-permute-start.1 = (f32[320,256]{1,0:T(8,128)S(1)}, f32[320,256]{1,0:T(8,128)}, u32[]{:S(2)}, u32[]{:S(2)}) collective-permute-start(f32[320,256]{1,0:T(8,128)S(1)} %bitcast.35), channel_id=1, source_target_pairs={{0,2},{1,3},{2,0},{3,1},{4,6},{5,7},{6,4},{7,5},{8,10},{9,11},{10,... | collective-permute-start | bytes 983048 | tf_op jit(solution)/shard_map/ppermute | solution.py:273
  101.1 16.6 %collective-permute-start = (f32[320,256]{1,0:T(8,128)S(1)}, f32[320,256]{1,0:T(8,128)S(1)}, u32[]{:S(2)}, u32[]{:S(2)}) collective-permute-start(f32[320,256]{1,0:T(8,128)S(1)} %bitcast.36), channel_id=1, source_target_pairs={{0,1},{1,2},{2,3},{3,0},{4,5},{5,6},{6,7},{7,4},{8,9},{9,10},{10,1... | collective-permute-start | bytes 983048 | tf_op jit(solution)/shard_map/ppermute | solution.py:273
  110.0 17.6 %all-to-all-start.2 = ((f32[16,16,256]{2,1,0:T(8,128)}), f32[16,16,256]{2,1,0:T(8,128)S(1)}, u32[]{:S(2)}, u32[]{:S(2)}) async-start(f32[16,16,256]{2,1,0:T(8,128)} %fusion.3), calls=%async_computation.2 | async-start | bytes 524288 | tf_op jit(solution)/shard_map/all_to_all | solution.py:272
  128.4 18.0 %all-to-all-start.3 = ((f32[16,16,256]{2,1,0:T(8,128)}), f32[16,16,256]{2,1,0:T(8,128)}, u32[]{:S(2)}, u32[]{:S(2)}) async-start(f32[16,16,256]{2,1,0:T(8,128)} %broadcast_in_dim.35), calls=%async_computation.3 | async-start | bytes 524288 | tf_op jit(solution)/shard_map/all_to_all | solution.py:241
  135.9 1.8 copy-start.4
  139.5 40.1 %collective-permute-start.8 = (f32[320,320]{1,0:T(8,128)S(1)}, f32[320,320]{1,0:T(8,128)}, u32[]{:S(2)}, u32[]{:S(2)}) collective-permute-start(f32[320,320]{1,0:T(8,128)S(1)} %fusion.left_raw_ref), channel_id=1, source_target_pairs={{0,0},{1,128},{2,256},{3,384},{128,1},{129,129},{130,257},{131,385... | collective-permute-start | bytes 1228808 | tf_op jit(solution)/shard_map/ppermute | solution.py:286
  146.4 1.0 copy-start.2
  147.4 0.9 copy-start.3
  172.5 23.6 %collective-permute-start.7 = (f32[320,256]{1,0:T(8,128)S(1)}, f32[320,256]{1,0:T(8,128)S(1)}, u32[]{:S(2)}, u32[]{:S(2)}) collective-permute-start(f32[320,256]{1,0:T(8,128)S(1)} %get-tuple-element.19.refs_0_), channel_id=1, source_target_pairs={{0,384},{128,0},{256,128},{384,256},{1,385},{129,1},{257,129},{385... | collective-permute-start | bytes 983048 | tf_op jit(solution)/shard_map/ppermute | solution.py:294
  177.7 19.5 %collective-permute-start.6 = (f32[320,256]{1,0:T(8,128)S(1)}, f32[320,256]{1,0:T(8,128)S(1)}, u32[]{:S(2)}, u32[]{:S(2)}) collective-permute-start(f32[320,256]{1,0:T(8,128)S(1)} %get-tuple-element.19.refs_0_), channel_id=1, source_target_pairs={{0,128},{128,256},{256,384},{384,0},{1,129},{129,257},{257,385},{3... | collective-permute-start | bytes 983048 | tf_op jit(solution)/shard_map/ppermute | solution.py:293
  197.2 12.0 %collective-permute-start.10 = (f32[160,256]{1,0:T(8,128)S(1)}, f32[160,256]{1,0:T(8,128)S(1)}, u32[]{:S(2)}, u32[]{:S(2)}) collective-permute-start(f32[160,256]{1,0:T(8,128)S(1)} %slice.15), channel_id=1, source_target_pairs={{0,384},{128,0},{256,128},{384,256},{1,385},{129,1},{257,129},{385... | collective-permute-start | bytes 491528 | tf_op jit(solution)/shard_map/ppermute | solution.py:300
  202.2 12.3 %collective-permute-start.9 = (f32[160,256]{1,0:T(8,128)S(1)}, f32[160,256]{1,0:T(8,128)S(1)}, u32[]{:S(2)}, u32[]{:S(2)}) collective-permute-start(f32[160,256]{1,0:T(8,128)S(1)} %slice.14), channel_id=1, source_target_pairs={{0,128},{128,256},{256,384},{384,0},{1,129},{129,257},{257,385},{3... | collective-permute-start | bytes 491528 | tf_op jit(solution)/shard_map/ppermute | solution.py:299

commit v3 on v2

--- a/solution.py
+++ b/solution.py
@@ -114,17 +114,28 @@
             apply_block(rows, other, s_ref, p_ref, qt_ref, at)
 
 
+def slots(shape, row_at, col_at):
+    row = lax.broadcasted_iota(jnp.int32, shape, 0)
+    col = lax.broadcasted_iota(jnp.int32, shape, 1)
+    return (row % 16 == row_at) & (col == row + col_at)
+
+
 def refresh_kernel(
-    member_ref, left_raw_ref, gl_ref, bl_ref, right_raw_ref, gr_ref, br_ref, tile_ref, moments_ref,
+    place_ref, left_raw_ref, gl_ref, bl_ref, right_raw_ref, gr_ref, br_ref, tile_ref, squares_ref,
+    mine_ref, other_ref,
     gr_out_ref, qr_out_ref, m_ref, v_ref, u_ref, factor_ref,
     sl_ref, pl_ref, qlt_ref, sr_ref, pr_ref, qrt_ref, ms_ref, vs_ref,
 ):
+    y2, zh = place_ref[0], place_ref[1]
+    for src_ref, pair in ((mine_ref, y2), (other_ref, 1 - y2)):
+        for n, shift in enumerate((0, -1, 1, 2)):
+            at = pl.multiple_of(40 * (4 * pair + lax.rem(zh + shift + 4, 4)), 8)
+            ms_ref[pl.ds(at, 40), :] = src_ref[80 * n : 80 * n + 40, :]
+            vs_ref[pl.ds(at, 40), :] = src_ref[80 * n + 40 : 80 * n + 80, :]
     packed = right_raw_ref[...]
-    row = lax.broadcasted_iota(jnp.int32, (RB, RB), 0)
-    col = lax.broadcasted_iota(jnp.int32, (RB, RB), 1)
-    slot = (row % 16 == 0) & (col == row + 1)
-    total = jnp.sum(jnp.where(slot, packed, 0.0), keepdims=True)
+    slot = slots((RB, RB), 0, 1)
     right_raw = jnp.where(slot, packed.T, packed)
+    total = (squares_ref[0] + squares_ref[1] + squares_ref[2] + squares_ref[3])[:1, :1]
     factor = clip_ratio * math.sqrt(D * KV) / (jnp.sqrt(total) + 1e-06)
     factor_ref[...] = jnp.broadcast_to(factor, factor_ref.shape)
     weight = (1.0 - beta_gram) * factor * factor
@@ -140,14 +151,13 @@
     qrt = qrt_ref[...]
     qr_out_ref[...] = qrt.T
     rotated = mm(mm(qlt_ref[...], tile_ref[...]) * factor, qrt, 1, 1)
-    moment = beta_first * moments_ref[:, :40, :].reshape(LB, RB) + (1.0 - beta_first) * rotated
-    second = beta_second * moments_ref[:, 40:, :].reshape(LB, RB)
-    second = second + (1.0 - beta_second) * rotated * rotated
+    moment = beta_first * ms_ref[...] + (1.0 - beta_first) * rotated
+    second = beta_second * vs_ref[...] + (1.0 - beta_second) * rotated * rotated
     ms_ref[...] = moment
     vs_ref[...] = second
     direction = moment / first_bias / (jnp.sqrt(second / second_bias) + 1e-08)
     u_ref[...] = mm(qlt_ref[...], mm(direction, qrt), 0, 0)
-    own = pl.ds(pl.multiple_of(member_ref[0] * 40, 8), 40)
+    own = pl.ds(pl.multiple_of(40 * (4 * y2 + zh), 8), 40)
     m_ref[...] = ms_ref[own, :]
     v_ref[...] = vs_ref[own, :]
 
@@ -160,7 +170,7 @@
     return pl.BlockSpec(memory_space=pltpu.VMEM)
 
 
-def refresh(member, left_raw, gl, bl, right_raw, gr, br, tile, moments):
+def refresh(spot, left_raw, gl, bl, right_raw, gr, br, tile, squares, mine, other):
     f32 = jnp.float32
     return pl.pallas_call(
         refresh_kernel,
@@ -168,7 +178,7 @@
             shape_of(RB, RB), shape_of(RB, RB), shape_of(40, RB), shape_of(40, RB),
             shape_of(LB, RB), shape_of(8, 128),
         ),
-        in_specs=[pl.BlockSpec(memory_space=pltpu.SMEM)] + [whole()] * 8,
+        in_specs=[pl.BlockSpec(memory_space=pltpu.SMEM)] + [whole()] * 10,
         out_specs=(whole(),) * 6,
         scratch_shapes=[pltpu.VMEM((LB, LB), f32)] * 3
         + [pltpu.VMEM((RB, RB), f32)] * 3
@@ -178,7 +188,7 @@
             flops=25_000_000_000, bytes_accessed=4_000_000, transcendentals=0
         ),
         name="refresh",
-    )(member, left_raw, gl, bl, right_raw, gr, br, tile, moments)
+    )(spot, left_raw, gl, bl, right_raw, gr, br, tile, squares, mine, other)
 
 
 def held_kernel(factor_ref, raw_ref, g_ref, b_ref, g_out_ref, q_out_ref, s_ref, p_ref, qt_ref):
@@ -205,6 +215,53 @@
     )(factor, raw, gram, basis)
 
 
+def own_sum_kernel(arrived_ref, out_ref):
+    total = arrived_ref[0]
+    for r in range(1, 32):
+        total = total + arrived_ref[r]
+    total = total * (1.0 / 32.0)
+    for n in range(8):
+        out_ref[n] = total
+
+
+def right_part_kernel(tile_ref, out_ref):
+    tile = tile_ref[...]
+    squares = jnp.sum(tile * tile, keepdims=True)
+    out_ref[...] = jnp.where(slots((RB, RB), 0, 1), squares, mm(tile, tile, 0, 0))
+
+
+def right_sum_kernel(group_ref, parts_ref, out_ref, squares_ref):
+    total = parts_ref[0]
+    for r in range(1, 16):
+        total = total + parts_ref[r]
+    for n in range(16):
+        out_ref[n] = total
+    slot = slots((16, RB), 0, 16 * group_ref[0] + 1)
+    squares = jnp.sum(jnp.where(slot, total, 0.0), keepdims=True)
+    squares_ref[...] = jnp.broadcast_to(squares, squares_ref.shape)
+
+
+def left_gram_kernel(tiles_ref, out_ref):
+    total = mm(tiles_ref[0], tiles_ref[0], 1, 1)
+    for n in range(1, 4):
+        total = total + mm(tiles_ref[n], tiles_ref[n], 1, 1)
+    out_ref[...] = total
+
+
+def small(kernel, name, out_shape, flops, *operands, scalars=0):
+    specs = [pl.BlockSpec(memory_space=pltpu.SMEM)] * scalars
+    specs = specs + [whole()] * (len(operands) - scalars)
+    return pl.pallas_call(
+        kernel,
+        out_shape=out_shape,
+        in_specs=specs,
+        out_specs=jax.tree.map(lambda _: whole(), out_shape),
+        compiler_params=pltpu.CompilerParams(vmem_limit_bytes=16 * 2**20),
+        cost_estimate=pl.CostEstimate(flops=flops, bytes_accessed=1_000_000, transcendentals=0),
+        name=name,
+    )(*operands)
+
+
 PLACES = ((0, 0, 320), (-1, 0, 320), (1, 0, 320), (2, 0, 160), (2, 160, 160))
 
 
@@ -250,11 +307,14 @@
 ):
     k = lax.axis_index("yk")
     x = lax.axis_index("x")
-    member = lax.axis_index(MEMBERS)
-
-    moments = lax.all_gather(
-        jnp.concatenate([first_moment, second_moment], axis=0), MEMBERS, axis=0, tiled=False
-    )
+
+    ours = jnp.concatenate([first_moment, second_moment], axis=0)
+    prev = lax.ppermute(ours, "zh", shift_perm(4, 1))
+    succ = lax.ppermute(ours, "zh", shift_perm(4, -1))
+    far_first = lax.ppermute(prev[:40], "zh", shift_perm(4, 1))
+    far_second = lax.ppermute(succ[40:], "zh", shift_perm(4, -1))
+    mine = jnp.concatenate([ours, prev, succ, far_first, far_second], axis=0)
+    other = lax.ppermute(mine, "y2", shift_perm(2, 1))
 
     held = jnp.concatenate([left_gram, left_basis], axis=0)
     moved = jnp.where(x == k, held, 0.0)
@@ -265,29 +325,26 @@
 
     pieces = pseudo_grads[0].astype(jnp.float32).reshape(32, 40, RB)
     arrived = lax.all_to_all(pieces, REP, 0, 0, tiled=True)
-    own = jnp.sum(arrived, axis=0) * (1.0 / 32.0)
-
-    tile = gather_all(own, MEMBERS, 8).reshape(LB, RB)
-    right_part = mm(tile, tile, 0, 0).reshape(16, 16, RB)
-    right_own = jnp.sum(lax.all_to_all(right_part, RIGHT_GROUP, 0, 0, tiled=True), axis=0)
-    tiles = [tile] + [lax.ppermute(tile, "x", shift_perm(4, by)) for by in range(1, 4)]
-    squares = sum(jnp.sum(t * t) for t in tiles)
-
-    group = lax.axis_index(RIGHT_GROUP)
-    row = lax.broadcasted_iota(jnp.int32, (16, RB), 0)
-    col = lax.broadcasted_iota(jnp.int32, (16, RB), 1)
-    packed = jnp.where((row == 0) & (col == 16 * group + 1), squares, right_own)
-    right_raw = gather_all(packed, RIGHT_GROUP, 16).reshape(RB, RB)
-
-    left_raw = mm(tiles[0], tiles[0], 1, 1)
-    for t in tiles[1:]:
-        left_raw = left_raw + mm(t, t, 1, 1)
+    copies = small(own_sum_kernel, "own_sum", shape_of(8, 40, RB), 10**8, arrived)
+    tile = lax.all_to_all(copies, MEMBERS, 0, 0, tiled=True).reshape(LB, RB)
+    tile, mine, other = lax.optimization_barrier((tile, mine, other))
+
+    right_part = small(right_part_kernel, "right_part", shape_of(RB, RB), 10**9, tile)
+    parts = lax.all_to_all(right_part.reshape(16, 16, RB), RIGHT_GROUP, 0, 0, tiled=True)
+    tiles = gather_all(tile, "x", 4)
+    right_own, squares_own = small(
+        right_sum_kernel, "right_sum", (shape_of(16, 16, RB), shape_of(4, 8, 128)), 10**8,
+        lax.axis_index(RIGHT_GROUP).astype(jnp.int32).reshape(1), parts, scalars=1,
+    )
+    right_raw = lax.all_to_all(right_own, RIGHT_GROUP, 0, 0, tiled=True).reshape(RB, RB)
+    squares = lax.all_to_all(squares_own, "x", 0, 0, tiled=True)
+    left_raw = small(left_gram_kernel, "left_gram", shape_of(LB, LB), 2 * 10**9, tiles)
     swap = [(a * 4 + b, b * 4 + a) for a in range(4) for b in range(4)]
     held_raw = lax.ppermute(left_raw, ("yk", "x"), swap)
 
     right_new, right_basis_new, moment, second, turned, factor = refresh(
-        member.astype(jnp.int32).reshape(1), left_raw, moved[0], moved[1], right_raw,
-        right_gram[0], right_basis[0], tile, moments,
+        jnp.stack([lax.axis_index("y2"), lax.axis_index("zh")]).astype(jnp.int32), left_raw,
+        moved[0], moved[1], right_raw, right_gram[0], right_basis[0], tile, squares, mine, other,
     )
 
     before = lax.ppermute(turned, "yk", shift_perm(4, 1))

time: 218 us -> 261 us (1.20)
  the two profiles are of different devices: /device:TPU:6 before, /device:TPU:12 now
where the time goes in v3:
time: 261 us; the launch traced here: 260 us
  starting transfers between devices  102 us (39%)
  waiting for transfers between devices  89.3 us (34%)
  Pallas kernels  46.4 us (18%)
  local copies, waits for them, and re-layouts  9.37 us (4%)
  blocking collectives  7.59 us (3%)
  other arithmetic  4.33 us (2%)
    all_to_all x1, waiting for transfers between devices, gather_all(): return lax.all_to_all(copies, axes, 0, 0, tiled=True)  30 us
    ppermute x1, starting transfers between devices, shards(): after = lax.ppermute(turned, 'yk', shift_perm(4, -1))  29.1 us
    ppermute x1, waiting for transfers between devices, shards(): succ = lax.ppermute(ours, 'zh', shift_perm(4, -1))  28.1 us
    pallas_call x1, Pallas kernels, refresh(): pl.pallas_call(refresh_kernel, out_shape=(shape_of(RB, RB), shape_of(RB,...  24.2 us
    all_to_all x1, starting transfers between devices, shards(): arrived = lax.all_to_all(pieces, REP, 0, 0, tiled=True)  16.3 us
    pallas_call x1, Pallas kernels, refresh_held(): pl.pallas_call(held_kernel, out_shape=(shape_of(LB, LB), shape_of(LB, LB)...  15.4 us
    all_to_all x1, waiting for transfers between devices, shards(): lax.all_to_all(right_part.reshape(16, 16, RB), RIGHT_GROUP, 0, 0, tiled=T...  10.1 us
    ppermute x1, waiting for transfers between devices, shards(): other = lax.ppermute(mine, 'y2', shift_perm(2, 1))  8.87 us
  transfers between devices with their start and end apart: 18, of which 8 were waited for; matrix products, arithmetic and copies ran while one was open for 2% of the time, Pallas kernels for 17%

profile of v3, /device:TPU:12, one launch (start us, length us, event | category | flops | bytes accessed | tf_op | source)
XLA Modules:
  0.0 259.9 jit_solution(17757920204060887654)
XLA Ops:
  0.6 2.3 convert.1
  2.9 16.3 %all-to-all-start = ((f32[32,40,256]{2,1,0:T(8,128)}), f32[32,40,256]{2,1,0:T(8,128)S(1)}, u32[]{:S(2)}, u32[]{:S(2)}) async-start(f32[32,40,256]{2,1,0:T(8,128)} %convert.1), calls=%async_computation | async-start | bytes 2621440 | tf_op jit(solution)/shard_map/all_to_all | solution.py:327
  19.3 5.5 %collective-permute-start.1 = (f32[80,256]{1,0:T(8,128)S(1)}, f32[80,256]{1,0:T(8,128)S(1)}, u32[]{:S(2)}, u32[]{:S(2)}) collective-permute-start(f32[80,256]{1,0:T(8,128)S(1)} %get-tuple-element.43), channel_id=1, source_target_pairs={{0,48},{16,0},{32,16},{48,32},{1,49},{17,1},{33,17},{49,33},{2,50}... | collective-permute-start | bytes 245768 | tf_op jit(solution)/shard_map/ppermute | solution.py:313
  24.8 1.9 collective-permute-start
  26.7 28.1 %collective-permute-done.1 = f32[80,256]{1,0:T(8,128)S(1)} collective-permute-done((f32[80,256]{1,0:T(8,128)S(1)}, f32[80,256]{1,0:T(8,128)S(1)}, u32[]{:S(2)}, u32[]{:S(2)}) %collective-permute-start.1) | collective-permute-done | bytes 81952 | tf_op jit(solution)/shard_map/ppermute | solution.py:313
  54.8 2.1 collective-permute-start.3
  56.9 4.6 %collective-permute-start.2 = (f32[40,256]{1,0:T(8,128)S(1)}, f32[40,256]{1,0:T(8,128)S(1)}, u32[]{:S(2)}, u32[]{:S(2)}) collective-permute-start(f32[40,256]{1,0:T(8,128)S(1)} %slice.24), channel_id=1, source_target_pairs={{0,16},{16,32},{32,48},{48,0},{1,17},{17,33},{33,49},{49,1},{2,18}... | collective-permute-start | bytes 122888 | tf_op jit(solution)/shard_map/ppermute | solution.py:314
  61.6 0.8 own_sum.1
  62.4 6.8 %all-to-all-start.1 = ((f32[8,40,256]{2,1,0:T(8,128)}), f32[8,40,256]{2,1,0:T(8,128)S(1)}, u32[]{:S(2)}, u32[]{:S(2)}) async-start(f32[8,40,256]{2,1,0:T(8,128)} %own_sum.1), calls=%async_computation.1 | async-start | bytes 655360 | tf_op jit(solution)/shard_map/all_to_all | solution.py:329
  69.3 0.0 copy-start.3
  69.3 1.9 collective-permute-start.4
  71.2 8.9 %collective-permute-done.4.other_ref = f32[320,256]{1,0:T(8,128)S(1)} collective-permute-done((f32[320,256]{1,0:T(8,128)S(1)}, f32[320,256]{1,0:T(8,128)S(1)}, u32[]{:S(2)}, u32[]{:S(2)}) %collective-permute-start.4) | collective-permute-done | bytes 327712 | tf_op jit(solution)/shard_map/ppermute | solution.py:317
  80.1 0.7 copy-done.5
  80.8 1.3 right_part.1
  82.2 5.7 %all-to-all-start.3 = ((f32[16,16,256]{2,1,0:T(8,128)}), f32[16,16,256]{2,1,0:T(8,128)S(1)}, u32[]{:S(2)}, u32[]{:S(2)}) async-start(f32[16,16,256]{2,1,0:T(8,128)} %bitcast.8), calls=%async_computation.3 | async-start | bytes 524288 | tf_op jit(solution)/shard_map/all_to_all | solution.py:333
  87.9 10.1 %all-to-all-done.3.parts_ref = f32[16,16,256]{2,1,0:T(8,128)S(1)} async-done(((f32[16,16,256]{2,1,0:T(8,128)}), f32[16,16,256]{2,1,0:T(8,128)S(1)}, u32[]{:S(2)}, u32[]{:S(2)}) %all-to-all-start.3) | async-done | bytes 262176 | tf_op jit(solution)/shard_map/all_to_all | solution.py:333
  98.0 0.7 right_sum.1
  98.8 7.6 %all_to_all.30.squares_ref = f32[4,8,128]{2,1,0:T(8,128)S(1)} all-to-all(f32[4,8,128]{2,1,0:T(8,128)S(1)} %get-tuple-element.26), channel_id=1, replica_groups=mesh['yk'=4,'y2'=2,'zh'=4,'zl'=2,'core'=2,'x'=4] {'x'}, dimensions={0} | all-to-all | bytes 32768 | tf_op jit(solution)/shard_map/all_to_all | solution.py:340
  106.3 1.2 broadcast_in_dim.22
  107.5 6.1 %all-to-all-start.2 = ((f32[4,320,256]{2,1,0:T(8,128)}), f32[4,320,256]{2,1,0:T(8,128)S(1)}, u32[]{:S(2)}, u32[]{:S(2)}) async-start(f32[4,320,256]{2,1,0:T(8,128)} %broadcast_in_dim.22), calls=%async_computation.2 | async-start | bytes 2621440 | tf_op jit(solution)/shard_map/all_to_all | solution.py:298
  113.6 0.8 constant_dynamic-update-slice_fusion.9
  114.4 0.8 constant_dynamic-update-slice_fusion.8
  115.3 1.6 collective-permute-start.7
  116.9 1.3 collective-permute-start.6
  118.2 1.6 collective-permute-start.5
  119.8 0.1 pad_add_fusion.place_ref
  119.9 30.0 %all-to-all-done.2.tiles_ref = f32[4,320,256]{2,1,0:T(8,128)S(1)} async-done(((f32[4,320,256]{2,1,0:T(8,128)}), f32[4,320,256]{2,1,0:T(8,128)S(1)}, u32[]{:S(2)}, u32[]{:S(2)}) %all-to-all-start.2) | async-done | bytes 1310752 | tf_op jit(solution)/shard_map/all_to_all | solution.py:298
  149.9 3.5 %all-to-all-start.4 = ((f32[16,16,256]{2,1,0:T(8,128)}), f32[16,16,256]{2,1,0:T(8,128)S(1)}, u32[]{:S(2)}, u32[]{:S(2)}) async-start(f32[16,16,256]{2,1,0:T(8,128)} %get-tuple-element.25), calls=%async_computation.4 | async-start | bytes 524288 | tf_op jit(solution)/shard_map/all_to_all | solution.py:339
  153.4 2.0 add_add_fusion
  155.4 0.8 slice_bitcast_fusion
  156.3 3.0 %left_gram.1.left_raw_ref = f32[320,320]{1,0:T(8,128)} custom-call(f32[4,320,256]{2,1,0:T(8,128)S(1)} %all-to-all-done.2.tiles_ref), custom_call_target="tpu_custom_call" | custom-call | flops 2000000000 | bytes 1000000 | tf_op jit(solution)/shard_map/left_gram/pallas_call | solution.py:254
  159.3 4.4 %collective-permute-start.10 = (f32[320,320]{1,0:T(8,128)}, f32[320,320]{1,0:T(8,128)S(1)}, u32[]{:S(2)}, u32[]{:S(2)}) collective-permute-start(f32[320,320]{1,0:T(8,128)} %left_gram.1.left_raw_ref), channel_id=1, source_target_pairs={{0,0},{1,128},{2,256},{3,384},{128,1},{129,129},{130,257},{131,385... | collective-permute-start | bytes 1228808 | tf_op jit(solution)/shard_map/ppermute | solution.py:343
  163.7 1.2 all-to-all-done.4
  164.8 1.0 copy-done.2
  165.9 1.0 copy-done.4
  166.8 1.0 copy-done.6
  167.8 0.9 copy-done.7
  168.8 0.9 copy-done.8
  169.7 24.2 %refresh.1 = (f32[256,256]{1,0:T(8,128)}, f32[256,256]{1,0:T(8,128)}, f32[40,256]{1,0:T(8,128)}, f32[40,256]{1,0:T(8,128)}, f32[320,256]{1,0:T(8,128)S(1)}, /*index=5*/f32[8,128]{1,0:T(8,128)S(1)}) custom-call(s32[2]{0:T(128)S(1)} %pad_add_fusion.place_ref, f32[320,320]{1,0:T(8,128)} %left_gram.1.left_raw_ref, f32[320,320]{1,0:T(8,128)S(1)} %copy-done.2, ...), custom_call_target="tpu_custom_call" | custom-call | flops 24999999488 | bytes 4000000 | tf_op jit(solution)/shard_map/refresh/pallas_call | solution.py:175
  193.9 29.1 %collective-permute-start.9 = (f32[320,256]{1,0:T(8,128)S(1)}, f32[320,256]{1,0:T(8,128)S(1)}, u32[]{:S(2)}, u32[]{:S(2)}) collective-permute-start(f32[320,256]{1,0:T(8,128)S(1)} %get-tuple-element.29.refs_0_), channel_id=1, source_target_pairs={{0,384},{128,0},{256,128},{384,256},{1,385},{129,1},{257,129},{385... | collective-permute-start | bytes 983048 | tf_op jit(solution)/shard_map/ppermute | solution.py:351
  223.0 1.9 collective-permute-start.8
  224.9 15.4 %refresh_held.1 = (f32[320,320]{1,0:T(8,128)}, f32[320,320]{1,0:T(8,128)}) custom-call(f32[8,128]{1,0:T(8,128)S(1)} %get-tuple-element.30.factor_ref, f32[320,320]{1,0:T(8,128)S(1)} %collective-permute-done.10.raw_ref, f32[320,320]{1,0:T(8,128)S(1)} %bitcast.24, f32[320,320]{1,0:T(8,128)S(1)} %bitcast.25), custom_call_target="tpu_custom_call" | custom-call | flops 17999998976 | bytes 2000000 | tf_op jit(solution)/shard_map/refresh_held/pallas_call | solution.py:204
  240.4 0.7 collective-permute-done.8.refs_1_
  241.1 5.4 %collective-permute-start.12 = (f32[160,256]{1,0:T(8,128)S(1)}, f32[160,256]{1,0:T(8,128)S(1)}, u32[]{:S(2)}, u32[]{:S(2)}) collective-permute-start(f32[160,256]{1,0:T(8,128)S(1)} %slice.23), channel_id=1, source_target_pairs={{0,384},{128,0},{256,128},{384,256},{1,385},{129,1},{257,129},{385... | collective-permute-start | bytes 491528 | tf_op jit(solution)/shard_map/ppermute | solution.py:357
  246.5 1.9 collective-permute-start.11
  248.4 3.8 %collective-permute-done.12.refs_4_ = f32[160,256]{1,0:T(8,128)S(1)} collective-permute-done((f32[160,256]{1,0:T(8,128)S(1)}, f32[160,256]{1,0:T(8,128)S(1)}, u32[]{:S(2)}, u32[]{:S(2)}) %collective-permute-start.12) | collective-permute-done | bytes 163872 | tf_op jit(solution)/shard_map/ppermute | solution.py:357
  252.2 6.7 %collective-permute-done.11.refs_3_ = f32[160,256]{1,0:T(8,128)S(1)} collective-permute-done((f32[160,256]{1,0:T(8,128)S(1)}, f32[160,256]{1,0:T(8,128)S(1)}, u32[]{:S(2)}, u32[]{:S(2)}) %collective-permute-start.11) | collective-permute-done | bytes 163872 | tf_op jit(solution)/shard_map/ppermute | solution.py:356
  258.9 0.9 place.1
  (35 shorter events, 0.1 us)
Async XLA Ops:
  2.9 16.3 %copy-start.9 = (f32[40,256]{1,0:T(8,128)S(1)}, f32[40,256]{1,0:T(8,128)}, u32[]{:S(2)}) copy-start(f32[40,256]{1,0:T(8,128)} %param.12) | copy-start | bytes 122884
  2.9 16.3 %copy-start.10 = (f32[40,256]{1,0:T(8,128)S(1)}, f32[40,256]{1,0:T(8,128)}, u32[]{:S(2)}) copy-start(f32[40,256]{1,0:T(8,128)} %param.13) | copy-start | bytes 122884
  2.9 58.6 %all-to-all-start = ((f32[32,40,256]{2,1,0:T(8,128)}), f32[32,40,256]{2,1,0:T(8,128)S(1)}, u32[]{:S(2)}, u32[]{:S(2)}) async-start(f32[32,40,256]{2,1,0:T(8,128)} %convert.1), calls=%async_computation | async-start | bytes 2621440 | tf_op jit(solution)/shard_map/all_to_all | solution.py:327
  19.3 35.5 %collective-permute-start.1 = (f32[80,256]{1,0:T(8,128)S(1)}, f32[80,256]{1,0:T(8,128)S(1)}, u32[]{:S(2)}, u32[]{:S(2)}) collective-permute-start(f32[80,256]{1,0:T(8,128)S(1)} %get-tuple-element.43), channel_id=1, source_target_pairs={{0,48},{16,0},{32,16},{48,32},{1,49},{17,1},{33,17},{49,33},{2,50}... | collective-permute-start | bytes 245768 | tf_op jit(solution)/shard_map/ppermute | solution.py:313
  24.8 32.1 %collective-permute-start = (f32[80,256]{1,0:T(8,128)S(1)}, f32[80,256]{1,0:T(8,128)S(1)}, u32[]{:S(2)}, u32[]{:S(2)}) collective-permute-start(f32[80,256]{1,0:T(8,128)S(1)} %get-tuple-element.43), channel_id=1, source_target_pairs={{0,16},{16,32},{32,48},{48,0},{1,17},{17,33},{33,49},{49,1},{2,18}... | collective-permute-start | bytes 245768 | tf_op jit(solution)/shard_map/ppermute | solution.py:312
  54.8 14.5 %collective-permute-start.3 = (f32[40,256]{1,0:T(8,128)S(1)}, f32[40,256]{1,0:T(8,128)S(1)}, u32[]{:S(2)}, u32[]{:S(2)}) collective-permute-start(f32[40,256]{1,0:T(8,128)S(1)} %slice.25), channel_id=1, source_target_pairs={{0,48},{16,0},{32,16},{48,32},{1,49},{17,1},{33,17},{49,33},{2,50}... | collective-permute-start | bytes 122888 | tf_op jit(solution)/shard_map/ppermute | solution.py:315
  56.9 12.3 %collective-permute-start.2 = (f32[40,256]{1,0:T(8,128)S(1)}, f32[40,256]{1,0:T(8,128)S(1)}, u32[]{:S(2)}, u32[]{:S(2)}) collective-permute-start(f32[40,256]{1,0:T(8,128)S(1)} %slice.24), channel_id=1, source_target_pairs={{0,16},{16,32},{32,48},{48,0},{1,17},{17,33},{33,49},{49,1},{2,18}... | collective-permute-start | bytes 122888 | tf_op jit(solution)/shard_map/ppermute | solution.py:314
  62.4 18.4 %all-to-all-start.1 = ((f32[8,40,256]{2,1,0:T(8,128)}), f32[8,40,256]{2,1,0:T(8,128)S(1)}, u32[]{:S(2)}, u32[]{:S(2)}) async-start(f32[8,40,256]{2,1,0:T(8,128)} %own_sum.1), calls=%async_computation.1 | async-start | bytes 655360 | tf_op jit(solution)/shard_map/all_to_all | solution.py:329
  69.3 12.9 %copy-start.3 = (f32[320,256]{1,0:T(8,128)}, f32[320,256]{1,0:T(8,128)S(1)}, u32[]{:S(2)}) copy-start(f32[320,256]{1,0:T(8,128)S(1)} %constant_dynamic-update-slice_fusion.2.mine_ref) | copy-start | bytes 983044
  69.3 10.8 %collective-permute-start.4 = (f32[320,256]{1,0:T(8,128)S(1)}, f32[320,256]{1,0:T(8,128)S(1)}, u32[]{:S(2)}, u32[]{:S(2)}) collective-permute-start(f32[320,256]{1,0:T(8,128)S(1)} %constant_dynamic-update-slice_fusion.2.mine_ref), channel_id=1, source_target_pairs={{0,64},{64,0},{1,65},{65,1},{2,66},{66,2},{3,67},{67,3},{4,68},{68... | collective-permute-start | bytes 983048 | tf_op jit(solution)/shard_map/ppermute | solution.py:317
  80.1 0.7 copy-start.5
  82.2 15.9 %all-to-all-start.3 = ((f32[16,16,256]{2,1,0:T(8,128)}), f32[16,16,256]{2,1,0:T(8,128)S(1)}, u32[]{:S(2)}, u32[]{:S(2)}) async-start(f32[16,16,256]{2,1,0:T(8,128)} %bitcast.8), calls=%async_computation.3 | async-start | bytes 524288 | tf_op jit(solution)/shard_map/all_to_all | solution.py:333
  107.5 6.1 %copy-start = (f32[1,320,320]{2,1,0:T(8,128)S(1)}, f32[1,320,320]{2,1,0:T(8,128)}, u32[]{:S(2)}) copy-start(f32[1,320,320]{2,1,0:T(8,128)} %param.8) | copy-start | bytes 1228804
  107.5 6.9 %copy-start.1 = (f32[1,320,320]{2,1,0:T(8,128)S(1)}, f32[1,320,320]{2,1,0:T(8,128)}, u32[]{:S(2)}) copy-start(f32[1,320,320]{2,1,0:T(8,128)} %param.10) | copy-start | bytes 1228804
  107.5 42.3 %all-to-all-start.2 = ((f32[4,320,256]{2,1,0:T(8,128)}), f32[4,320,256]{2,1,0:T(8,128)S(1)}, u32[]{:S(2)}, u32[]{:S(2)}) async-start(f32[4,320,256]{2,1,0:T(8,128)} %broadcast_in_dim.22), calls=%async_computation.2 | async-start | bytes 2621440 | tf_op jit(solution)/shard_map/all_to_all | solution.py:298
  115.3 38.1 %collective-permute-start.7 = (f32[2,320,320]{2,1,0:T(8,128)}, f32[2,320,320]{2,1,0:T(8,128)}, u32[]{:S(2)}, u32[]{:S(2)}) collective-permute-start(f32[2,320,320]{2,1,0:T(8,128)} %constant_dynamic-update-slice_fusion.8), channel_id=1, source_target_pairs={{0,3},{129,128},{258,257},{387,386},{4,7},{133,132},{262,261},{391... | collective-permute-start | bytes 2457608 | tf_op jit(solution)/shard_map/ppermute | solution.py:322
  116.9 36.5 %collective-permute-start.6 = (f32[2,320,320]{2,1,0:T(8,128)}, f32[2,320,320]{2,1,0:T(8,128)}, u32[]{:S(2)}, u32[]{:S(2)}) collective-permute-start(f32[2,320,320]{2,1,0:T(8,128)} %constant_dynamic-update-slice_fusion.8), channel_id=1, source_target_pairs={{0,2},{129,131},{258,256},{387,385},{4,6},{133,135},{262,260},{391... | collective-permute-start | bytes 2457608 | tf_op jit(solution)/shard_map/ppermute | solution.py:322
  118.2 35.2 %collective-permute-start.5 = (f32[2,320,320]{2,1,0:T(8,128)}, f32[2,320,320]{2,1,0:T(8,128)}, u32[]{:S(2)}, u32[]{:S(2)}) collective-permute-start(f32[2,320,320]{2,1,0:T(8,128)} %constant_dynamic-update-slice_fusion.8), channel_id=1, source_target_pairs={{0,1},{129,130},{258,259},{387,384},{4,5},{133,134},{262,263},{391... | collective-permute-start | bytes 2457608 | tf_op jit(solution)/shard_map/ppermute | solution.py:322
  149.9 15.0 %all-to-all-start.4 = ((f32[16,16,256]{2,1,0:T(8,128)}), f32[16,16,256]{2,1,0:T(8,128)S(1)}, u32[]{:S(2)}, u32[]{:S(2)}) async-start(f32[16,16,256]{2,1,0:T(8,128)} %get-tuple-element.25), calls=%async_computation.4 | async-start | bytes 524288 | tf_op jit(solution)/shard_map/all_to_all | solution.py:339
  159.3 65.6 %collective-permute-start.10 = (f32[320,320]{1,0:T(8,128)}, f32[320,320]{1,0:T(8,128)S(1)}, u32[]{:S(2)}, u32[]{:S(2)}) collective-permute-start(f32[320,320]{1,0:T(8,128)} %left_gram.1.left_raw_ref), channel_id=1, source_target_pairs={{0,0},{1,128},{2,256},{3,384},{128,1},{129,129},{130,257},{131,385... | collective-permute-start | bytes 1228808 | tf_op jit(solution)/shard_map/ppermute | solution.py:343
  164.8 1.0 copy-start.2
  165.9 1.0 copy-start.4
  166.8 1.0 copy-start.6
  167.8 0.9 copy-start.7
  168.8 0.9 copy-start.8
  193.9 46.5 %collective-permute-start.9 = (f32[320,256]{1,0:T(8,128)S(1)}, f32[320,256]{1,0:T(8,128)S(1)}, u32[]{:S(2)}, u32[]{:S(2)}) collective-permute-start(f32[320,256]{1,0:T(8,128)S(1)} %get-tuple-element.29.refs_0_), channel_id=1, source_target_pairs={{0,384},{128,0},{256,128},{384,256},{1,385},{129,1},{257,129},{385... | collective-permute-start | bytes 983048 | tf_op jit(solution)/shard_map/ppermute | solution.py:351
  223.0 18.0 %collective-permute-start.8 = (f32[320,256]{1,0:T(8,128)S(1)}, f32[320,256]{1,0:T(8,128)S(1)}, u32[]{:S(2)}, u32[]{:S(2)}) collective-permute-start(f32[320,256]{1,0:T(8,128)S(1)} %get-tuple-element.29.refs_0_), channel_id=1, source_target_pairs={{0,128},{128,256},{256,384},{384,0},{1,129},{129,257},{257,385},{3... | collective-permute-start | bytes 983048 | tf_op jit(solution)/shard_map/ppermute | solution.py:350
  241.1 11.1 %collective-permute-start.12 = (f32[160,256]{1,0:T(8,128)S(1)}, f32[160,256]{1,0:T(8,128)S(1)}, u32[]{:S(2)}, u32[]{:S(2)}) collective-permute-start(f32[160,256]{1,0:T(8,128)S(1)} %slice.23), channel_id=1, source_target_pairs={{0,384},{128,0},{256,128},{384,256},{1,385},{129,1},{257,129},{385... | collective-permute-start | bytes 491528 | tf_op jit(solution)/shard_map/ppermute | solution.py:357
  246.5 12.4 %collective-permute-start.11 = (f32[160,256]{1,0:T(8,128)S(1)}, f32[160,256]{1,0:T(8,128)S(1)}, u32[]{:S(2)}, u32[]{:S(2)}) collective-permute-start(f32[160,256]{1,0:T(8,128)S(1)} %slice.22), channel_id=1, source_target_pairs={{0,128},{128,256},{256,384},{384,0},{1,129},{129,257},{257,385},{3... | collective-permute-start | bytes 491528 | tf_op jit(solution)/shard_map/ppermute | solution.py:356

commit v4 on v3

--- a/solution.py
+++ b/solution.py
@@ -121,21 +121,21 @@
 
 
 def refresh_kernel(
-    place_ref, left_raw_ref, gl_ref, bl_ref, right_raw_ref, gr_ref, br_ref, tile_ref, squares_ref,
-    mine_ref, other_ref,
+    place_ref, left_raw_ref, gl_ref, bl_ref, right_raw_ref, gr_ref, br_ref, tile_ref, sq0_ref, sq1_ref,
+    sq2_ref, sq3_ref, mine_ref, other_ref,
     gr_out_ref, qr_out_ref, m_ref, v_ref, u_ref, factor_ref,
     sl_ref, pl_ref, qlt_ref, sr_ref, pr_ref, qrt_ref, ms_ref, vs_ref,
 ):
     y2, zh = place_ref[0], place_ref[1]
     for src_ref, pair in ((mine_ref, y2), (other_ref, 1 - y2)):
-        for n, shift in enumerate((0, -1, 1, 2)):
+        for n, shift in enumerate((0, -1, -2, -3)):
             at = pl.multiple_of(40 * (4 * pair + lax.rem(zh + shift + 4, 4)), 8)
             ms_ref[pl.ds(at, 40), :] = src_ref[80 * n : 80 * n + 40, :]
             vs_ref[pl.ds(at, 40), :] = src_ref[80 * n + 40 : 80 * n + 80, :]
     packed = right_raw_ref[...]
     slot = slots((RB, RB), 0, 1)
     right_raw = jnp.where(slot, packed.T, packed)
-    total = (squares_ref[0] + squares_ref[1] + squares_ref[2] + squares_ref[3])[:1, :1]
+    total = (sq0_ref[...] + sq1_ref[...] + (sq2_ref[...] + sq3_ref[...]))[:1, :1]
     factor = clip_ratio * math.sqrt(D * KV) / (jnp.sqrt(total) + 1e-06)
     factor_ref[...] = jnp.broadcast_to(factor, factor_ref.shape)
     weight = (1.0 - beta_gram) * factor * factor
@@ -178,7 +178,7 @@
             shape_of(RB, RB), shape_of(RB, RB), shape_of(40, RB), shape_of(40, RB),
             shape_of(LB, RB), shape_of(8, 128),
         ),
-        in_specs=[pl.BlockSpec(memory_space=pltpu.SMEM)] + [whole()] * 10,
+        in_specs=[pl.BlockSpec(memory_space=pltpu.SMEM)] + [whole()] * 4 + [pl.BlockSpec()] * 2 + [whole()] * 7,
         out_specs=(whole(),) * 6,
         scratch_shapes=[pltpu.VMEM((LB, LB), f32)] * 3
         + [pltpu.VMEM((RB, RB), f32)] * 3
@@ -188,7 +188,7 @@
             flops=25_000_000_000, bytes_accessed=4_000_000, transcendentals=0
         ),
         name="refresh",
-    )(spot, left_raw, gl, bl, right_raw, gr, br, tile, squares, mine, other)
+    )(spot, left_raw, gl, bl, right_raw, gr, br, tile, *squares, mine, other)
 
 
 def held_kernel(factor_ref, raw_ref, g_ref, b_ref, g_out_ref, q_out_ref, s_ref, p_ref, qt_ref):
@@ -204,7 +204,7 @@
     return pl.pallas_call(
         held_kernel,
         out_shape=(shape_of(LB, LB), shape_of(LB, LB)),
-        in_specs=[whole()] * 4,
+        in_specs=[whole()] * 2 + [pl.BlockSpec()] * 2,
         out_specs=(whole(),) * 2,
         scratch_shapes=[pltpu.VMEM((LB, LB), f32)] * 3,
         compiler_params=pltpu.CompilerParams(vmem_limit_bytes=24 * 2**20),
@@ -241,11 +241,11 @@
     squares_ref[...] = jnp.broadcast_to(squares, squares_ref.shape)
 
 
-def left_gram_kernel(tiles_ref, out_ref):
-    total = mm(tiles_ref[0], tiles_ref[0], 1, 1)
+def left_gram_kernel(*refs):
+    total = mm(refs[0][...], refs[0][...], 1, 1)
     for n in range(1, 4):
-        total = total + mm(tiles_ref[n], tiles_ref[n], 1, 1)
-    out_ref[...] = total
+        total = total + mm(refs[n][...], refs[n][...], 1, 1)
+    refs[4][...] = total
 
 
 def small(kernel, name, out_shape, flops, *operands, scalars=0):
@@ -262,15 +262,15 @@
     )(*operands)
 
 
-PLACES = ((0, 0, 320), (-1, 0, 320), (1, 0, 320), (2, 0, 160), (2, 160, 160))
+PLACES = (0, -2, -1, -3)
 
 
 def place_kernel(k_ref, *refs):
     parts, out_ref, rounded_ref, sems = refs[:-3], refs[-3], refs[-2], refs[-1]
     copies = []
-    for n, (shift, first, count) in enumerate(PLACES):
+    for n, shift in enumerate(PLACES):
         source = lax.rem(k_ref[0] + shift + 4, 4)
-        at = pl.ds(pl.multiple_of(source * LB + first, 16), count)
+        at = pl.ds(pl.multiple_of(source * LB, 16), LB)
         rounded_ref[at, :] = parts[n][...].astype(jnp.bfloat16)
         copies.append(pltpu.make_async_copy(rounded_ref.at[at], out_ref.at[at], sems.at[n]))
         copies[-1].start()
@@ -309,12 +309,7 @@
     x = lax.axis_index("x")
 
     ours = jnp.concatenate([first_moment, second_moment], axis=0)
-    prev = lax.ppermute(ours, "zh", shift_perm(4, 1))
-    succ = lax.ppermute(ours, "zh", shift_perm(4, -1))
-    far_first = lax.ppermute(prev[:40], "zh", shift_perm(4, 1))
-    far_second = lax.ppermute(succ[40:], "zh", shift_perm(4, -1))
-    mine = jnp.concatenate([ours, prev, succ, far_first, far_second], axis=0)
-    other = lax.ppermute(mine, "y2", shift_perm(2, 1))
+    column = [ours] + [lax.ppermute(ours, "zh", shift_perm(4, by)) for by in range(1, 4)]
 
     held = jnp.concatenate([left_gram, left_basis], axis=0)
     moved = jnp.where(x == k, held, 0.0)
@@ -325,20 +320,27 @@
 
     pieces = pseudo_grads[0].astype(jnp.float32).reshape(32, 40, RB)
     arrived = lax.all_to_all(pieces, REP, 0, 0, tiled=True)
+    arrived, moved = lax.optimization_barrier((arrived, moved))
     copies = small(own_sum_kernel, "own_sum", shape_of(8, 40, RB), 10**8, arrived)
+    copies, *column = lax.optimization_barrier((copies, *column))
     tile = lax.all_to_all(copies, MEMBERS, 0, 0, tiled=True).reshape(LB, RB)
+    mine = jnp.concatenate(column, axis=0)
+    other = lax.ppermute(mine, "y2", shift_perm(2, 1))
     tile, mine, other = lax.optimization_barrier((tile, mine, other))
 
     right_part = small(right_part_kernel, "right_part", shape_of(RB, RB), 10**9, tile)
+    sent, right_part = lax.optimization_barrier((tile, right_part))
     parts = lax.all_to_all(right_part.reshape(16, 16, RB), RIGHT_GROUP, 0, 0, tiled=True)
-    tiles = gather_all(tile, "x", 4)
+    tiles = [tile] + [lax.ppermute(sent, "x", shift_perm(4, by)) for by in range(1, 4)]
     right_own, squares_own = small(
-        right_sum_kernel, "right_sum", (shape_of(16, 16, RB), shape_of(4, 8, 128)), 10**8,
+        right_sum_kernel, "right_sum", (shape_of(16, 16, RB), shape_of(8, 128)), 10**8,
         lax.axis_index(RIGHT_GROUP).astype(jnp.int32).reshape(1), parts, scalars=1,
     )
     right_raw = lax.all_to_all(right_own, RIGHT_GROUP, 0, 0, tiled=True).reshape(RB, RB)
-    squares = lax.all_to_all(squares_own, "x", 0, 0, tiled=True)
-    left_raw = small(left_gram_kernel, "left_gram", shape_of(LB, LB), 2 * 10**9, tiles)
+    squares = [squares_own] + [
+        lax.ppermute(squares_own, "x", shift_perm(4, by)) for by in range(1, 4)
+    ]
+    left_raw = small(left_gram_kernel, "left_gram", shape_of(LB, LB), 2 * 10**9, *tiles)
     swap = [(a * 4 + b, b * 4 + a) for a in range(4) for b in range(4)]
     held_raw = lax.ppermute(left_raw, ("yk", "x"), swap)
 
@@ -347,15 +349,12 @@
         moved[0], moved[1], right_raw, right_gram[0], right_basis[0], tile, squares, mine, other,
     )
 
-    before = lax.ppermute(turned, "yk", shift_perm(4, 1))
-    after = lax.ppermute(turned, "yk", shift_perm(4, -1))
+    blocks = [turned] + [lax.ppermute(turned, "yk", shift_perm(4, by)) for by in (2, 1, 3)]
     left_new, left_basis_new = refresh_held(factor, held_raw, left_gram[0], left_basis[0])
-    before, after, left_new, left_basis_new = lax.optimization_barrier(
-        (before, after, left_new, left_basis_new)
-    )
-    upper = lax.ppermute(before[:160], "yk", shift_perm(4, 1))
-    lower = lax.ppermute(after[160:], "yk", shift_perm(4, -1))
-    update = place(k.astype(jnp.int32).reshape(1), [turned, before, after, upper, lower])
+    *blocks, left_new, left_basis_new = lax.optimization_barrier(
+        (*blocks, left_new, left_basis_new)
+    )
+    update = place(k.astype(jnp.int32).reshape(1), blocks)
     return (
         update, left_new[None], left_basis_new[None], right_new[None], right_basis_new[None],
         moment, second,

time: 261 us -> 219 us (0.84)
  the two profiles are of different devices: /device:TPU:12 before, /device:TPU:6 now
where the time goes in v4:
time: 219 us; the launch traced here: 215 us
  starting transfers between devices  110 us (50%)
  Pallas kernels  47.1 us (22%)
  waiting for transfers between devices  40.1 us (18%)
  local copies, waits for them, and re-layouts  10.6 us (5%)
  other arithmetic  5.8 us (3%)
    pallas_call x1, Pallas kernels, refresh(): pl.pallas_call(refresh_kernel, out_shape=(shape_of(RB, RB), shape_of(RB,...  23.7 us
    all_to_all x1, starting transfers between devices, shards(): lax.all_to_all(right_part.reshape(16, 16, RB), RIGHT_GROUP, 0, 0, tiled=T...  18.6 us
    pallas_call x1, Pallas kernels, refresh_held(): pl.pallas_call(held_kernel, out_shape=(shape_of(LB, LB), shape_of(LB, LB)...  16.5 us
    all_to_all x1, starting transfers between devices, shards(): arrived = lax.all_to_all(pieces, REP, 0, 0, tiled=True)  16.1 us
    ppermute x3, starting transfers between devices, shards(): lax.ppermute(ours, 'zh', shift_perm(4, by))  15.6 us
    ppermute x1, waiting for transfers between devices, shards(): held_raw = lax.ppermute(left_raw, ('yk', 'x'), swap)  14.6 us
    ppermute x3, starting transfers between devices, shards(): lax.ppermute(turned, 'yk', shift_perm(4, by))  10.8 us
    ppermute x3, waiting for transfers between devices, shards(): lax.ppermute(held, ('yk', 'x'), [(b * 4 + b, b * 4 + (b + by) % 4) for b...  10.6 us
  transfers between devices with their start and end apart: 21, of which 6 were waited for; matrix products, arithmetic and copies ran while one was open for 3% of the time, Pallas kernels for 21%

profile of v4, /device:TPU:6, one launch (start us, length us, event | category | flops | bytes accessed | tf_op | source)
XLA Modules:
  0.0 214.9 jit_solution(9316352392793694944)
XLA Ops:
  0.6 2.3 %convert.1 = f32[32,40,256]{2,1,0:T(8,128)} convert(bf16[32,40,256]{2,1,0:T(8,128)(2,1)} %bitcast.32) | non-fusion elementwise | flops 327680 | bytes 1966080 | tf_op jit(solution)/shard_map/convert_element_type | solution.py:321
  2.9 16.1 %all-to-all-start = ((f32[32,40,256]{2,1,0:T(8,128)}), f32[32,40,256]{2,1,0:T(8,128)S(1)}, u32[]{:S(2)}, u32[]{:S(2)}) async-start(f32[32,40,256]{2,1,0:T(8,128)} %convert.1), calls=%async_computation | async-start | bytes 2621440 | tf_op jit(solution)/shard_map/all_to_all | solution.py:322
  19.0 0.8 constant_dynamic-update-slice_fusion.1
  19.9 0.8 constant_dynamic-update-slice_fusion
  20.7 1.6 collective-permute-start
  22.3 1.6 collective-permute-start.1
  23.9 1.3 collective-permute-start.2
  25.3 4.6 %collective-permute-start.3 = (f32[80,256]{1,0:T(8,128)S(1)}, f32[80,256]{1,0:T(8,128)S(1)}, u32[]{:S(2)}, u32[]{:S(2)}) collective-permute-start(f32[80,256]{1,0:T(8,128)S(1)} %constant_dynamic-update-slice_fusion.2), channel_id=1, source_target_pairs={{0,16},{16,32},{32,48},{48,0},{1,17},{17,33},{33,49},{49,1},{2,18}... | collective-permute-start | bytes 245768 | tf_op jit(solution)/shard_map/ppermute | solution.py:312
  29.9 5.5 %collective-permute-start.4 = (f32[80,256]{1,0:T(8,128)S(1)}, f32[80,256]{1,0:T(8,128)S(1)}, u32[]{:S(2)}, u32[]{:S(2)}) collective-permute-start(f32[80,256]{1,0:T(8,128)S(1)} %constant_dynamic-update-slice_fusion.2), channel_id=1, source_target_pairs={{0,32},{16,48},{32,0},{48,16},{1,33},{17,49},{33,1},{49,17},{2,34}... | collective-permute-start | bytes 245768 | tf_op jit(solution)/shard_map/ppermute | solution.py:312
  35.4 5.5 %collective-permute-start.5 = (f32[80,256]{1,0:T(8,128)S(1)}, f32[80,256]{1,0:T(8,128)S(1)}, u32[]{:S(2)}, u32[]{:S(2)}) collective-permute-start(f32[80,256]{1,0:T(8,128)S(1)} %constant_dynamic-update-slice_fusion.2), channel_id=1, source_target_pairs={{0,48},{16,0},{32,16},{48,32},{1,49},{17,1},{33,17},{49,33},{2,50}... | collective-permute-start | bytes 245768 | tf_op jit(solution)/shard_map/ppermute | solution.py:312
  40.9 10.6 %collective-permute-done.2 = f32[2,320,320]{2,1,0:T(8,128)} collective-permute-done((f32[2,320,320]{2,1,0:T(8,128)}, f32[2,320,320]{2,1,0:T(8,128)}, u32[]{:S(2)}, u32[]{:S(2)}) %collective-permute-start.2) | collective-permute-done | bytes 819232 | tf_op jit(solution)/shard_map/ppermute | solution.py:317
  51.4 2.9 %add_add_fusion = f32[2,320,320]{2,1,0:T(8,128)} fusion(f32[2,320,320]{2,1,0:T(8,128)} %collective-permute-done.2, f32[2,320,320]{2,1,0:T(8,128)} %collective-permute-done.1, f32[2,320,320]{2,1,0:T(8,128)} %collective-permute-done, f32[2,320,320]{2,1,0:T(8,128)} %constant_dynamic-update-slice_fusion, pred[]{:T(512)S(6)} %eq.3), kind=kLoop, calls=%fused_computation | loop fusion | flops 819200 | bytes 4096001 | tf_op jit(solution)/shard_map/add | solution.py:317
  54.4 0.8 own_sum.1
  55.2 1.2 collective-permute-done.3
  56.4 4.0 %collective-permute-done.4 = f32[80,256]{1,0:T(8,128)S(1)} collective-permute-done((f32[80,256]{1,0:T(8,128)S(1)}, f32[80,256]{1,0:T(8,128)S(1)}, u32[]{:S(2)}, u32[]{:S(2)}) %collective-permute-start.4) | collective-permute-done | bytes 81952 | tf_op jit(solution)/shard_map/ppermute | solution.py:312
  60.4 3.4 %all-to-all-start.1 = ((f32[8,40,256]{2,1,0:T(8,128)}), f32[8,40,256]{2,1,0:T(8,128)S(1)}, u32[]{:S(2)}, u32[]{:S(2)}) async-start(f32[8,40,256]{2,1,0:T(8,128)} %own_sum.1), calls=%async_computation.1 | async-start | bytes 655360 | tf_op jit(solution)/shard_map/all_to_all | solution.py:326
  63.9 3.8 %collective-permute-start.6 = (f32[320,256]{1,0:T(8,128)S(1)}, f32[320,256]{1,0:T(8,128)S(1)}, u32[]{:S(2)}, u32[]{:S(2)}) collective-permute-start(f32[320,256]{1,0:T(8,128)S(1)} %constant_dynamic-update-slice_fusion.4.mine_ref), channel_id=1, source_target_pairs={{0,64},{64,0},{1,65},{65,1},{2,66},{66,2},{3,67},{67,3},{4,68},{68... | collective-permute-start | bytes 983048 | tf_op jit(solution)/shard_map/ppermute | solution.py:328
  67.7 9.5 %collective-permute-done.6.other_ref = f32[320,256]{1,0:T(8,128)S(1)} collective-permute-done((f32[320,256]{1,0:T(8,128)S(1)}, f32[320,256]{1,0:T(8,128)S(1)}, u32[]{:S(2)}, u32[]{:S(2)}) %collective-permute-start.6) | collective-permute-done | bytes 327712 | tf_op jit(solution)/shard_map/ppermute | solution.py:328
  77.2 0.7 copy-done.2
  77.9 1.3 right_part.1
  79.3 18.6 %all-to-all-start.2 = ((f32[16,16,256]{2,1,0:T(8,128)}), f32[16,16,256]{2,1,0:T(8,128)S(1)}, u32[]{:S(2)}, u32[]{:S(2)}) async-start(f32[16,16,256]{2,1,0:T(8,128)} %bitcast.8), calls=%async_computation.2 | async-start | bytes 524288 | tf_op jit(solution)/shard_map/all_to_all | solution.py:333
  97.9 5.5 %collective-permute-start.7 = (f32[320,256]{1,0:T(8,128)S(1)}, f32[320,256]{1,0:T(8,128)S(1)}, u32[]{:S(2)}, u32[]{:S(2)}) collective-permute-start(f32[320,256]{1,0:T(8,128)S(1)} %bitcast.24), channel_id=1, source_target_pairs={{0,1},{1,2},{2,3},{3,0},{4,5},{5,6},{6,7},{7,4},{8,9},{9,10},{10,1... | collective-permute-start | bytes 983048 | tf_op jit(solution)/shard_map/ppermute | solution.py:334
  103.4 2.6 %collective-permute-start.8 = (f32[320,256]{1,0:T(8,128)S(1)}, f32[320,256]{1,0:T(8,128)S(1)}, u32[]{:S(2)}, u32[]{:S(2)}) collective-permute-start(f32[320,256]{1,0:T(8,128)S(1)} %bitcast.25), channel_id=1, source_target_pairs={{0,2},{1,3},{2,0},{3,1},{4,6},{5,7},{6,4},{7,5},{8,10},{9,11},{10,... | collective-permute-start | bytes 983048 | tf_op jit(solution)/shard_map/ppermute | solution.py:334
  106.1 2.1 collective-permute-start.9
  108.4 0.7 right_sum.1
  109.1 7.8 %all-to-all-start.3 = ((f32[16,16,256]{2,1,0:T(8,128)}), f32[16,16,256]{2,1,0:T(8,128)S(1)}, u32[]{:S(2)}, u32[]{:S(2)}) async-start(f32[16,16,256]{2,1,0:T(8,128)} %get-tuple-element.45), calls=%async_computation.3 | async-start | bytes 524288 | tf_op jit(solution)/shard_map/all_to_all | solution.py:339
  117.0 0.6 pad_add_fusion.place_ref
  117.6 1.2 slice_bitcast_fusion
  118.8 5.0 %collective-permute-start.10 = (f32[8,128]{1,0:T(8,128)S(1)}, f32[8,128]{1,0:T(8,128)S(1)}, u32[]{:S(2)}, u32[]{:S(2)}) collective-permute-start(f32[8,128]{1,0:T(8,128)S(1)} %get-tuple-element.46.sq0_ref), channel_id=1, source_target_pairs={{0,1},{1,2},{2,3},{3,0},{4,5},{5,6},{6,7},{7,4},{8,9},{9,10},{10,1... | collective-permute-start | bytes 12296 | tf_op jit(solution)/shard_map/ppermute | solution.py:341
  123.8 3.5 %collective-permute-start.11 = (f32[8,128]{1,0:T(8,128)S(1)}, f32[8,128]{1,0:T(8,128)S(1)}, u32[]{:S(2)}, u32[]{:S(2)}) collective-permute-start(f32[8,128]{1,0:T(8,128)S(1)} %get-tuple-element.46.sq0_ref), channel_id=1, source_target_pairs={{0,2},{1,3},{2,0},{3,1},{4,6},{5,7},{6,4},{7,5},{8,10},{9,11},{10,... | collective-permute-start | bytes 12296 | tf_op jit(solution)/shard_map/ppermute | solution.py:341
  127.4 0.7 copy-done.4
  128.1 1.9 collective-permute-start.12
  130.0 0.7 copy-done.6
  130.7 1.0 copy-done.5
  131.7 1.0 copy-done.7
  132.7 3.2 %left_gram.1.left_raw_ref = f32[320,320]{1,0:T(8,128)S(1)} custom-call(f32[320,256]{1,0:T(8,128)S(1)} %bitcast.27, f32[320,256]{1,0:T(8,128)S(1)} %copy-done.5, f32[320,256]{1,0:T(8,128)S(1)} %copy-done.7, f32[320,256]{1,0:T(8,128)} %collective-permute-done.9.refs_3_), custom_call_target="tpu_custom_call" | custom-call | flops 2000000000 | bytes 1000000 | tf_op jit(solution)/shard_map/left_gram/pallas_call | solution.py:254
  135.9 8.8 %collective-permute-start.16 = (f32[320,320]{1,0:T(8,128)S(1)}, f32[320,320]{1,0:T(8,128)}, u32[]{:S(2)}, u32[]{:S(2)}) collective-permute-start(f32[320,320]{1,0:T(8,128)S(1)} %left_gram.1.left_raw_ref), channel_id=1, source_target_pairs={{0,0},{1,128},{2,256},{3,384},{128,1},{129,129},{130,257},{131,385... | collective-permute-start | bytes 1228808 | tf_op jit(solution)/shard_map/ppermute | solution.py:345
  144.7 1.0 copy-done.3
  145.7 0.9 copy-done.8
  146.6 0.9 copy-done.9
  147.6 0.7 copy-done.10
  148.2 23.7 %refresh.1 = (f32[256,256]{1,0:T(8,128)}, f32[256,256]{1,0:T(8,128)}, f32[40,256]{1,0:T(8,128)}, f32[40,256]{1,0:T(8,128)}, f32[320,256]{1,0:T(8,128)S(1)}, /*index=5*/f32[8,128]{1,0:T(8,128)S(1)}) custom-call(s32[2]{0:T(128)S(1)} %copy-done.10, f32[320,320]{1,0:T(8,128)S(1)} %left_gram.1.left_raw_ref, f32[320,320]{1,0:T(8,128)S(1)} %get-tuple-element.64.gl_ref, ...), custom_call_target="tpu_custom_call" | custom-call | flops 24999999488 | bytes 4000000 | tf_op jit(solution)/shard_map/refresh/pallas_call | solution.py:175
  171.9 2.9 %collective-permute-start.13 = (f32[320,256]{1,0:T(8,128)S(1)}, f32[320,256]{1,0:T(8,128)S(1)}, u32[]{:S(2)}, u32[]{:S(2)}) collective-permute-start(f32[320,256]{1,0:T(8,128)S(1)} %get-tuple-element.53.refs_0_), channel_id=1, source_target_pairs={{0,256},{128,384},{256,0},{384,128},{1,257},{129,385},{257,1},{385... | collective-permute-start | bytes 983048 | tf_op jit(solution)/shard_map/ppermute | solution.py:352
  174.8 2.2 %collective-permute-start.14 = (f32[320,256]{1,0:T(8,128)S(1)}, f32[320,256]{1,0:T(8,128)S(1)}, u32[]{:S(2)}, u32[]{:S(2)}) collective-permute-start(f32[320,256]{1,0:T(8,128)S(1)} %get-tuple-element.53.refs_0_), channel_id=1, source_target_pairs={{0,128},{128,256},{256,384},{384,0},{1,129},{129,257},{257,385},{3... | collective-permute-start | bytes 983048 | tf_op jit(solution)/shard_map/ppermute | solution.py:352
  176.9 5.8 %collective-permute-start.15 = (f32[320,256]{1,0:T(8,128)S(1)}, f32[320,256]{1,0:T(8,128)S(1)}, u32[]{:S(2)}, u32[]{:S(2)}) collective-permute-start(f32[320,256]{1,0:T(8,128)S(1)} %get-tuple-element.53.refs_0_), channel_id=1, source_target_pairs={{0,384},{128,0},{256,128},{384,256},{1,385},{129,1},{257,129},{385... | collective-permute-start | bytes 983048 | tf_op jit(solution)/shard_map/ppermute | solution.py:352
  182.7 14.6 %collective-permute-done.16.raw_ref = f32[320,320]{1,0:T(8,128)} collective-permute-done((f32[320,320]{1,0:T(8,128)S(1)}, f32[320,320]{1,0:T(8,128)}, u32[]{:S(2)}, u32[]{:S(2)}) %collective-permute-start.16) | collective-permute-done | bytes 409632 | tf_op jit(solution)/shard_map/ppermute | solution.py:345
  197.3 16.5 %refresh_held.1 = (f32[320,320]{1,0:T(8,128)}, f32[320,320]{1,0:T(8,128)}) custom-call(f32[8,128]{1,0:T(8,128)S(1)} %get-tuple-element.50.factor_ref, f32[320,320]{1,0:T(8,128)} %collective-permute-done.16.raw_ref, f32[320,320]{1,0:T(8,128)S(1)} %bitcast.21, f32[320,320]{1,0:T(8,128)S(1)} %bitcast.22), custom_call_target="tpu_custom_call" | custom-call | flops 17999998976 | bytes 2000000 | tf_op jit(solution)/shard_map/refresh_held/pallas_call | solution.py:204
  213.8 0.9 place.1
  (39 shorter events, 0.4 us)
Async XLA Ops:
  2.9 16.1 %copy-start = (f32[1,320,320]{2,1,0:T(8,128)S(1)}, f32[1,320,320]{2,1,0:T(8,128)}, u32[]{:S(2)}) copy-start(f32[1,320,320]{2,1,0:T(8,128)} %param.8) | copy-start | bytes 1228804
  2.9 16.9 %copy-start.1 = (f32[1,320,320]{2,1,0:T(8,128)S(1)}, f32[1,320,320]{2,1,0:T(8,128)}, u32[]{:S(2)}) copy-start(f32[1,320,320]{2,1,0:T(8,128)} %param.10) | copy-start | bytes 1228804
  2.9 51.5 %all-to-all-start = ((f32[32,40,256]{2,1,0:T(8,128)}), f32[32,40,256]{2,1,0:T(8,128)S(1)}, u32[]{:S(2)}, u32[]{:S(2)}) async-start(f32[32,40,256]{2,1,0:T(8,128)} %convert.1), calls=%async_computation | async-start | bytes 2621440 | tf_op jit(solution)/shard_map/all_to_all | solution.py:322
  19.0 6.2 %copy-start.11 = (f32[40,256]{1,0:T(8,128)S(1)}, f32[40,256]{1,0:T(8,128)}, u32[]{:S(2)}) copy-start(f32[40,256]{1,0:T(8,128)} %param.12) | copy-start | bytes 122884
  19.0 6.2 %copy-start.12 = (f32[40,256]{1,0:T(8,128)S(1)}, f32[40,256]{1,0:T(8,128)}, u32[]{:S(2)}) copy-start(f32[40,256]{1,0:T(8,128)} %param.13) | copy-start | bytes 122884
  20.7 14.7 %collective-permute-start = (f32[2,320,320]{2,1,0:T(8,128)}, f32[2,320,320]{2,1,0:T(8,128)}, u32[]{:S(2)}, u32[]{:S(2)}) collective-permute-start(f32[2,320,320]{2,1,0:T(8,128)} %constant_dynamic-update-slice_fusion), channel_id=1, source_target_pairs={{0,1},{129,130},{258,259},{387,384},{4,5},{133,134},{262,263},{391... | collective-permute-start | bytes 2457608 | tf_op jit(solution)/shard_map/ppermute | solution.py:317
  22.3 18.5 %collective-permute-start.1 = (f32[2,320,320]{2,1,0:T(8,128)}, f32[2,320,320]{2,1,0:T(8,128)}, u32[]{:S(2)}, u32[]{:S(2)}) collective-permute-start(f32[2,320,320]{2,1,0:T(8,128)} %constant_dynamic-update-slice_fusion), channel_id=1, source_target_pairs={{0,2},{129,131},{258,256},{387,385},{4,6},{133,135},{262,260},{391... | collective-permute-start | bytes 2457608 | tf_op jit(solution)/shard_map/ppermute | solution.py:317
  23.9 27.5 %collective-permute-start.2 = (f32[2,320,320]{2,1,0:T(8,128)}, f32[2,320,320]{2,1,0:T(8,128)}, u32[]{:S(2)}, u32[]{:S(2)}) collective-permute-start(f32[2,320,320]{2,1,0:T(8,128)} %constant_dynamic-update-slice_fusion), channel_id=1, source_target_pairs={{0,3},{129,128},{258,257},{387,386},{4,7},{133,132},{262,261},{391... | collective-permute-start | bytes 2457608 | tf_op jit(solution)/shard_map/ppermute | solution.py:317
  25.3 31.1 %collective-permute-start.3 = (f32[80,256]{1,0:T(8,128)S(1)}, f32[80,256]{1,0:T(8,128)S(1)}, u32[]{:S(2)}, u32[]{:S(2)}) collective-permute-start(f32[80,256]{1,0:T(8,128)S(1)} %constant_dynamic-update-slice_fusion.2), channel_id=1, source_target_pairs={{0,16},{16,32},{32,48},{48,0},{1,17},{17,33},{33,49},{49,1},{2,18}... | collective-permute-start | bytes 245768 | tf_op jit(solution)/shard_map/ppermute | solution.py:312
  29.9 30.5 %collective-permute-start.4 = (f32[80,256]{1,0:T(8,128)S(1)}, f32[80,256]{1,0:T(8,128)S(1)}, u32[]{:S(2)}, u32[]{:S(2)}) collective-permute-start(f32[80,256]{1,0:T(8,128)S(1)} %constant_dynamic-update-slice_fusion.2), channel_id=1, source_target_pairs={{0,32},{16,48},{32,0},{48,16},{1,33},{17,49},{33,1},{49,17},{2,34}... | collective-permute-start | bytes 245768 | tf_op jit(solution)/shard_map/ppermute | solution.py:312
  35.4 25.0 %collective-permute-start.5 = (f32[80,256]{1,0:T(8,128)S(1)}, f32[80,256]{1,0:T(8,128)S(1)}, u32[]{:S(2)}, u32[]{:S(2)}) collective-permute-start(f32[80,256]{1,0:T(8,128)S(1)} %constant_dynamic-update-slice_fusion.2), channel_id=1, source_target_pairs={{0,48},{16,0},{32,16},{48,32},{1,49},{17,1},{33,17},{49,33},{2,50}... | collective-permute-start | bytes 245768 | tf_op jit(solution)/shard_map/ppermute | solution.py:312
  60.4 17.5 %all-to-all-start.1 = ((f32[8,40,256]{2,1,0:T(8,128)}), f32[8,40,256]{2,1,0:T(8,128)S(1)}, u32[]{:S(2)}, u32[]{:S(2)}) async-start(f32[8,40,256]{2,1,0:T(8,128)} %own_sum.1), calls=%async_computation.1 | async-start | bytes 655360 | tf_op jit(solution)/shard_map/all_to_all | solution.py:326
  63.9 13.3 %collective-permute-start.6 = (f32[320,256]{1,0:T(8,128)S(1)}, f32[320,256]{1,0:T(8,128)S(1)}, u32[]{:S(2)}, u32[]{:S(2)}) collective-permute-start(f32[320,256]{1,0:T(8,128)S(1)} %constant_dynamic-update-slice_fusion.4.mine_ref), channel_id=1, source_target_pairs={{0,64},{64,0},{1,65},{65,1},{2,66},{66,2},{3,67},{67,3},{4,68},{68... | collective-permute-start | bytes 983048 | tf_op jit(solution)/shard_map/ppermute | solution.py:328
  77.2 0.7 copy-start.2
  79.3 29.1 %all-to-all-start.2 = ((f32[16,16,256]{2,1,0:T(8,128)}), f32[16,16,256]{2,1,0:T(8,128)S(1)}, u32[]{:S(2)}, u32[]{:S(2)}) async-start(f32[16,16,256]{2,1,0:T(8,128)} %bitcast.8), calls=%async_computation.2 | async-start | bytes 524288 | tf_op jit(solution)/shard_map/all_to_all | solution.py:333
  97.9 29.4 %collective-permute-start.7 = (f32[320,256]{1,0:T(8,128)S(1)}, f32[320,256]{1,0:T(8,128)S(1)}, u32[]{:S(2)}, u32[]{:S(2)}) collective-permute-start(f32[320,256]{1,0:T(8,128)S(1)} %bitcast.24), channel_id=1, source_target_pairs={{0,1},{1,2},{2,3},{3,0},{4,5},{5,6},{6,7},{7,4},{8,9},{9,10},{10,1... | collective-permute-start | bytes 983048 | tf_op jit(solution)/shard_map/ppermute | solution.py:334
  103.4 26.5 %collective-permute-start.8 = (f32[320,256]{1,0:T(8,128)S(1)}, f32[320,256]{1,0:T(8,128)S(1)}, u32[]{:S(2)}, u32[]{:S(2)}) collective-permute-start(f32[320,256]{1,0:T(8,128)S(1)} %bitcast.25), channel_id=1, source_target_pairs={{0,2},{1,3},{2,0},{3,1},{4,6},{5,7},{6,4},{7,5},{8,10},{9,11},{10,... | collective-permute-start | bytes 983048 | tf_op jit(solution)/shard_map/ppermute | solution.py:334
  106.1 24.7 %collective-permute-start.9 = (f32[320,256]{1,0:T(8,128)S(1)}, f32[320,256]{1,0:T(8,128)}, u32[]{:S(2)}, u32[]{:S(2)}) collective-permute-start(f32[320,256]{1,0:T(8,128)S(1)} %bitcast.26), channel_id=1, source_target_pairs={{0,3},{1,0},{2,1},{3,2},{4,7},{5,4},{6,5},{7,6},{8,11},{9,8},{10,9... | collective-permute-start | bytes 983048 | tf_op jit(solution)/shard_map/ppermute | solution.py:334
  109.1 35.6 %all-to-all-start.3 = ((f32[16,16,256]{2,1,0:T(8,128)}), f32[16,16,256]{2,1,0:T(8,128)S(1)}, u32[]{:S(2)}, u32[]{:S(2)}) async-start(f32[16,16,256]{2,1,0:T(8,128)} %get-tuple-element.45), calls=%async_computation.3 | async-start | bytes 524288 | tf_op jit(solution)/shard_map/all_to_all | solution.py:339
  118.8 25.9 %collective-permute-start.10 = (f32[8,128]{1,0:T(8,128)S(1)}, f32[8,128]{1,0:T(8,128)S(1)}, u32[]{:S(2)}, u32[]{:S(2)}) collective-permute-start(f32[8,128]{1,0:T(8,128)S(1)} %get-tuple-element.46.sq0_ref), channel_id=1, source_target_pairs={{0,1},{1,2},{2,3},{3,0},{4,5},{5,6},{6,7},{7,4},{8,9},{9,10},{10,1... | collective-permute-start | bytes 12296 | tf_op jit(solution)/shard_map/ppermute | solution.py:341
  123.8 20.9 %collective-permute-start.11 = (f32[8,128]{1,0:T(8,128)S(1)}, f32[8,128]{1,0:T(8,128)S(1)}, u32[]{:S(2)}, u32[]{:S(2)}) collective-permute-start(f32[8,128]{1,0:T(8,128)S(1)} %get-tuple-element.46.sq0_ref), channel_id=1, source_target_pairs={{0,2},{1,3},{2,0},{3,1},{4,6},{5,7},{6,4},{7,5},{8,10},{9,11},{10,... | collective-permute-start | bytes 12296 | tf_op jit(solution)/shard_map/ppermute | solution.py:341
  127.3 0.7 copy-start.4
  128.1 16.6 %collective-permute-start.12 = (f32[8,128]{1,0:T(8,128)S(1)}, f32[8,128]{1,0:T(8,128)S(1)}, u32[]{:S(2)}, u32[]{:S(2)}) collective-permute-start(f32[8,128]{1,0:T(8,128)S(1)} %get-tuple-element.46.sq0_ref), channel_id=1, source_target_pairs={{0,3},{1,0},{2,1},{3,2},{4,7},{5,4},{6,5},{7,6},{8,11},{9,8},{10,9... | collective-permute-start | bytes 12296 | tf_op jit(solution)/shard_map/ppermute | solution.py:341
  130.0 0.7 copy-start.6
  130.7 1.0 copy-start.5
  131.7 1.0 copy-start.7
  135.9 61.5 %collective-permute-start.16 = (f32[320,320]{1,0:T(8,128)S(1)}, f32[320,320]{1,0:T(8,128)}, u32[]{:S(2)}, u32[]{:S(2)}) collective-permute-start(f32[320,320]{1,0:T(8,128)S(1)} %left_gram.1.left_raw_ref), channel_id=1, source_target_pairs={{0,0},{1,128},{2,256},{3,384},{128,1},{129,129},{130,257},{131,385... | collective-permute-start | bytes 1228808 | tf_op jit(solution)/shard_map/ppermute | solution.py:345
  144.7 1.0 copy-start.3
  145.7 0.9 copy-start.8
  146.6 0.9 copy-start.9
  147.6 0.7 copy-start.10
  171.9 41.9 %collective-permute-start.13 = (f32[320,256]{1,0:T(8,128)S(1)}, f32[320,256]{1,0:T(8,128)S(1)}, u32[]{:S(2)}, u32[]{:S(2)}) collective-permute-start(f32[320,256]{1,0:T(8,128)S(1)} %get-tuple-element.53.refs_0_), channel_id=1, source_target_pairs={{0,256},{128,384},{256,0},{384,128},{1,257},{129,385},{257,1},{385... | collective-permute-start | bytes 983048 | tf_op jit(solution)/shard_map/ppermute | solution.py:352
  174.8 39.0 %collective-permute-start.14 = (f32[320,256]{1,0:T(8,128)S(1)}, f32[320,256]{1,0:T(8,128)S(1)}, u32[]{:S(2)}, u32[]{:S(2)}) collective-permute-start(f32[320,256]{1,0:T(8,128)S(1)} %get-tuple-element.53.refs_0_), channel_id=1, source_target_pairs={{0,128},{128,256},{256,384},{384,0},{1,129},{129,257},{257,385},{3... | collective-permute-start | bytes 983048 | tf_op jit(solution)/shard_map/ppermute | solution.py:352
  176.9 36.9 %collective-permute-start.15 = (f32[320,256]{1,0:T(8,128)S(1)}, f32[320,256]{1,0:T(8,128)S(1)}, u32[]{:S(2)}, u32[]{:S(2)}) collective-permute-start(f32[320,256]{1,0:T(8,128)S(1)} %get-tuple-element.53.refs_0_), channel_id=1, source_target_pairs={{0,384},{128,0},{256,128},{384,256},{1,385},{129,1},{257,129},{385... | collective-permute-start | bytes 983048 | tf_op jit(solution)/shard_map/ppermute | solution.py:352

commit v5 on v4

--- a/solution.py
+++ b/solution.py
@@ -121,12 +121,12 @@
 
 
 def refresh_kernel(
-    place_ref, left_raw_ref, gl_ref, bl_ref, right_raw_ref, gr_ref, br_ref, tile_ref, sq0_ref, sq1_ref,
+    member_ref, left_raw_ref, moved_ref, right_raw_ref, gr_ref, br_ref, tile_ref, sq0_ref, sq1_ref,
     sq2_ref, sq3_ref, mine_ref, other_ref,
     gr_out_ref, qr_out_ref, m_ref, v_ref, u_ref, factor_ref,
     sl_ref, pl_ref, qlt_ref, sr_ref, pr_ref, qrt_ref, ms_ref, vs_ref,
 ):
-    y2, zh = place_ref[0], place_ref[1]
+    y2, zh = member_ref[0] // 4, lax.rem(member_ref[0], 4)
     for src_ref, pair in ((mine_ref, y2), (other_ref, 1 - y2)):
         for n, shift in enumerate((0, -1, -2, -3)):
             at = pl.multiple_of(40 * (4 * pair + lax.rem(zh + shift + 4, 4)), 8)
@@ -141,10 +141,10 @@
     weight = (1.0 - beta_gram) * factor * factor
     right_new = beta_gram * gr_ref[...] + weight * right_raw
     gr_out_ref[...] = right_new
-    left_new = beta_gram * gl_ref[...] + weight * left_raw_ref[...]
+    left_new = beta_gram * moved_ref[0] + weight * left_raw_ref[...]
     factorize(
         [
-            (left_new, bl_ref[...], sl_ref, pl_ref, qlt_ref),
+            (left_new, moved_ref[1], sl_ref, pl_ref, qlt_ref),
             (right_new, br_ref[...], sr_ref, pr_ref, qrt_ref),
         ]
     )
@@ -170,7 +170,7 @@
     return pl.BlockSpec(memory_space=pltpu.VMEM)
 
 
-def refresh(spot, left_raw, gl, bl, right_raw, gr, br, tile, squares, mine, other):
+def refresh(member, left_raw, moved, right_raw, gr, br, tile, squares, mine, other):
     f32 = jnp.float32
     return pl.pallas_call(
         refresh_kernel,
@@ -178,17 +178,17 @@
             shape_of(RB, RB), shape_of(RB, RB), shape_of(40, RB), shape_of(40, RB),
             shape_of(LB, RB), shape_of(8, 128),
         ),
-        in_specs=[pl.BlockSpec(memory_space=pltpu.SMEM)] + [whole()] * 4 + [pl.BlockSpec()] * 2 + [whole()] * 7,
+        in_specs=[pl.BlockSpec(memory_space=pltpu.SMEM)] + [whole()] * 12,
         out_specs=(whole(),) * 6,
         scratch_shapes=[pltpu.VMEM((LB, LB), f32)] * 3
         + [pltpu.VMEM((RB, RB), f32)] * 3
         + [pltpu.VMEM((LB, RB), f32)] * 2,
-        compiler_params=pltpu.CompilerParams(vmem_limit_bytes=24 * 2**20),
+        compiler_params=pltpu.CompilerParams(vmem_limit_bytes=12 * 2**20),
         cost_estimate=pl.CostEstimate(
             flops=25_000_000_000, bytes_accessed=4_000_000, transcendentals=0
         ),
         name="refresh",
-    )(spot, left_raw, gl, bl, right_raw, gr, br, tile, *squares, mine, other)
+    )(member, left_raw, moved, right_raw, gr, br, tile, *squares, mine, other)
 
 
 def held_kernel(factor_ref, raw_ref, g_ref, b_ref, g_out_ref, q_out_ref, s_ref, p_ref, qt_ref):
@@ -204,10 +204,10 @@
     return pl.pallas_call(
         held_kernel,
         out_shape=(shape_of(LB, LB), shape_of(LB, LB)),
-        in_specs=[whole()] * 2 + [pl.BlockSpec()] * 2,
+        in_specs=[whole()] * 4,
         out_specs=(whole(),) * 2,
         scratch_shapes=[pltpu.VMEM((LB, LB), f32)] * 3,
-        compiler_params=pltpu.CompilerParams(vmem_limit_bytes=24 * 2**20),
+        compiler_params=pltpu.CompilerParams(vmem_limit_bytes=12 * 2**20),
         cost_estimate=pl.CostEstimate(
             flops=18_000_000_000, bytes_accessed=2_000_000, transcendentals=0
         ),
@@ -256,41 +256,36 @@
         out_shape=out_shape,
         in_specs=specs,
         out_specs=jax.tree.map(lambda _: whole(), out_shape),
-        compiler_params=pltpu.CompilerParams(vmem_limit_bytes=16 * 2**20),
+        compiler_params=pltpu.CompilerParams(vmem_limit_bytes=6 * 2**20),
         cost_estimate=pl.CostEstimate(flops=flops, bytes_accessed=1_000_000, transcendentals=0),
         name=name,
     )(*operands)
 
 
-PLACES = (0, -2, -1, -3)
-
-
-def place_kernel(k_ref, *refs):
-    parts, out_ref, rounded_ref, sems = refs[:-3], refs[-3], refs[-2], refs[-1]
+def place_kernel(blocks_ref, out_ref, rounded_ref, sems):
     copies = []
-    for n, shift in enumerate(PLACES):
-        source = lax.rem(k_ref[0] + shift + 4, 4)
-        at = pl.ds(pl.multiple_of(source * LB, 16), LB)
-        rounded_ref[at, :] = parts[n][...].astype(jnp.bfloat16)
+    for n in range(4):
+        rounded_ref[n * LB : (n + 1) * LB, :] = blocks_ref[n].astype(jnp.bfloat16)
+        at = pl.ds(n * LB, LB)
         copies.append(pltpu.make_async_copy(rounded_ref.at[at], out_ref.at[at], sems.at[n]))
         copies[-1].start()
     for copy in copies:
         copy.wait()
 
 
-def place(k, parts):
+def place(blocks):
     return pl.pallas_call(
         place_kernel,
         out_shape=jax.ShapeDtypeStruct((4 * LB, RB), jnp.bfloat16),
-        in_specs=[pl.BlockSpec(memory_space=pltpu.SMEM)] + [whole()] * len(parts),
+        in_specs=[whole()],
         out_specs=pl.BlockSpec(memory_space=pl.ANY),
         scratch_shapes=[
             pltpu.VMEM((4 * LB, RB), jnp.bfloat16),
-            pltpu.SemaphoreType.DMA((len(PLACES),)),
+            pltpu.SemaphoreType.DMA((4,)),
         ],
-        compiler_params=pltpu.CompilerParams(vmem_limit_bytes=16 * 2**20),
+        compiler_params=pltpu.CompilerParams(vmem_limit_bytes=6 * 2**20),
         name="place",
-    )(k, *parts)
+    )(blocks)
 
 
 def gather_all(x, axes, count):
@@ -320,13 +315,12 @@
 
     pieces = pseudo_grads[0].astype(jnp.float32).reshape(32, 40, RB)
     arrived = lax.all_to_all(pieces, REP, 0, 0, tiled=True)
-    arrived, moved = lax.optimization_barrier((arrived, moved))
     copies = small(own_sum_kernel, "own_sum", shape_of(8, 40, RB), 10**8, arrived)
     copies, *column = lax.optimization_barrier((copies, *column))
     tile = lax.all_to_all(copies, MEMBERS, 0, 0, tiled=True).reshape(LB, RB)
     mine = jnp.concatenate(column, axis=0)
     other = lax.ppermute(mine, "y2", shift_perm(2, 1))
-    tile, mine, other = lax.optimization_barrier((tile, mine, other))
+    tile, mine, other, moved = lax.optimization_barrier((tile, mine, other, moved))
 
     right_part = small(right_part_kernel, "right_part", shape_of(RB, RB), 10**9, tile)
     sent, right_part = lax.optimization_barrier((tile, right_part))
@@ -341,20 +335,22 @@
         lax.ppermute(squares_own, "x", shift_perm(4, by)) for by in range(1, 4)
     ]
     left_raw = small(left_gram_kernel, "left_gram", shape_of(LB, LB), 2 * 10**9, *tiles)
-    swap = [(a * 4 + b, b * 4 + a) for a in range(4) for b in range(4)]
-    held_raw = lax.ppermute(left_raw, ("yk", "x"), swap)
+    along_y = [(j * 4 + c, (c - j) % 4 * 4 + c) for j in range(4) for c in range(4)]
+    along_x = [(g * 4 + c, g * 4 + (c - g) % 4) for g in range(4) for c in range(4)]
+    passed = lax.ppermute(left_raw, ("yk", "x"), along_y)
 
     right_new, right_basis_new, moment, second, turned, factor = refresh(
-        jnp.stack([lax.axis_index("y2"), lax.axis_index("zh")]).astype(jnp.int32), left_raw,
-        moved[0], moved[1], right_raw, right_gram[0], right_basis[0], tile, squares, mine, other,
-    )
-
-    blocks = [turned] + [lax.ppermute(turned, "yk", shift_perm(4, by)) for by in (2, 1, 3)]
+        lax.axis_index(MEMBERS).astype(jnp.int32).reshape(1), left_raw, moved, right_raw,
+        right_gram[0], right_basis[0], tile, squares, mine, other,
+    )
+
+    held_raw = lax.ppermute(passed, ("yk", "x"), along_x)
+    blocks = gather_all(turned, "yk", 4)
     left_new, left_basis_new = refresh_held(factor, held_raw, left_gram[0], left_basis[0])
-    *blocks, left_new, left_basis_new = lax.optimization_barrier(
-        (*blocks, left_new, left_basis_new)
-    )
-    update = place(k.astype(jnp.int32).reshape(1), blocks)
+    blocks, left_new, left_basis_new = lax.optimization_barrier(
+        (blocks, left_new, left_basis_new)
+    )
+    update = place(blocks)
     return (
         update, left_new[None], left_basis_new[None], right_new[None], right_basis_new[None],
         moment, second,

time: 219 us -> 220 us (level)
  waiting for transfers between devices: 40.1 us -> 58.5 us
  starting transfers between devices: 110 us -> 96.7 us
    ppermute x3, waiting for transfers between devices: 5.19 us -> 25 us  [shards(): lax.ppermute(ours, 'zh', shift_perm(4, by))]
    all_to_all x0 -> x1, waiting for transfers between devices: none -> 15.2 us  [gather_all(): return lax.all_to_all(copies, axes, 0, 0, tiled=True)]
    all_to_all x1, starting transfers between devices: 18.6 us -> 5.32 us  [shards(): lax.all_to_all(right_part.reshape(16, 16, RB), RIGHT_GROUP, 0, 0, tiled=T...]
    ppermute x3, waiting for transfers between devices: 10.6 us -> 0.01 us  [shards(): lax.ppermute(held, ('yk', 'x'), [(b * 4 + b, b * 4 + (b + by) % 4) for b...]
    ppermute x4 -> x2, starting transfers between devices: 19.6 us -> 10.9 us  [the longest x1 5.66 us: shards(): passed = lax.ppermute(left_raw, ('yk', 'x'), along_y)]
    ppermute x4 -> x2, waiting for transfers between devices: 14.6 us -> 8.34 us  [the longest x1 8.34 us: shards(): passed = lax.ppermute(left_raw, ('yk', 'x'), along_y)]
    all_to_all x0 -> x1, starting transfers between devices: none -> 5.94 us  [gather_all(): return lax.all_to_all(copies, axes, 0, 0, tiled=True)]
    all_to_all x1, starting transfers between devices: 3.45 us -> 6.64 us  [shards(): tile = lax.all_to_all(copies, MEMBERS, 0, 0, tiled=True).reshape(LB, RB)]
  transfers between devices with their start and end apart: 21 -> 20, of which waited for: 6 -> 8; matrix products, arithmetic and copies ran while one was open for 3% -> 2% of each run, Pallas kernels for 21% -> 20%
where the time goes in v5:
time: 220 us; the launch traced here: 217 us
  starting transfers between devices  96.7 us (44%)
  waiting for transfers between devices  58.5 us (27%)
  Pallas kernels  46.6 us (21%)
  local copies, waits for them, and re-layouts  9.88 us (4%)
  other arithmetic  4.25 us (2%)
    ppermute x3, waiting for transfers between devices, shards(): lax.ppermute(ours, 'zh', shift_perm(4, by))  25 us
    pallas_call x1, Pallas kernels, refresh(): pl.pallas_call(refresh_kernel, out_shape=(shape_of(RB, RB), shape_of(RB,...  23.1 us
    pallas_call x1, Pallas kernels, refresh_held(): pl.pallas_call(held_kernel, out_shape=(shape_of(LB, LB), shape_of(LB, LB)...  16.5 us
    all_to_all x1, starting transfers between devices, shards(): arrived = lax.all_to_all(pieces, REP, 0, 0, tiled=True)  16.1 us
    all_to_all x1, waiting for transfers between devices, gather_all(): return lax.all_to_all(copies, axes, 0, 0, tiled=True)  15.2 us
    ppermute x3, starting transfers between devices, shards(): lax.ppermute(ours, 'zh', shift_perm(4, by))  14.9 us
    ppermute x3, starting transfers between devices, shards(): lax.ppermute(squares_own, 'x', shift_perm(4, by))  11.5 us
    ppermute x3, starting transfers between devices, shards(): lax.ppermute(sent, 'x', shift_perm(4, by))  10.1 us
  transfers between devices with their start and end apart: 20, of which 8 were waited for; matrix products, arithmetic and copies ran while one was open for 2% of the time, Pallas kernels for 20%

profile of v5, /device:TPU:6, one launch (start us, length us, event | category | flops | bytes accessed | tf_op | source)
XLA Modules:
  0.0 217.0 jit_solution(7425415322654296616)
XLA Ops:
  0.6 2.3 %convert.1 = f32[32,40,256]{2,1,0:T(8,128)} convert(bf16[32,40,256]{2,1,0:T(8,128)(2,1)} %bitcast.26) | non-fusion elementwise | flops 327680 | bytes 1966080 | tf_op jit(solution)/shard_map/convert_element_type | solution.py:316
  2.9 16.1 %all-to-all-start = ((f32[32,40,256]{2,1,0:T(8,128)}), f32[32,40,256]{2,1,0:T(8,128)S(1)}, u32[]{:S(2)}, u32[]{:S(2)}) async-start(f32[32,40,256]{2,1,0:T(8,128)} %convert.1), calls=%async_computation | async-start | bytes 2621440 | tf_op jit(solution)/shard_map/all_to_all | solution.py:317
  19.0 0.8 constant_dynamic-update-slice_fusion.7
  19.8 0.8 constant_dynamic-update-slice_fusion.6
  20.7 1.3 collective-permute-start.6
  22.0 1.6 collective-permute-start.5
  23.6 1.6 collective-permute-start.4
  25.2 5.8 %collective-permute-start.2 = (f32[80,256]{1,0:T(8,128)S(1)}, f32[80,256]{1,0:T(8,128)S(1)}, u32[]{:S(2)}, u32[]{:S(2)}) collective-permute-start(f32[80,256]{1,0:T(8,128)S(1)} %constant_dynamic-update-slice_fusion), channel_id=1, source_target_pairs={{0,48},{16,0},{32,16},{48,32},{1,49},{17,1},{33,17},{49,33},{2,50}... | collective-permute-start | bytes 245768 | tf_op jit(solution)/shard_map/ppermute | solution.py:307
  31.1 4.3 %collective-permute-start.1 = (f32[80,256]{1,0:T(8,128)S(1)}, f32[80,256]{1,0:T(8,128)S(1)}, u32[]{:S(2)}, u32[]{:S(2)}) collective-permute-start(f32[80,256]{1,0:T(8,128)S(1)} %constant_dynamic-update-slice_fusion), channel_id=1, source_target_pairs={{0,32},{16,48},{32,0},{48,16},{1,33},{17,49},{33,1},{49,17},{2,34}... | collective-permute-start | bytes 245768 | tf_op jit(solution)/shard_map/ppermute | solution.py:307
  35.3 21.5 %collective-permute-done.2 = f32[80,256]{1,0:T(8,128)S(1)} collective-permute-done((f32[80,256]{1,0:T(8,128)S(1)}, f32[80,256]{1,0:T(8,128)S(1)}, u32[]{:S(2)}, u32[]{:S(2)}) %collective-permute-start.2) | collective-permute-done | bytes 81952 | tf_op jit(solution)/shard_map/ppermute | solution.py:307
  56.8 4.8 %collective-permute-start = (f32[80,256]{1,0:T(8,128)S(1)}, f32[80,256]{1,0:T(8,128)S(1)}, u32[]{:S(2)}, u32[]{:S(2)}) collective-permute-start(f32[80,256]{1,0:T(8,128)S(1)} %constant_dynamic-update-slice_fusion), channel_id=1, source_target_pairs={{0,16},{16,32},{32,48},{48,0},{1,17},{17,33},{33,49},{49,1},{2,18}... | collective-permute-start | bytes 245768 | tf_op jit(solution)/shard_map/ppermute | solution.py:307
  61.7 0.8 own_sum.1
  62.5 3.5 %collective-permute-done = f32[80,256]{1,0:T(8,128)S(1)} collective-permute-done((f32[80,256]{1,0:T(8,128)S(1)}, f32[80,256]{1,0:T(8,128)S(1)}, u32[]{:S(2)}, u32[]{:S(2)}) %collective-permute-start) | collective-permute-done | bytes 81952 | tf_op jit(solution)/shard_map/ppermute | solution.py:307
  66.0 6.6 %all-to-all-start.1 = ((f32[8,40,256]{2,1,0:T(8,128)}), f32[8,40,256]{2,1,0:T(8,128)S(1)}, u32[]{:S(2)}, u32[]{:S(2)}) async-start(f32[8,40,256]{2,1,0:T(8,128)} %own_sum.1), calls=%async_computation.1 | async-start | bytes 655360 | tf_op jit(solution)/shard_map/all_to_all | solution.py:320
  72.7 3.9 %collective-permute-start.3 = (f32[320,256]{1,0:T(8,128)S(1)}, f32[320,256]{1,0:T(8,128)S(1)}, u32[]{:S(2)}, u32[]{:S(2)}) collective-permute-start(f32[320,256]{1,0:T(8,128)S(1)} %constant_dynamic-update-slice_fusion.2.mine_ref), channel_id=1, source_target_pairs={{0,64},{64,0},{1,65},{65,1},{2,66},{66,2},{3,67},{67,3},{4,68},{68... | collective-permute-start | bytes 983048 | tf_op jit(solution)/shard_map/ppermute | solution.py:322
  76.7 2.0 add_add_fusion.moved_ref
  78.7 6.3 %collective-permute-done.3.other_ref = f32[320,256]{1,0:T(8,128)S(1)} collective-permute-done((f32[320,256]{1,0:T(8,128)S(1)}, f32[320,256]{1,0:T(8,128)S(1)}, u32[]{:S(2)}, u32[]{:S(2)}) %collective-permute-start.3) | collective-permute-done | bytes 327712 | tf_op jit(solution)/shard_map/ppermute | solution.py:322
  85.0 0.7 copy-done.2
  85.7 1.3 right_part.1
  87.1 5.3 %all-to-all-start.2 = ((f32[16,16,256]{2,1,0:T(8,128)}), f32[16,16,256]{2,1,0:T(8,128)S(1)}, u32[]{:S(2)}, u32[]{:S(2)}) async-start(f32[16,16,256]{2,1,0:T(8,128)} %bitcast.4), calls=%async_computation.2 | async-start | bytes 524288 | tf_op jit(solution)/shard_map/all_to_all | solution.py:327
  92.4 3.5 %collective-permute-start.9 = (f32[320,256]{1,0:T(8,128)S(1)}, f32[320,256]{1,0:T(8,128)S(1)}, u32[]{:S(2)}, u32[]{:S(2)}) collective-permute-start(f32[320,256]{1,0:T(8,128)S(1)} %bitcast.18), channel_id=1, source_target_pairs={{0,3},{1,0},{2,1},{3,2},{4,7},{5,4},{6,5},{7,6},{8,11},{9,8},{10,9... | collective-permute-start | bytes 983048 | tf_op jit(solution)/shard_map/ppermute | solution.py:328
  95.9 2.2 %collective-permute-start.8 = (f32[320,256]{1,0:T(8,128)S(1)}, f32[320,256]{1,0:T(8,128)S(1)}, u32[]{:S(2)}, u32[]{:S(2)}) collective-permute-start(f32[320,256]{1,0:T(8,128)S(1)} %bitcast.19), channel_id=1, source_target_pairs={{0,2},{1,3},{2,0},{3,1},{4,6},{5,7},{6,4},{7,5},{8,10},{9,11},{10,... | collective-permute-start | bytes 983048 | tf_op jit(solution)/shard_map/ppermute | solution.py:328
  98.1 4.3 %collective-permute-start.7 = (f32[320,256]{1,0:T(8,128)S(1)}, f32[320,256]{1,0:T(8,128)}, u32[]{:S(2)}, u32[]{:S(2)}) collective-permute-start(f32[320,256]{1,0:T(8,128)S(1)} %bitcast.20), channel_id=1, source_target_pairs={{0,1},{1,2},{2,3},{3,0},{4,5},{5,6},{6,7},{7,4},{8,9},{9,10},{10,1... | collective-permute-start | bytes 983048 | tf_op jit(solution)/shard_map/ppermute | solution.py:328
  102.5 1.3 all-to-all-done.2.parts_ref
  103.7 0.7 right_sum.1
  104.5 6.8 %all-to-all-start.3 = ((f32[16,16,256]{2,1,0:T(8,128)}), f32[16,16,256]{2,1,0:T(8,128)S(1)}, u32[]{:S(2)}, u32[]{:S(2)}) async-start(f32[16,16,256]{2,1,0:T(8,128)} %get-tuple-element.40), calls=%async_computation.3 | async-start | bytes 524288 | tf_op jit(solution)/shard_map/all_to_all | solution.py:333
  111.3 1.2 collective-permute-done.9.refs_3_
  112.6 0.7 copy-done.4
  113.3 0.7 copy-done.6
  114.0 1.2 collective-permute-done.7.refs_1_
  115.2 1.0 copy-done.5
  116.2 1.0 copy-done.7
  117.1 3.2 %left_gram.1.left_raw_ref = f32[320,320]{1,0:T(8,128)S(1)} custom-call(f32[320,256]{1,0:T(8,128)S(1)} %bitcast.21, f32[320,256]{1,0:T(8,128)} %collective-permute-done.7.refs_1_, f32[320,256]{1,0:T(8,128)S(1)} %copy-done.7, f32[320,256]{1,0:T(8,128)S(1)} %copy-done.5), custom_call_target="tpu_custom_call" | custom-call | flops 2000000000 | bytes 1000000 | tf_op jit(solution)/shard_map/left_gram/pallas_call | solution.py:254
  120.3 5.7 %collective-permute-start.13 = (f32[320,320]{1,0:T(8,128)S(1)}, f32[320,320]{1,0:T(8,128)}, u32[]{:S(2)}, u32[]{:S(2)}) collective-permute-start(f32[320,320]{1,0:T(8,128)S(1)} %left_gram.1.left_raw_ref), channel_id=1, source_target_pairs={{0,0},{1,129},{2,258},{3,387},{128,384},{129,1},{130,130},{131,259... | collective-permute-start | bytes 1228808 | tf_op jit(solution)/shard_map/ppermute | solution.py:340
  126.0 5.0 %collective-permute-start.12 = (f32[8,128]{1,0:T(8,128)S(1)}, f32[8,128]{1,0:T(8,128)S(1)}, u32[]{:S(2)}, u32[]{:S(2)}) collective-permute-start(f32[8,128]{1,0:T(8,128)S(1)} %get-tuple-element.41.sq0_ref), channel_id=1, source_target_pairs={{0,3},{1,0},{2,1},{3,2},{4,7},{5,4},{6,5},{7,6},{8,11},{9,8},{10,9... | collective-permute-start | bytes 12296 | tf_op jit(solution)/shard_map/ppermute | solution.py:335
  131.0 1.9 collective-permute-start.11
  133.0 4.6 %collective-permute-start.10 = (f32[8,128]{1,0:T(8,128)S(1)}, f32[8,128]{1,0:T(8,128)S(1)}, u32[]{:S(2)}, u32[]{:S(2)}) collective-permute-start(f32[8,128]{1,0:T(8,128)S(1)} %get-tuple-element.41.sq0_ref), channel_id=1, source_target_pairs={{0,1},{1,2},{2,3},{3,0},{4,5},{5,6},{6,7},{7,4},{8,9},{9,10},{10,1... | collective-permute-start | bytes 12296 | tf_op jit(solution)/shard_map/ppermute | solution.py:335
  137.6 8.3 %collective-permute-done.13 = f32[320,320]{1,0:T(8,128)} collective-permute-done((f32[320,320]{1,0:T(8,128)S(1)}, f32[320,320]{1,0:T(8,128)}, u32[]{:S(2)}, u32[]{:S(2)}) %collective-permute-start.13) | collective-permute-done | bytes 409632 | tf_op jit(solution)/shard_map/ppermute | solution.py:340
  145.9 5.3 %collective-permute-start.14 = (f32[320,320]{1,0:T(8,128)}, f32[320,320]{1,0:T(8,128)}, u32[]{:S(2)}, u32[]{:S(2)}) collective-permute-start(f32[320,320]{1,0:T(8,128)} %collective-permute-done.13), channel_id=1, source_target_pairs={{0,0},{1,1},{2,2},{3,3},{128,131},{129,128},{130,129},{131,130},{2... | collective-permute-start | bytes 1228808 | tf_op jit(solution)/shard_map/ppermute | solution.py:347
  151.2 1.0 copy-done.3
  152.2 0.9 copy-done.8
  153.1 0.9 copy-done.9
  154.1 23.1 %refresh.1 = (f32[256,256]{1,0:T(8,128)}, f32[256,256]{1,0:T(8,128)}, f32[40,256]{1,0:T(8,128)}, f32[40,256]{1,0:T(8,128)}, f32[320,256]{1,0:T(8,128)S(1)}, /*index=5*/f32[8,128]{1,0:T(8,128)S(1)}) custom-call(s32[1]{0:T(128)} %bitcast.member_ref, f32[320,320]{1,0:T(8,128)S(1)} %left_gram.1.left_raw_ref, f32[2,320,320]{2,1,0:T(8,128)S(1)} %add_add_fusion.moved_ref, ...), custom_call_target="tpu_custom_call" | custom-call | flops 24999999488 | bytes 4000000 | tf_op jit(solution)/shard_map/refresh/pallas_call | solution.py:175
  177.2 1.2 broadcast_in_dim.23
  178.4 5.9 %all-to-all-start.4 = ((f32[4,320,256]{2,1,0:T(8,128)}), f32[4,320,256]{2,1,0:T(8,128)S(1)}, u32[]{:S(2)}, u32[]{:S(2)}) async-start(f32[4,320,256]{2,1,0:T(8,128)} %broadcast_in_dim.23), calls=%async_computation.4 | async-start | bytes 2621440 | tf_op jit(solution)/shard_map/all_to_all | solution.py:293
  184.3 16.5 %refresh_held.1 = (f32[320,320]{1,0:T(8,128)}, f32[320,320]{1,0:T(8,128)}) custom-call(f32[8,128]{1,0:T(8,128)S(1)} %get-tuple-element.45.factor_ref, f32[320,320]{1,0:T(8,128)} %collective-permute-done.14.raw_ref, f32[320,320]{1,0:T(8,128)S(1)} %bitcast.15, f32[320,320]{1,0:T(8,128)S(1)} %bitcast.16), custom_call_target="tpu_custom_call" | custom-call | flops 17999998976 | bytes 2000000 | tf_op jit(solution)/shard_map/refresh_held/pallas_call | solution.py:204
  200.8 15.2 %all-to-all-done.4.blocks_ref = f32[4,320,256]{2,1,0:T(8,128)S(1)} async-done(((f32[4,320,256]{2,1,0:T(8,128)}), f32[4,320,256]{2,1,0:T(8,128)S(1)}, u32[]{:S(2)}, u32[]{:S(2)}) %all-to-all-start.4) | async-done | bytes 1310752 | tf_op jit(solution)/shard_map/all_to_all | solution.py:293
  216.0 0.9 place.1
  (34 shorter events, 0.1 us)
Async XLA Ops:
  2.9 16.1 %copy-start = (f32[1,320,320]{2,1,0:T(8,128)S(1)}, f32[1,320,320]{2,1,0:T(8,128)}, u32[]{:S(2)}) copy-start(f32[1,320,320]{2,1,0:T(8,128)} %param.8) | copy-start | bytes 1228804
  2.9 16.9 %copy-start.1 = (f32[1,320,320]{2,1,0:T(8,128)S(1)}, f32[1,320,320]{2,1,0:T(8,128)}, u32[]{:S(2)}) copy-start(f32[1,320,320]{2,1,0:T(8,128)} %param.10) | copy-start | bytes 1228804
  2.9 58.8 %all-to-all-start = ((f32[32,40,256]{2,1,0:T(8,128)}), f32[32,40,256]{2,1,0:T(8,128)S(1)}, u32[]{:S(2)}, u32[]{:S(2)}) async-start(f32[32,40,256]{2,1,0:T(8,128)} %convert.1), calls=%async_computation | async-start | bytes 2621440 | tf_op jit(solution)/shard_map/all_to_all | solution.py:317
  19.0 6.2 %copy-start.10 = (f32[40,256]{1,0:T(8,128)S(1)}, f32[40,256]{1,0:T(8,128)}, u32[]{:S(2)}) copy-start(f32[40,256]{1,0:T(8,128)} %param.12) | copy-start | bytes 122884
  19.0 6.2 %copy-start.11 = (f32[40,256]{1,0:T(8,128)S(1)}, f32[40,256]{1,0:T(8,128)}, u32[]{:S(2)}) copy-start(f32[40,256]{1,0:T(8,128)} %param.13) | copy-start | bytes 122884
  20.7 56.0 %collective-permute-start.6 = (f32[2,320,320]{2,1,0:T(8,128)}, f32[2,320,320]{2,1,0:T(8,128)}, u32[]{:S(2)}, u32[]{:S(2)}) collective-permute-start(f32[2,320,320]{2,1,0:T(8,128)} %constant_dynamic-update-slice_fusion.6), channel_id=1, source_target_pairs={{0,3},{129,128},{258,257},{387,386},{4,7},{133,132},{262,261},{391... | collective-permute-start | bytes 2457608 | tf_op jit(solution)/shard_map/ppermute | solution.py:312
  22.0 54.7 %collective-permute-start.5 = (f32[2,320,320]{2,1,0:T(8,128)}, f32[2,320,320]{2,1,0:T(8,128)}, u32[]{:S(2)}, u32[]{:S(2)}) collective-permute-start(f32[2,320,320]{2,1,0:T(8,128)} %constant_dynamic-update-slice_fusion.6), channel_id=1, source_target_pairs={{0,2},{129,131},{258,256},{387,385},{4,6},{133,135},{262,260},{391... | collective-permute-start | bytes 2457608 | tf_op jit(solution)/shard_map/ppermute | solution.py:312
  23.6 53.1 %collective-permute-start.4 = (f32[2,320,320]{2,1,0:T(8,128)}, f32[2,320,320]{2,1,0:T(8,128)}, u32[]{:S(2)}, u32[]{:S(2)}) collective-permute-start(f32[2,320,320]{2,1,0:T(8,128)} %constant_dynamic-update-slice_fusion.6), channel_id=1, source_target_pairs={{0,1},{129,130},{258,259},{387,384},{4,5},{133,134},{262,263},{391... | collective-permute-start | bytes 2457608 | tf_op jit(solution)/shard_map/ppermute | solution.py:312
  25.2 31.6 %collective-permute-start.2 = (f32[80,256]{1,0:T(8,128)S(1)}, f32[80,256]{1,0:T(8,128)S(1)}, u32[]{:S(2)}, u32[]{:S(2)}) collective-permute-start(f32[80,256]{1,0:T(8,128)S(1)} %constant_dynamic-update-slice_fusion), channel_id=1, source_target_pairs={{0,48},{16,0},{32,16},{48,32},{1,49},{17,1},{33,17},{49,33},{2,50}... | collective-permute-start | bytes 245768 | tf_op jit(solution)/shard_map/ppermute | solution.py:307
  31.1 31.5 %collective-permute-start.1 = (f32[80,256]{1,0:T(8,128)S(1)}, f32[80,256]{1,0:T(8,128)S(1)}, u32[]{:S(2)}, u32[]{:S(2)}) collective-permute-start(f32[80,256]{1,0:T(8,128)S(1)} %constant_dynamic-update-slice_fusion), channel_id=1, source_target_pairs={{0,32},{16,48},{32,0},{48,16},{1,33},{17,49},{33,1},{49,17},{2,34}... | collective-permute-start | bytes 245768 | tf_op jit(solution)/shard_map/ppermute | solution.py:307
  56.8 9.2 %collective-permute-start = (f32[80,256]{1,0:T(8,128)S(1)}, f32[80,256]{1,0:T(8,128)S(1)}, u32[]{:S(2)}, u32[]{:S(2)}) collective-permute-start(f32[80,256]{1,0:T(8,128)S(1)} %constant_dynamic-update-slice_fusion), channel_id=1, source_target_pairs={{0,16},{16,32},{32,48},{48,0},{1,17},{17,33},{33,49},{49,1},{2,18}... | collective-permute-start | bytes 245768 | tf_op jit(solution)/shard_map/ppermute | solution.py:307
  66.0 19.7 %all-to-all-start.1 = ((f32[8,40,256]{2,1,0:T(8,128)}), f32[8,40,256]{2,1,0:T(8,128)S(1)}, u32[]{:S(2)}, u32[]{:S(2)}) async-start(f32[8,40,256]{2,1,0:T(8,128)} %own_sum.1), calls=%async_computation.1 | async-start | bytes 655360 | tf_op jit(solution)/shard_map/all_to_all | solution.py:320
  72.7 12.3 %collective-permute-start.3 = (f32[320,256]{1,0:T(8,128)S(1)}, f32[320,256]{1,0:T(8,128)S(1)}, u32[]{:S(2)}, u32[]{:S(2)}) collective-permute-start(f32[320,256]{1,0:T(8,128)S(1)} %constant_dynamic-update-slice_fusion.2.mine_ref), channel_id=1, source_target_pairs={{0,64},{64,0},{1,65},{65,1},{2,66},{66,2},{3,67},{67,3},{4,68},{68... | collective-permute-start | bytes 983048 | tf_op jit(solution)/shard_map/ppermute | solution.py:322
  85.0 0.7 copy-start.2
  87.1 16.7 %all-to-all-start.2 = ((f32[16,16,256]{2,1,0:T(8,128)}), f32[16,16,256]{2,1,0:T(8,128)S(1)}, u32[]{:S(2)}, u32[]{:S(2)}) async-start(f32[16,16,256]{2,1,0:T(8,128)} %bitcast.4), calls=%async_computation.2 | async-start | bytes 524288 | tf_op jit(solution)/shard_map/all_to_all | solution.py:327
  92.4 20.2 %collective-permute-start.9 = (f32[320,256]{1,0:T(8,128)S(1)}, f32[320,256]{1,0:T(8,128)S(1)}, u32[]{:S(2)}, u32[]{:S(2)}) collective-permute-start(f32[320,256]{1,0:T(8,128)S(1)} %bitcast.18), channel_id=1, source_target_pairs={{0,3},{1,0},{2,1},{3,2},{4,7},{5,4},{6,5},{7,6},{8,11},{9,8},{10,9... | collective-permute-start | bytes 983048 | tf_op jit(solution)/shard_map/ppermute | solution.py:328
  95.9 17.3 %collective-permute-start.8 = (f32[320,256]{1,0:T(8,128)S(1)}, f32[320,256]{1,0:T(8,128)S(1)}, u32[]{:S(2)}, u32[]{:S(2)}) collective-permute-start(f32[320,256]{1,0:T(8,128)S(1)} %bitcast.19), channel_id=1, source_target_pairs={{0,2},{1,3},{2,0},{3,1},{4,6},{5,7},{6,4},{7,5},{8,10},{9,11},{10,... | collective-permute-start | bytes 983048 | tf_op jit(solution)/shard_map/ppermute | solution.py:328
  98.1 17.1 %collective-permute-start.7 = (f32[320,256]{1,0:T(8,128)S(1)}, f32[320,256]{1,0:T(8,128)}, u32[]{:S(2)}, u32[]{:S(2)}) collective-permute-start(f32[320,256]{1,0:T(8,128)S(1)} %bitcast.20), channel_id=1, source_target_pairs={{0,1},{1,2},{2,3},{3,0},{4,5},{5,6},{6,7},{7,4},{8,9},{9,10},{10,1... | collective-permute-start | bytes 983048 | tf_op jit(solution)/shard_map/ppermute | solution.py:328
  104.5 46.7 %all-to-all-start.3 = ((f32[16,16,256]{2,1,0:T(8,128)}), f32[16,16,256]{2,1,0:T(8,128)S(1)}, u32[]{:S(2)}, u32[]{:S(2)}) async-start(f32[16,16,256]{2,1,0:T(8,128)} %get-tuple-element.40), calls=%async_computation.3 | async-start | bytes 524288 | tf_op jit(solution)/shard_map/all_to_all | solution.py:333
  112.6 0.7 copy-start.4
  113.3 0.7 copy-start.6
  115.2 1.0 copy-start.5
  116.2 1.0 copy-start.7
  120.3 25.6 %collective-permute-start.13 = (f32[320,320]{1,0:T(8,128)S(1)}, f32[320,320]{1,0:T(8,128)}, u32[]{:S(2)}, u32[]{:S(2)}) collective-permute-start(f32[320,320]{1,0:T(8,128)S(1)} %left_gram.1.left_raw_ref), channel_id=1, source_target_pairs={{0,0},{1,129},{2,258},{3,387},{128,384},{129,1},{130,130},{131,259... | collective-permute-start | bytes 1228808 | tf_op jit(solution)/shard_map/ppermute | solution.py:340
  126.0 25.2 %collective-permute-start.12 = (f32[8,128]{1,0:T(8,128)S(1)}, f32[8,128]{1,0:T(8,128)S(1)}, u32[]{:S(2)}, u32[]{:S(2)}) collective-permute-start(f32[8,128]{1,0:T(8,128)S(1)} %get-tuple-element.41.sq0_ref), channel_id=1, source_target_pairs={{0,3},{1,0},{2,1},{3,2},{4,7},{5,4},{6,5},{7,6},{8,11},{9,8},{10,9... | collective-permute-start | bytes 12296 | tf_op jit(solution)/shard_map/ppermute | solution.py:335
  131.0 20.1 %collective-permute-start.11 = (f32[8,128]{1,0:T(8,128)S(1)}, f32[8,128]{1,0:T(8,128)S(1)}, u32[]{:S(2)}, u32[]{:S(2)}) collective-permute-start(f32[8,128]{1,0:T(8,128)S(1)} %get-tuple-element.41.sq0_ref), channel_id=1, source_target_pairs={{0,2},{1,3},{2,0},{3,1},{4,6},{5,7},{6,4},{7,5},{8,10},{9,11},{10,... | collective-permute-start | bytes 12296 | tf_op jit(solution)/shard_map/ppermute | solution.py:335
  133.0 18.2 %collective-permute-start.10 = (f32[8,128]{1,0:T(8,128)S(1)}, f32[8,128]{1,0:T(8,128)S(1)}, u32[]{:S(2)}, u32[]{:S(2)}) collective-permute-start(f32[8,128]{1,0:T(8,128)S(1)} %get-tuple-element.41.sq0_ref), channel_id=1, source_target_pairs={{0,1},{1,2},{2,3},{3,0},{4,5},{5,6},{6,7},{7,4},{8,9},{9,10},{10,1... | collective-permute-start | bytes 12296 | tf_op jit(solution)/shard_map/ppermute | solution.py:335
  145.9 38.4 %collective-permute-start.14 = (f32[320,320]{1,0:T(8,128)}, f32[320,320]{1,0:T(8,128)}, u32[]{:S(2)}, u32[]{:S(2)}) collective-permute-start(f32[320,320]{1,0:T(8,128)} %collective-permute-done.13), channel_id=1, source_target_pairs={{0,0},{1,1},{2,2},{3,3},{128,131},{129,128},{130,129},{131,130},{2... | collective-permute-start | bytes 1228808 | tf_op jit(solution)/shard_map/ppermute | solution.py:347
  151.2 1.0 copy-start.3
  152.2 0.9 copy-start.8
  153.1 0.9 copy-start.9
  178.4 37.6 %all-to-all-start.4 = ((f32[4,320,256]{2,1,0:T(8,128)}), f32[4,320,256]{2,1,0:T(8,128)S(1)}, u32[]{:S(2)}, u32[]{:S(2)}) async-start(f32[4,320,256]{2,1,0:T(8,128)} %broadcast_in_dim.23), calls=%async_computation.4 | async-start | bytes 2621440 | tf_op jit(solution)/shard_map/all_to_all | solution.py:293

commit v6 on v5

--- a/solution.py
+++ b/solution.py
@@ -121,24 +121,29 @@
 
 
 def refresh_kernel(
-    member_ref, left_raw_ref, moved_ref, right_raw_ref, gr_ref, br_ref, tile_ref, sq0_ref, sq1_ref,
-    sq2_ref, sq3_ref, mine_ref, other_ref,
+    member_ref, left_raw_ref, moved_ref, right_raw_ref, tile_ref, gr_hbm, br_hbm, mine_hbm, other_hbm,
     gr_out_ref, qr_out_ref, m_ref, v_ref, u_ref, factor_ref,
     sl_ref, pl_ref, qlt_ref, sr_ref, pr_ref, qrt_ref, ms_ref, vs_ref,
+    gr_ref, br_ref, mine_ref, other_ref, sems,
 ):
+    fetched = [
+        pltpu.make_async_copy(src, dst, sems.at[n])
+        for n, (src, dst) in enumerate(
+            ((gr_hbm, gr_ref), (br_hbm, br_ref), (mine_hbm, mine_ref), (other_hbm, other_ref))
+        )
+    ]
+    for copy in fetched:
+        copy.start()
     y2, zh = member_ref[0] // 4, lax.rem(member_ref[0], 4)
-    for src_ref, pair in ((mine_ref, y2), (other_ref, 1 - y2)):
-        for n, shift in enumerate((0, -1, -2, -3)):
-            at = pl.multiple_of(40 * (4 * pair + lax.rem(zh + shift + 4, 4)), 8)
-            ms_ref[pl.ds(at, 40), :] = src_ref[80 * n : 80 * n + 40, :]
-            vs_ref[pl.ds(at, 40), :] = src_ref[80 * n + 40 : 80 * n + 80, :]
     packed = right_raw_ref[...]
     slot = slots((RB, RB), 0, 1)
     right_raw = jnp.where(slot, packed.T, packed)
-    total = (sq0_ref[...] + sq1_ref[...] + (sq2_ref[...] + sq3_ref[...]))[:1, :1]
+    total = jnp.sum(jnp.where(slot, packed, 0.0), keepdims=True)
     factor = clip_ratio * math.sqrt(D * KV) / (jnp.sqrt(total) + 1e-06)
     factor_ref[...] = jnp.broadcast_to(factor, factor_ref.shape)
     weight = (1.0 - beta_gram) * factor * factor
+    fetched[0].wait()
+    fetched[1].wait()
     right_new = beta_gram * gr_ref[...] + weight * right_raw
     gr_out_ref[...] = right_new
     left_new = beta_gram * moved_ref[0] + weight * left_raw_ref[...]
@@ -151,6 +156,13 @@
     qrt = qrt_ref[...]
     qr_out_ref[...] = qrt.T
     rotated = mm(mm(qlt_ref[...], tile_ref[...]) * factor, qrt, 1, 1)
+    fetched[2].wait()
+    fetched[3].wait()
+    for src_ref, pair in ((mine_ref, y2), (other_ref, 1 - y2)):
+        for n, shift in enumerate((0, -1, -2, -3)):
+            at = pl.multiple_of(40 * (4 * pair + lax.rem(zh + shift + 4, 4)), 8)
+            ms_ref[pl.ds(at, 40), :] = src_ref[80 * n : 80 * n + 40, :]
+            vs_ref[pl.ds(at, 40), :] = src_ref[80 * n + 40 : 80 * n + 80, :]
     moment = beta_first * ms_ref[...] + (1.0 - beta_first) * rotated
     second = beta_second * vs_ref[...] + (1.0 - beta_second) * rotated * rotated
     ms_ref[...] = moment
@@ -170,7 +182,7 @@
     return pl.BlockSpec(memory_space=pltpu.VMEM)
 
 
-def refresh(member, left_raw, moved, right_raw, gr, br, tile, squares, mine, other):
+def refresh(member, left_raw, moved, right_raw, tile, gr, br, mine, other):
     f32 = jnp.float32
     return pl.pallas_call(
         refresh_kernel,
@@ -178,17 +190,22 @@
             shape_of(RB, RB), shape_of(RB, RB), shape_of(40, RB), shape_of(40, RB),
             shape_of(LB, RB), shape_of(8, 128),
         ),
-        in_specs=[pl.BlockSpec(memory_space=pltpu.SMEM)] + [whole()] * 12,
+        in_specs=[pl.BlockSpec(memory_space=pltpu.SMEM)]
+        + [whole()] * 4
+        + [pl.BlockSpec(memory_space=pl.ANY)] * 4,
         out_specs=(whole(),) * 6,
         scratch_shapes=[pltpu.VMEM((LB, LB), f32)] * 3
         + [pltpu.VMEM((RB, RB), f32)] * 3
-        + [pltpu.VMEM((LB, RB), f32)] * 2,
+        + [pltpu.VMEM((LB, RB), f32)] * 2
+        + [pltpu.VMEM((RB, RB), f32)] * 2
+        + [pltpu.VMEM((LB, RB), f32)] * 2
+        + [pltpu.SemaphoreType.DMA((4,))],
         compiler_params=pltpu.CompilerParams(vmem_limit_bytes=12 * 2**20),
         cost_estimate=pl.CostEstimate(
             flops=25_000_000_000, bytes_accessed=4_000_000, transcendentals=0
         ),
         name="refresh",
-    )(member, left_raw, moved, right_raw, gr, br, tile, *squares, mine, other)
+    )(member, left_raw, moved, right_raw, tile, gr, br, mine, other)
 
 
 def held_kernel(factor_ref, raw_ref, g_ref, b_ref, g_out_ref, q_out_ref, s_ref, p_ref, qt_ref):
@@ -226,36 +243,54 @@
 
 def right_part_kernel(tile_ref, out_ref):
     tile = tile_ref[...]
-    squares = jnp.sum(tile * tile, keepdims=True)
-    out_ref[...] = jnp.where(slots((RB, RB), 0, 1), squares, mm(tile, tile, 0, 0))
-
-
-def right_sum_kernel(group_ref, parts_ref, out_ref, squares_ref):
+    out_ref[...] = mm(tile, tile, 0, 0)
+
+
+def fetch(refs, landed_ref, sems):
+    copies = [
+        pltpu.make_async_copy(ref, landed_ref.at[n], sems.at[n]) for n, ref in enumerate(refs)
+    ]
+    for copy in copies:
+        copy.start()
+    return copies
+
+
+def right_sum_kernel(group_ref, parts_ref, tile_ref, *refs):
+    others, out_ref, landed_ref, sems = refs[:3], refs[3], refs[4], refs[5]
+    copies = fetch(others, landed_ref, sems)
     total = parts_ref[0]
     for r in range(1, 16):
         total = total + parts_ref[r]
+    squares = jnp.sum(tile_ref[...] * tile_ref[...], keepdims=True)
+    for n, copy in enumerate(copies):
+        copy.wait()
+        squares = squares + jnp.sum(landed_ref[n] * landed_ref[n], keepdims=True)
+    total = jnp.where(slots((16, RB), 0, 16 * group_ref[0] + 1), squares, total)
     for n in range(16):
         out_ref[n] = total
-    slot = slots((16, RB), 0, 16 * group_ref[0] + 1)
-    squares = jnp.sum(jnp.where(slot, total, 0.0), keepdims=True)
-    squares_ref[...] = jnp.broadcast_to(squares, squares_ref.shape)
-
-
-def left_gram_kernel(*refs):
-    total = mm(refs[0][...], refs[0][...], 1, 1)
-    for n in range(1, 4):
-        total = total + mm(refs[n][...], refs[n][...], 1, 1)
-    refs[4][...] = total
-
-
-def small(kernel, name, out_shape, flops, *operands, scalars=0):
+
+
+def left_gram_kernel(tile_ref, *refs):
+    others, out_ref, landed_ref, sems = refs[:3], refs[3], refs[4], refs[5]
+    copies = fetch(others, landed_ref, sems)
+    total = mm(tile_ref[...], tile_ref[...], 1, 1)
+    for n, copy in enumerate(copies):
+        copy.wait()
+        total = total + mm(landed_ref[n], landed_ref[n], 1, 1)
+    out_ref[...] = total
+
+
+def small(kernel, name, out_shape, flops, *operands, scalars=0, places=0):
     specs = [pl.BlockSpec(memory_space=pltpu.SMEM)] * scalars
-    specs = specs + [whole()] * (len(operands) - scalars)
+    specs = specs + [whole()] * (len(operands) - scalars - places)
+    specs = specs + [pl.BlockSpec(memory_space=pl.ANY)] * places
+    scratch = [pltpu.VMEM((places, LB, RB), jnp.float32), pltpu.SemaphoreType.DMA((places,))]
     return pl.pallas_call(
         kernel,
         out_shape=out_shape,
         in_specs=specs,
-        out_specs=jax.tree.map(lambda _: whole(), out_shape),
+        out_specs=whole(),
+        scratch_shapes=scratch if places else [],
         compiler_params=pltpu.CompilerParams(vmem_limit_bytes=6 * 2**20),
         cost_estimate=pl.CostEstimate(flops=flops, bytes_accessed=1_000_000, transcendentals=0),
         name=name,
@@ -307,16 +342,18 @@
     column = [ours] + [lax.ppermute(ours, "zh", shift_perm(4, by)) for by in range(1, 4)]
 
     held = jnp.concatenate([left_gram, left_basis], axis=0)
-    moved = jnp.where(x == k, held, 0.0)
-    for by in range(1, 4):
-        moved = moved + lax.ppermute(
-            held, ("yk", "x"), [(b * 4 + b, b * 4 + (b + by) % 4) for b in range(4)]
-        )
+    near = lax.ppermute(held, ("yk", "x"), [(b * 4 + b, b * 4 + (b + 1) % 4) for b in range(4)])
+    near = jnp.where(x == k, held, near)
+    far = lax.ppermute(
+        near, ("yk", "x"),
+        [(b * 4 + (b + n) % 4, b * 4 + (b + n + 2) % 4) for b in range(4) for n in range(2)],
+    )
+    moved = near + far
 
     pieces = pseudo_grads[0].astype(jnp.float32).reshape(32, 40, RB)
     arrived = lax.all_to_all(pieces, REP, 0, 0, tiled=True)
     copies = small(own_sum_kernel, "own_sum", shape_of(8, 40, RB), 10**8, arrived)
-    copies, *column = lax.optimization_barrier((copies, *column))
+    _, *column = lax.optimization_barrier((copies, *column))
     tile = lax.all_to_all(copies, MEMBERS, 0, 0, tiled=True).reshape(LB, RB)
     mine = jnp.concatenate(column, axis=0)
     other = lax.ppermute(mine, "y2", shift_perm(2, 1))
@@ -325,25 +362,24 @@
     right_part = small(right_part_kernel, "right_part", shape_of(RB, RB), 10**9, tile)
     sent, right_part = lax.optimization_barrier((tile, right_part))
     parts = lax.all_to_all(right_part.reshape(16, 16, RB), RIGHT_GROUP, 0, 0, tiled=True)
-    tiles = [tile] + [lax.ppermute(sent, "x", shift_perm(4, by)) for by in range(1, 4)]
-    right_own, squares_own = small(
-        right_sum_kernel, "right_sum", (shape_of(16, 16, RB), shape_of(8, 128)), 10**8,
-        lax.axis_index(RIGHT_GROUP).astype(jnp.int32).reshape(1), parts, scalars=1,
+    tiles = [lax.ppermute(sent, "x", shift_perm(4, by)) for by in range(1, 4)]
+    right_own = small(
+        right_sum_kernel, "right_sum", shape_of(16, 16, RB), 10**8,
+        lax.axis_index(RIGHT_GROUP).astype(jnp.int32).reshape(1), parts, tile, *tiles,
+        scalars=1, places=3,
     )
     right_raw = lax.all_to_all(right_own, RIGHT_GROUP, 0, 0, tiled=True).reshape(RB, RB)
-    squares = [squares_own] + [
-        lax.ppermute(squares_own, "x", shift_perm(4, by)) for by in range(1, 4)
-    ]
-    left_raw = small(left_gram_kernel, "left_gram", shape_of(LB, LB), 2 * 10**9, *tiles)
+    left_raw = small(left_gram_kernel, "left_gram", shape_of(LB, LB), 2 * 10**9, tile, *tiles, places=3)
     along_y = [(j * 4 + c, (c - j) % 4 * 4 + c) for j in range(4) for c in range(4)]
     along_x = [(g * 4 + c, g * 4 + (c - g) % 4) for g in range(4) for c in range(4)]
     passed = lax.ppermute(left_raw, ("yk", "x"), along_y)
 
     right_new, right_basis_new, moment, second, turned, factor = refresh(
         lax.axis_index(MEMBERS).astype(jnp.int32).reshape(1), left_raw, moved, right_raw,
-        right_gram[0], right_basis[0], tile, squares, mine, other,
-    )
-
+        tile, right_gram[0], right_basis[0], mine, other,
+    )
+
+    passed, turned = lax.optimization_barrier((passed, turned))
     held_raw = lax.ppermute(passed, ("yk", "x"), along_x)
     blocks = gather_all(turned, "yk", 4)
     left_new, left_basis_new = refresh_held(factor, held_raw, left_gram[0], left_basis[0])

time: 220 us -> 201 us (0.914)
  the two profiles are of different devices: /device:TPU:6 before, /device:TPU:4 now
where the time goes in v6:
time: 201 us; the launch traced here: 200 us
  starting transfers between devices  83.7 us (42%)
  waiting for transfers between devices  53.1 us (26%)
  Pallas kernels  48.5 us (24%)
  local copies, waits for them, and re-layouts  8.35 us (4%)
  other arithmetic  4.88 us (2%)
    pallas_call x1, Pallas kernels, refresh(): pl.pallas_call(refresh_kernel, out_shape=(shape_of(RB, RB), shape_of(RB,...  24.6 us
    all_to_all x1, waiting for transfers between devices, gather_all(): return lax.all_to_all(copies, axes, 0, 0, tiled=True)  18 us
    all_to_all x1, starting transfers between devices, shards(): arrived = lax.all_to_all(pieces, REP, 0, 0, tiled=True)  16.1 us
    pallas_call x1, Pallas kernels, refresh_held(): pl.pallas_call(held_kernel, out_shape=(shape_of(LB, LB), shape_of(LB, LB)...  15.4 us
    all_to_all x1, waiting for transfers between devices, shards(): arrived = lax.all_to_all(pieces, REP, 0, 0, tiled=True)  14.9 us
    ppermute x3, starting transfers between devices, shards(): lax.ppermute(ours, 'zh', shift_perm(4, by))  14.3 us
    ppermute x3, waiting for transfers between devices, shards(): tiles = [lax.ppermute(sent, 'x', shift_perm(4, by)) for by in range(1, 4)]  13.8 us
    all_to_all x1, starting transfers between devices, shards(): lax.all_to_all(right_part.reshape(16, 16, RB), RIGHT_GROUP, 0, 0, tiled=T...  8.85 us
  transfers between devices with their start and end apart: 16, of which 7 were waited for; matrix products, arithmetic and copies ran while one was open for 3% of the time, Pallas kernels for 22%

profile of v6, /device:TPU:4, one launch (start us, length us, event | category | flops | bytes accessed | tf_op | source)
XLA Modules:
  0.0 199.6 jit_solution(8660400202183215664)
XLA Ops:
  0.6 2.3 %convert.1 = f32[32,40,256]{2,1,0:T(8,128)} convert(bf16[32,40,256]{2,1,0:T(8,128)(2,1)} %bitcast.27) | non-fusion elementwise | flops 327680 | bytes 1966080 | tf_op jit(solution)/shard_map/convert_element_type | solution.py:353
  2.9 16.1 %all-to-all-start = ((f32[32,40,256]{2,1,0:T(8,128)}), f32[32,40,256]{2,1,0:T(8,128)S(1)}, u32[]{:S(2)}, u32[]{:S(2)}) async-start(f32[32,40,256]{2,1,0:T(8,128)} %convert.1), calls=%async_computation | async-start | bytes 2621440 | tf_op jit(solution)/shard_map/all_to_all | solution.py:354
  19.0 0.0 copy-start.8
  19.0 0.0 copy-start.9
  19.0 0.8 constant_dynamic-update-slice_fusion.7
  19.9 0.8 constant_dynamic-update-slice_fusion.6
  20.7 1.6 collective-permute-start.4
  22.3 5.8 %collective-permute-start.2 = (f32[80,256]{1,0:T(8,128)S(1)}, f32[80,256]{1,0:T(8,128)S(1)}, u32[]{:S(2)}, u32[]{:S(2)}) collective-permute-start(f32[80,256]{1,0:T(8,128)S(1)} %constant_dynamic-update-slice_fusion), channel_id=1, source_target_pairs={{0,48},{16,0},{32,16},{48,32},{1,49},{17,1},{33,17},{49,33},{2,50}... | collective-permute-start | bytes 245768 | tf_op jit(solution)/shard_map/ppermute | solution.py:342
  28.1 4.3 %collective-permute-start.1 = (f32[80,256]{1,0:T(8,128)S(1)}, f32[80,256]{1,0:T(8,128)S(1)}, u32[]{:S(2)}, u32[]{:S(2)}) collective-permute-start(f32[80,256]{1,0:T(8,128)S(1)} %constant_dynamic-update-slice_fusion), channel_id=1, source_target_pairs={{0,32},{16,48},{32,0},{48,16},{1,33},{17,49},{33,1},{49,17},{2,34}... | collective-permute-start | bytes 245768 | tf_op jit(solution)/shard_map/ppermute | solution.py:342
  32.4 4.3 %collective-permute-start = (f32[80,256]{1,0:T(8,128)S(1)}, f32[80,256]{1,0:T(8,128)}, u32[]{:S(2)}, u32[]{:S(2)}) collective-permute-start(f32[80,256]{1,0:T(8,128)S(1)} %constant_dynamic-update-slice_fusion), channel_id=1, source_target_pairs={{0,16},{16,32},{32,48},{48,0},{1,17},{17,33},{33,49},{49,1},{2,18}... | collective-permute-start | bytes 245768 | tf_op jit(solution)/shard_map/ppermute | solution.py:342
  36.7 0.0 collective-permute-done.4
  36.7 1.3 broadcast_select_fusion
  38.0 1.3 collective-permute-start.5
  39.3 14.9 %all-to-all-done.arrived_ref = f32[32,40,256]{2,1,0:T(8,128)S(1)} async-done(((f32[32,40,256]{2,1,0:T(8,128)}), f32[32,40,256]{2,1,0:T(8,128)S(1)}, u32[]{:S(2)}, u32[]{:S(2)}) %all-to-all-start) | async-done | bytes 1310752 | tf_op jit(solution)/shard_map/all_to_all | solution.py:354
  54.2 0.8 own_sum.1
  55.0 5.5 %all-to-all-start.1 = ((f32[8,40,256]{2,1,0:T(8,128)}), f32[8,40,256]{2,1,0:T(8,128)S(1)}, u32[]{:S(2)}, u32[]{:S(2)}) async-start(f32[8,40,256]{2,1,0:T(8,128)} %own_sum.1), calls=%async_computation.1 | async-start | bytes 655360 | tf_op jit(solution)/shard_map/all_to_all | solution.py:357
  60.5 0.0 collective-permute-done.2
  60.5 0.9 constant_dynamic-update-slice_fusion.4
  61.5 0.0 copy-start.2
  61.5 3.9 %collective-permute-start.3 = (f32[320,256]{1,0:T(8,128)S(1)}, f32[320,256]{1,0:T(8,128)S(1)}, u32[]{:S(2)}, u32[]{:S(2)}) collective-permute-start(f32[320,256]{1,0:T(8,128)S(1)} %constant_dynamic-update-slice_fusion.2.mine_hbm), channel_id=1, source_target_pairs={{0,64},{64,0},{1,65},{65,1},{2,66},{66,2},{3,67},{67,3},{4,68},{68... | collective-permute-start | bytes 983048 | tf_op jit(solution)/shard_map/ppermute | solution.py:359
  65.4 3.5 %collective-permute-done.5 = f32[2,320,320]{2,1,0:T(8,128)} collective-permute-done((f32[2,320,320]{2,1,0:T(8,128)S(1)}, f32[2,320,320]{2,1,0:T(8,128)}, u32[]{:S(2)}, u32[]{:S(2)}) %collective-permute-start.5) | collective-permute-done | bytes 819232 | tf_op jit(solution)/shard_map/ppermute | solution.py:347
  68.9 1.3 add.12.moved_ref
  70.2 2.9 %collective-permute-done.3.other_hbm = f32[320,256]{1,0:T(8,128)S(1)} collective-permute-done((f32[320,256]{1,0:T(8,128)S(1)}, f32[320,256]{1,0:T(8,128)S(1)}, u32[]{:S(2)}, u32[]{:S(2)}) %collective-permute-start.3) | collective-permute-done | bytes 327712 | tf_op jit(solution)/shard_map/ppermute | solution.py:359
  73.0 0.7 copy-done.4
  73.8 1.3 right_part.1
  75.1 8.8 %all-to-all-start.2 = ((f32[16,16,256]{2,1,0:T(8,128)}), f32[16,16,256]{2,1,0:T(8,128)S(1)}, u32[]{:S(2)}, u32[]{:S(2)}) async-start(f32[16,16,256]{2,1,0:T(8,128)} %bitcast.4), calls=%async_computation.2 | async-start | bytes 524288 | tf_op jit(solution)/shard_map/all_to_all | solution.py:364
  84.0 2.5 %collective-permute-start.8 = (f32[320,256]{1,0:T(8,128)S(1)}, f32[320,256]{1,0:T(8,128)S(1)}, u32[]{:S(2)}, u32[]{:S(2)}) collective-permute-start(f32[320,256]{1,0:T(8,128)S(1)} %bitcast.16), channel_id=1, source_target_pairs={{0,3},{1,0},{2,1},{3,2},{4,7},{5,4},{6,5},{7,6},{8,11},{9,8},{10,9... | collective-permute-start | bytes 983048 | tf_op jit(solution)/shard_map/ppermute | solution.py:365
  86.4 3.8 %collective-permute-start.7 = (f32[320,256]{1,0:T(8,128)S(1)}, f32[320,256]{1,0:T(8,128)S(1)}, u32[]{:S(2)}, u32[]{:S(2)}) collective-permute-start(f32[320,256]{1,0:T(8,128)S(1)} %bitcast.17), channel_id=1, source_target_pairs={{0,2},{1,3},{2,0},{3,1},{4,6},{5,7},{6,4},{7,5},{8,10},{9,11},{10,... | collective-permute-start | bytes 983048 | tf_op jit(solution)/shard_map/ppermute | solution.py:365
  90.3 2.5 %collective-permute-start.6 = (f32[320,256]{1,0:T(8,128)S(1)}, f32[320,256]{1,0:T(8,128)S(1)}, u32[]{:S(2)}, u32[]{:S(2)}) collective-permute-start(f32[320,256]{1,0:T(8,128)S(1)} %bitcast.18), channel_id=1, source_target_pairs={{0,1},{1,2},{2,3},{3,0},{4,5},{5,6},{6,7},{7,4},{8,9},{9,10},{10,1... | collective-permute-start | bytes 983048 | tf_op jit(solution)/shard_map/ppermute | solution.py:365
  92.8 3.6 %collective-permute-done.8.refs_2_ = f32[320,256]{1,0:T(8,128)S(1)} collective-permute-done((f32[320,256]{1,0:T(8,128)S(1)}, f32[320,256]{1,0:T(8,128)S(1)}, u32[]{:S(2)}, u32[]{:S(2)}) %collective-permute-start.8) | collective-permute-done | bytes 327712 | tf_op jit(solution)/shard_map/ppermute | solution.py:365
  96.4 4.0 %collective-permute-done.7.refs_1_ = f32[320,256]{1,0:T(8,128)S(1)} collective-permute-done((f32[320,256]{1,0:T(8,128)S(1)}, f32[320,256]{1,0:T(8,128)S(1)}, u32[]{:S(2)}, u32[]{:S(2)}) %collective-permute-start.7) | collective-permute-done | bytes 327712 | tf_op jit(solution)/shard_map/ppermute | solution.py:365
  100.4 6.2 %collective-permute-done.6.refs_0_ = f32[320,256]{1,0:T(8,128)S(1)} collective-permute-done((f32[320,256]{1,0:T(8,128)S(1)}, f32[320,256]{1,0:T(8,128)S(1)}, u32[]{:S(2)}, u32[]{:S(2)}) %collective-permute-start.6) | collective-permute-done | bytes 327712 | tf_op jit(solution)/shard_map/ppermute | solution.py:365
  106.6 1.9 right_sum.1
  108.5 7.8 %all-to-all-start.3 = ((f32[16,16,256]{2,1,0:T(8,128)}), f32[16,16,256]{2,1,0:T(8,128)S(1)}, u32[]{:S(2)}, u32[]{:S(2)}) async-start(f32[16,16,256]{2,1,0:T(8,128)} %right_sum.1), calls=%async_computation.3 | async-start | bytes 524288 | tf_op jit(solution)/shard_map/all_to_all | solution.py:371
  116.3 3.6 %left_gram.1.left_raw_ref = f32[320,320]{1,0:T(8,128)} custom-call(f32[320,256]{1,0:T(8,128)S(1)} %bitcast.20, f32[320,256]{1,0:T(8,128)S(1)} %collective-permute-done.6.refs_0_, f32[320,256]{1,0:T(8,128)S(1)} %collective-permute-done.7.refs_1_, f32[320,256]{1,0:T(8,128)S(1)} %collective-permute-done.8.refs_2_), custom_call_target="tpu_custom_call" | custom-call | flops 2000000000 | bytes 1000000 | tf_op jit(solution)/shard_map/left_gram/pallas_call | solution.py:288
  119.9 7.7 %collective-permute-start.9 = (f32[320,320]{1,0:T(8,128)}, f32[320,320]{1,0:T(8,128)S(1)}, u32[]{:S(2)}, u32[]{:S(2)}) collective-permute-start(f32[320,320]{1,0:T(8,128)} %left_gram.1.left_raw_ref), channel_id=1, source_target_pairs={{0,0},{1,129},{2,258},{3,387},{128,384},{129,1},{130,130},{131,259... | collective-permute-start | bytes 1228808 | tf_op jit(solution)/shard_map/ppermute | solution.py:375
  127.6 0.0 all-to-all-done.3
  127.7 1.0 copy-done.3
  128.6 1.0 copy-done.5
  129.6 0.9 copy-done.6
  130.6 0.9 copy-done.7
  131.5 24.6 %refresh.1 = (f32[256,256]{1,0:T(8,128)}, f32[256,256]{1,0:T(8,128)}, f32[40,256]{1,0:T(8,128)}, f32[40,256]{1,0:T(8,128)}, f32[320,256]{1,0:T(8,128)S(1)}, /*index=5*/f32[8,128]{1,0:T(8,128)S(1)}) custom-call(s32[1]{0:T(128)} %bitcast.2.member_ref, f32[320,320]{1,0:T(8,128)} %left_gram.1.left_raw_ref, f32[2,320,320]{2,1,0:T(8,128)S(1)} %add.12.moved_ref, ...), custom_call_target="tpu_custom_call" | custom-call | flops 24999999488 | bytes 4000000 | tf_op jit(solution)/shard_map/refresh/pallas_call | solution.py:187
  156.1 0.7 collective-permute-start.10
  156.8 1.2 broadcast_in_dim.18
  158.0 7.0 %all-to-all-start.4 = ((f32[4,320,256]{2,1,0:T(8,128)}), f32[4,320,256]{2,1,0:T(8,128)S(1)}, u32[]{:S(2)}, u32[]{:S(2)}) async-start(f32[4,320,256]{2,1,0:T(8,128)} %broadcast_in_dim.18), calls=%async_computation.4 | async-start | bytes 2621440 | tf_op jit(solution)/shard_map/all_to_all | solution.py:328
  165.1 15.4 %refresh_held.1 = (f32[320,320]{1,0:T(8,128)}, f32[320,320]{1,0:T(8,128)}) custom-call(f32[8,128]{1,0:T(8,128)S(1)} %get-tuple-element.42.factor_ref, f32[320,320]{1,0:T(8,128)S(1)} %collective-permute-done.10.raw_ref, f32[320,320]{1,0:T(8,128)S(1)} %bitcast.22, f32[320,320]{1,0:T(8,128)S(1)} %bitcast.23), custom_call_target="tpu_custom_call" | custom-call | flops 17999998976 | bytes 2000000 | tf_op jit(solution)/shard_map/refresh_held/pallas_call | solution.py:221
  180.5 18.0 %all-to-all-done.4.blocks_ref = f32[4,320,256]{2,1,0:T(8,128)S(1)} async-done(((f32[4,320,256]{2,1,0:T(8,128)}), f32[4,320,256]{2,1,0:T(8,128)S(1)}, u32[]{:S(2)}, u32[]{:S(2)}) %all-to-all-start.4) | async-done | bytes 1310752 | tf_op jit(solution)/shard_map/all_to_all | solution.py:328
  198.5 0.9 place.1
  (23 shorter events, 0.1 us)
Async XLA Ops:
  2.9 16.1 %copy-start = (f32[1,320,320]{2,1,0:T(8,128)S(1)}, f32[1,320,320]{2,1,0:T(8,128)}, u32[]{:S(2)}) copy-start(f32[1,320,320]{2,1,0:T(8,128)} %param.8) | copy-start | bytes 1228804
  2.9 17.0 %copy-start.1 = (f32[1,320,320]{2,1,0:T(8,128)S(1)}, f32[1,320,320]{2,1,0:T(8,128)}, u32[]{:S(2)}) copy-start(f32[1,320,320]{2,1,0:T(8,128)} %param.10) | copy-start | bytes 1228804
  2.9 51.3 %all-to-all-start = ((f32[32,40,256]{2,1,0:T(8,128)}), f32[32,40,256]{2,1,0:T(8,128)S(1)}, u32[]{:S(2)}, u32[]{:S(2)}) async-start(f32[32,40,256]{2,1,0:T(8,128)} %convert.1), calls=%async_computation | async-start | bytes 2621440 | tf_op jit(solution)/shard_map/all_to_all | solution.py:354
  19.0 3.3 %copy-start.8 = (f32[40,256]{1,0:T(8,128)S(1)}, f32[40,256]{1,0:T(8,128)}, u32[]{:S(2)}) copy-start(f32[40,256]{1,0:T(8,128)} %param.12) | copy-start | bytes 122884
  19.0 3.3 %copy-start.9 = (f32[40,256]{1,0:T(8,128)S(1)}, f32[40,256]{1,0:T(8,128)}, u32[]{:S(2)}) copy-start(f32[40,256]{1,0:T(8,128)} %param.13) | copy-start | bytes 122884
  20.7 16.0 %collective-permute-start.4 = (f32[2,320,320]{2,1,0:T(8,128)}, f32[2,320,320]{2,1,0:T(8,128)}, u32[]{:S(2)}, u32[]{:S(2)}) collective-permute-start(f32[2,320,320]{2,1,0:T(8,128)} %constant_dynamic-update-slice_fusion.6), channel_id=1, source_target_pairs={{0,1},{129,130},{258,259},{387,384},{4,5},{133,134},{262,263},{391... | collective-permute-start | bytes 2457608 | tf_op jit(solution)/shard_map/ppermute | solution.py:345
  22.3 38.2 %collective-permute-start.2 = (f32[80,256]{1,0:T(8,128)S(1)}, f32[80,256]{1,0:T(8,128)S(1)}, u32[]{:S(2)}, u32[]{:S(2)}) collective-permute-start(f32[80,256]{1,0:T(8,128)S(1)} %constant_dynamic-update-slice_fusion), channel_id=1, source_target_pairs={{0,48},{16,0},{32,16},{48,32},{1,49},{17,1},{33,17},{49,33},{2,50}... | collective-permute-start | bytes 245768 | tf_op jit(solution)/shard_map/ppermute | solution.py:342
  28.1 32.4 %collective-permute-start.1 = (f32[80,256]{1,0:T(8,128)S(1)}, f32[80,256]{1,0:T(8,128)S(1)}, u32[]{:S(2)}, u32[]{:S(2)}) collective-permute-start(f32[80,256]{1,0:T(8,128)S(1)} %constant_dynamic-update-slice_fusion), channel_id=1, source_target_pairs={{0,32},{16,48},{32,0},{48,16},{1,33},{17,49},{33,1},{49,17},{2,34}... | collective-permute-start | bytes 245768 | tf_op jit(solution)/shard_map/ppermute | solution.py:342
  32.4 28.1 %collective-permute-start = (f32[80,256]{1,0:T(8,128)S(1)}, f32[80,256]{1,0:T(8,128)}, u32[]{:S(2)}, u32[]{:S(2)}) collective-permute-start(f32[80,256]{1,0:T(8,128)S(1)} %constant_dynamic-update-slice_fusion), channel_id=1, source_target_pairs={{0,16},{16,32},{32,48},{48,0},{1,17},{17,33},{33,49},{49,1},{2,18}... | collective-permute-start | bytes 245768 | tf_op jit(solution)/shard_map/ppermute | solution.py:342
  38.0 30.8 %collective-permute-start.5 = (f32[2,320,320]{2,1,0:T(8,128)S(1)}, f32[2,320,320]{2,1,0:T(8,128)}, u32[]{:S(2)}, u32[]{:S(2)}) collective-permute-start(f32[2,320,320]{2,1,0:T(8,128)S(1)} %broadcast_select_fusion), channel_id=1, source_target_pairs={{0,2},{1,3},{129,131},{130,128},{258,256},{259,257},{387,385},{384... | collective-permute-start | bytes 2457608 | tf_op jit(solution)/shard_map/ppermute | solution.py:347
  55.0 18.8 %all-to-all-start.1 = ((f32[8,40,256]{2,1,0:T(8,128)}), f32[8,40,256]{2,1,0:T(8,128)S(1)}, u32[]{:S(2)}, u32[]{:S(2)}) async-start(f32[8,40,256]{2,1,0:T(8,128)} %own_sum.1), calls=%async_computation.1 | async-start | bytes 655360 | tf_op jit(solution)/shard_map/all_to_all | solution.py:357
  61.5 8.7 %copy-start.2 = (f32[320,256]{1,0:T(8,128)}, f32[320,256]{1,0:T(8,128)S(1)}, u32[]{:S(2)}) copy-start(f32[320,256]{1,0:T(8,128)S(1)} %constant_dynamic-update-slice_fusion.2.mine_hbm) | copy-start | bytes 983044
  61.5 11.6 %collective-permute-start.3 = (f32[320,256]{1,0:T(8,128)S(1)}, f32[320,256]{1,0:T(8,128)S(1)}, u32[]{:S(2)}, u32[]{:S(2)}) collective-permute-start(f32[320,256]{1,0:T(8,128)S(1)} %constant_dynamic-update-slice_fusion.2.mine_hbm), channel_id=1, source_target_pairs={{0,64},{64,0},{1,65},{65,1},{2,66},{66,2},{3,67},{67,3},{4,68},{68... | collective-permute-start | bytes 983048 | tf_op jit(solution)/shard_map/ppermute | solution.py:359
  73.0 0.7 copy-start.4
  75.1 31.5 %all-to-all-start.2 = ((f32[16,16,256]{2,1,0:T(8,128)}), f32[16,16,256]{2,1,0:T(8,128)S(1)}, u32[]{:S(2)}, u32[]{:S(2)}) async-start(f32[16,16,256]{2,1,0:T(8,128)} %bitcast.4), calls=%async_computation.2 | async-start | bytes 524288 | tf_op jit(solution)/shard_map/all_to_all | solution.py:364
  84.0 12.4 %collective-permute-start.8 = (f32[320,256]{1,0:T(8,128)S(1)}, f32[320,256]{1,0:T(8,128)S(1)}, u32[]{:S(2)}, u32[]{:S(2)}) collective-permute-start(f32[320,256]{1,0:T(8,128)S(1)} %bitcast.16), channel_id=1, source_target_pairs={{0,3},{1,0},{2,1},{3,2},{4,7},{5,4},{6,5},{7,6},{8,11},{9,8},{10,9... | collective-permute-start | bytes 983048 | tf_op jit(solution)/shard_map/ppermute | solution.py:365
  86.4 14.0 %collective-permute-start.7 = (f32[320,256]{1,0:T(8,128)S(1)}, f32[320,256]{1,0:T(8,128)S(1)}, u32[]{:S(2)}, u32[]{:S(2)}) collective-permute-start(f32[320,256]{1,0:T(8,128)S(1)} %bitcast.17), channel_id=1, source_target_pairs={{0,2},{1,3},{2,0},{3,1},{4,6},{5,7},{6,4},{7,5},{8,10},{9,11},{10,... | collective-permute-start | bytes 983048 | tf_op jit(solution)/shard_map/ppermute | solution.py:365
  90.3 16.4 %collective-permute-start.6 = (f32[320,256]{1,0:T(8,128)S(1)}, f32[320,256]{1,0:T(8,128)S(1)}, u32[]{:S(2)}, u32[]{:S(2)}) collective-permute-start(f32[320,256]{1,0:T(8,128)S(1)} %bitcast.18), channel_id=1, source_target_pairs={{0,1},{1,2},{2,3},{3,0},{4,5},{5,6},{6,7},{7,4},{8,9},{9,10},{10,1... | collective-permute-start | bytes 983048 | tf_op jit(solution)/shard_map/ppermute | solution.py:365
  108.5 19.2 %all-to-all-start.3 = ((f32[16,16,256]{2,1,0:T(8,128)}), f32[16,16,256]{2,1,0:T(8,128)S(1)}, u32[]{:S(2)}, u32[]{:S(2)}) async-start(f32[16,16,256]{2,1,0:T(8,128)} %right_sum.1), calls=%async_computation.3 | async-start | bytes 524288 | tf_op jit(solution)/shard_map/all_to_all | solution.py:371
  119.9 36.3 %collective-permute-start.9 = (f32[320,320]{1,0:T(8,128)}, f32[320,320]{1,0:T(8,128)S(1)}, u32[]{:S(2)}, u32[]{:S(2)}) collective-permute-start(f32[320,320]{1,0:T(8,128)} %left_gram.1.left_raw_ref), channel_id=1, source_target_pairs={{0,0},{1,129},{2,258},{3,387},{128,384},{129,1},{130,130},{131,259... | collective-permute-start | bytes 1228808 | tf_op jit(solution)/shard_map/ppermute | solution.py:375
  127.7 1.0 copy-start.3
  128.6 1.0 copy-start.5
  129.6 0.9 copy-start.6
  130.6 0.9 copy-start.7
  156.1 8.9 %collective-permute-start.10 = (f32[320,320]{1,0:T(8,128)S(1)}, f32[320,320]{1,0:T(8,128)S(1)}, u32[]{:S(2)}, u32[]{:S(2)}) collective-permute-start(f32[320,320]{1,0:T(8,128)S(1)} %collective-permute-done.9), channel_id=1, source_target_pairs={{0,0},{1,1},{2,2},{3,3},{128,131},{129,128},{130,129},{131,130},{2... | collective-permute-start | bytes 1228808 | tf_op jit(solution)/shard_map/ppermute | solution.py:383
  158.0 40.5 %all-to-all-start.4 = ((f32[4,320,256]{2,1,0:T(8,128)}), f32[4,320,256]{2,1,0:T(8,128)S(1)}, u32[]{:S(2)}, u32[]{:S(2)}) async-start(f32[4,320,256]{2,1,0:T(8,128)} %broadcast_in_dim.18), calls=%async_computation.4 | async-start | bytes 2621440 | tf_op jit(solution)/shard_map/all_to_all | solution.py:328
